TPU v7x, 128 devices: a whole 4x4x4 slice. The times are simulated.
128 devices in a mesh: ctx: 4 (over y_lo, core), fsdp: 32 (over y_hi, x, z).
Axes of the slice: x: 4, y: 4 (y_hi: 2, y_lo: 2; y = y_hi * 2 + y_lo), z: 4, core: 2. Of those that a mesh axis runs over, the one named last changes fastest.
Arguments:
- tokens: bfloat16 [32, 512, 1024], P('fsdp', 'ctx'), may hold values from -6 to 6
- cotangent: bfloat16 [32, 512, 2048], P('fsdp', 'ctx'), may hold values from -6 to 6
- w_xz: bfloat16 [1024, 4096], P('fsdp'), may hold values from -0.1875 to 0.1875
- w_bcdt: bfloat16 [1024, 288], P('fsdp'), may hold values from -0.1875 to 0.1875
- rate: float32 [32], replicated, may hold values from 0.0001953125 to 1
- dt_bias: float32 [32], replicated, may hold values from -3 to 0.5
- skip: float32 [32], replicated, may hold values from 0.5 to 1.5
- gain: float32 [2048], replicated, may hold values from 0.5 to 1.5
Outputs:
- layer_out: bfloat16 [32, 512, 2048], P('fsdp', 'ctx')
- grad_input: bfloat16 [32, 512, 1024], P('fsdp', 'ctx')
- grad_xz: float32 [1024, 4096], P(('ctx', 'fsdp'))
- grad_bcdt: float32 [1024, 288], P(('ctx', 'fsdp'))
All inputs are finite; a program needn't handle non-finite values.
Results may differ from a plain program's by a relative error of at most 0.005.
Values may be sent and summed in bfloat16 or wider, within the bound.
No kernel may reach another device: no remote copies, remote signals or barrier semaphores. Data moves between devices by JAX's collectives and lax.ppermute only.
A program may use at most 128 MiB of HBM per device.

v0:
```python
import math

import jax
import jax.numpy as jnp
from jax import lax
from jax.sharding import PartitionSpec as P

highest = lax.Precision.HIGHEST
norm_eps = 1e-05


def shifted(shard, axis, by):
    count = lax.axis_size(axis)
    pairs = [(i, i + by) for i in range(count) if 0 <= i + by < count]
    return lax.ppermute(shard, axis, pairs)


def split_proj(xz, bcdt, dt_bias, rate):
    inner = xz.shape[1] // 2
    heads = dt_bias.shape[0]
    states = (bcdt.shape[1] - heads) // 2
    values = jax.nn.silu(xz[:, :inner])
    gate_in = xz[:, inner:]
    b_in = bcdt[:, :states]
    c_out = bcdt[:, states : 2 * states]
    step_size = jax.nn.softplus(bcdt[:, 2 * states :] + dt_bias)
    log_decay = -step_size * rate
    return (values, gate_in, b_in, c_out, step_size, log_decay)


def ssd_blocks(values, b_in, c_out, step_size, log_decay, start):
    length = values.shape[0]
    heads, width, states = start.shape
    block = math.gcd(length, 128)
    count = length // block
    vals_b = values.reshape(count, block, heads, width)
    b_blocks = b_in.reshape(count, block, states)
    c_blocks = c_out.reshape(count, block, states)
    step_b = step_size.reshape(count, block, heads)
    log_b = log_decay.reshape(count, block, heads)
    causal = jnp.arange(block)[:, None] >= jnp.arange(block)[None, :]

    def one_block(state, pieces):
        vals, b_part, c_part, steps, logs = pieces
        cumul = jnp.cumsum(logs, axis=0)
        scores = jnp.dot(c_part, b_part.T, precision=highest)
        gaps = jnp.where(causal[:, :, None], cumul[:, None, :] - cumul[None, :, :], -1e30)
        weights = scores[:, :, None] * jnp.exp(gaps) * steps[None, :, :]
        inner = jnp.einsum("tsh,shp->thp", weights, vals, precision=highest)
        carried = jnp.exp(cumul)[:, :, None] * jnp.einsum(
            "tn,hpn->thp", c_part, state, precision=highest
        )
        tail = jnp.exp(cumul[-1][None, :] - cumul) * steps
        update = jnp.einsum("sh,shp,sn->hpn", tail, vals, b_part, precision=highest)
        new_state = jnp.exp(cumul[-1])[:, None, None] * state + update
        return (new_state, (inner + carried).reshape(block, heads * width))

    final, outs = lax.scan(one_block, start, (vals_b, b_blocks, c_blocks, step_b, log_b))
    return (outs.reshape(length, heads * width), final)


def gated_norm(ssd, gate_in, gain):
    mixed = ssd * jax.nn.silu(gate_in)
    scale = lax.rsqrt(jnp.mean(mixed * mixed, axis=-1, keepdims=True) + norm_eps)
    return mixed * scale * gain


def body(tokens, cotangent, w_xz, w_bcdt, rate, dt_bias, skip, gain):
    full_xz, full_bcdt = (
        lax.all_gather(w_xz, "fsdp", axis=0, tiled=True),
        lax.all_gather(w_bcdt, "fsdp", axis=0, tiled=True),
    )
    seqs, length, model = tokens.shape
    heads = rate.shape[0]
    flat = tokens.reshape(seqs * length, model)
    xz = jnp.dot(flat, full_xz, preferred_element_type=jnp.float32).reshape(seqs, length, -1)
    bcdt = jnp.dot(flat, full_bcdt, preferred_element_type=jnp.float32).reshape(seqs, length, -1)

    def zero_pass(xz_one, bcdt_one):
        values, gate_in, b_in, c_out, step_size, log_decay = split_proj(
            xz_one, bcdt_one, dt_bias, rate
        )
        width = values.shape[1] // heads
        start = jnp.zeros((heads, width, b_in.shape[1]), jnp.float32)
        partial_value, local_state = ssd_blocks(values, b_in, c_out, step_size, log_decay, start)
        cumul = jnp.cumsum(log_decay, axis=0)
        return (partial_value, local_state, values, gate_in, c_out, cumul)

    def finish(partial_value, values, gate_in, c_out, cumul, entry):
        width = values.shape[1] // heads
        carried = jnp.exp(cumul)[:, :, None] * jnp.einsum(
            "tn,hpn->thp", c_out, entry, precision=highest
        )
        ssd = (
            partial_value
            + carried.reshape(length, heads * width)
            + values * jnp.repeat(skip, width)
        )
        return gated_norm(ssd, gate_in, gain)

    outputs, pull_zero = jax.vjp(jax.vmap(zero_pass), xz, bcdt)
    partial_value, local_state, values, gate_in, c_out, cumul = outputs
    total = cumul[:, -1, :]
    decay_all = jnp.exp(total)[:, :, None, None]

    def advance(step, entry_now):
        ending = decay_all * entry_now + local_state
        return shifted(ending, "ctx", 1)

    entry = lax.fori_loop(0, lax.axis_size("ctx") - 1, advance, jnp.zeros_like(local_state))
    normed, pull_finish = jax.vjp(
        jax.vmap(finish), partial_value, values, gate_in, c_out, cumul, entry
    )
    layer_out = normed.astype(jnp.bfloat16)
    d_partial, d_values, d_gate, d_cout, d_cumul, direct = pull_finish(
        cotangent.astype(jnp.float32)
    )

    def retreat(step, later_now):
        pending = direct + decay_all * later_now
        return shifted(pending, "ctx", -1)

    later_grad = lax.fori_loop(0, lax.axis_size("ctx") - 1, retreat, jnp.zeros_like(direct))
    d_total = jnp.exp(total) * jnp.sum(later_grad * entry, axis=(2, 3))
    d_cumul = d_cumul.at[:, -1, :].add(d_total)
    d_xz, d_bcdt = pull_zero((d_partial, later_grad, d_values, d_gate, d_cout, d_cumul))
    d_xz = d_xz.astype(jnp.bfloat16).reshape(seqs * length, -1)
    d_bcdt = d_bcdt.astype(jnp.bfloat16).reshape(seqs * length, -1)
    grad_input = (
        jnp.dot(d_xz, full_xz.T, preferred_element_type=jnp.float32)
        + jnp.dot(d_bcdt, full_bcdt.T, preferred_element_type=jnp.float32)
    ).astype(jnp.bfloat16)
    term_xz = jnp.dot(flat.T, d_xz, preferred_element_type=jnp.float32)
    term_bcdt = jnp.dot(flat.T, d_bcdt, preferred_element_type=jnp.float32)
    grad_xz, grad_bcdt = (
        lax.psum_scatter(term_xz, ("ctx", "fsdp"), scatter_dimension=0, tiled=True),
        lax.psum_scatter(term_bcdt, ("ctx", "fsdp"), scatter_dimension=0, tiled=True),
    )
    return (layer_out, grad_input.reshape(seqs, length, model), grad_xz, grad_bcdt)


def solution(mesh):
    placed = (
        P("fsdp", "ctx", None),
        P("fsdp", "ctx", None),
        P("fsdp", None),
        P("fsdp", None),
        P(),
        P(),
        P(),
        P(),
    )
    return jax.shard_map(
        body,
        mesh=mesh,
        in_specs=placed,
        out_specs=(
            P("fsdp", "ctx", None),
            P("fsdp", "ctx", None),
            P(("ctx", "fsdp"), None),
            P(("ctx", "fsdp"), None),
        ),
        check_vma=False,
    )
```

profile of v0, /device:TPU:24, one launch (start us, length us, event | category | flops | bytes accessed | tf_op | source)
XLA Modules:
  0.0 1189.5 jit_solution(12357164636136479261)
XLA Ops:
  8.0 0.7 broadcast_in_dim.131
  9.4 101.2 %all_gather.7 = bf16[1024,288]{1,0:T(8,128)(2,1)S(1)} all-gather(bf16[32,288]{1,0:T(8,128)(2,1)} %param.17), channel_id=1, replica_groups=mesh['ctx'=4,'fsdp'=32] {'fsdp'}, dimensions={0}, use_global_device_ids=true | all-gather | bytes 608256 | tf_op jit(solution)/shard_map/all_gather | solution.py:71
  111.6 1.3 copy.83
  113.5 0.8 slice_reduce_fusion
  114.8 0.7 multiply_bitcast_fusion
  115.5 0.9 fusion.62
  116.4 1.0 fusion.45
  117.4 1.6 all-gather.2.cloned.1.call-done
  119.1 4.6 convolution_bitcast_fusion.1
  123.7 1.3 copy-done.1
  125.7 5.3 fusion.7
  131.0 1.3 copy.81
  132.3 1.7 fusion.5
  134.1 51.3 %while.5 = (s32[]{:T(128)}, f32[1,32,64,128]{3,2,1,0:T(8,128)S(1)}, f32[1,32,1,1]{1,3,2,0:T(1,128)}, f32[1,32,64,128]{3,2,1,0:T(8,128)S(1)}, s32[]{:T(128)}) while((s32[]{:T(128)}, f32[1,32,64,128]{3,2,1,0:T(8,128)S(1)}, f32[1,32,1,1]{1,3,2,0:T(1,128)}, f32[1,32,64,128]{3,2,1,0:T(8,128)S(1)}, s32[]{:T(128)}) %tuple.72), condition=%wide.region_2.3_spmd, body=%wide.region_1.2_spmd.sunk | while | flops 524290 | bytes 7340261 | solution.py:110
  134.6 0.8 multiply_add_fusion.7
  135.4 1.9 collective-permute-start
  137.4 14.2 %collective-permute-done = f32[1,32,64,128]{3,2,1,0:T(8,128)S(1)} collective-permute-done((f32[1,32,64,128]{3,2,1,0:T(8,128)S(1)}, f32[1,32,64,128]{3,2,1,0:T(8,128)S(1)}, u32[]{:S(2)}, u32[]{:S(2)}) %collective-permute-start) | collective-permute-done | bytes 1048608 | tf_op jit(solution)/shard_map/while/body/eval_jaxpr/ppermute | solution.py:15
  151.5 0.8 multiply_add_fusion.7
  152.4 1.9 collective-permute-start
  154.3 14.2 %collective-permute-done = f32[1,32,64,128]{3,2,1,0:T(8,128)S(1)} collective-permute-done((f32[1,32,64,128]{3,2,1,0:T(8,128)S(1)}, f32[1,32,64,128]{3,2,1,0:T(8,128)S(1)}, u32[]{:S(2)}, u32[]{:S(2)}) %collective-permute-start) | collective-permute-done | bytes 1048608 | tf_op jit(solution)/shard_map/while/body/eval_jaxpr/ppermute | solution.py:15
  168.5 0.8 multiply_add_fusion.7
  169.3 1.9 collective-permute-start
  171.3 14.2 %collective-permute-done = f32[1,32,64,128]{3,2,1,0:T(8,128)S(1)} collective-permute-done((f32[1,32,64,128]{3,2,1,0:T(8,128)S(1)}, f32[1,32,64,128]{3,2,1,0:T(8,128)S(1)}, u32[]{:S(2)}, u32[]{:S(2)}) %collective-permute-start) | collective-permute-done | bytes 1048608 | tf_op jit(solution)/shard_map/while/body/eval_jaxpr/ppermute | solution.py:15
  185.4 3.2 broadcast_multiply_fusion
  188.6 2.6 copy.82
  191.3 2.6 multiply_reduce_fusion.6
  194.0 2.4 fusion.97
  196.3 1.5 copy.84
  197.9 1.8 convolution_bitcast_fusion.8
  199.7 2.4 convolution_bitcast_fusion.9
  202.1 1.0 convolution_bitcast_fusion.4
  203.2 52.8 %while.6 = (s32[]{:T(128)}, f32[1,32,64,128]{3,2,1,0:T(8,128)S(1)}, f32[1,32,1,1]{1,3,2,0:T(1,128)}, f32[1,32,64,128]{3,2,1,0:T(8,128)S(1)}, s32[]{:T(128)}) while((s32[]{:T(128)}, f32[1,32,64,128]{3,2,1,0:T(8,128)S(1)}, f32[1,32,1,1]{1,3,2,0:T(1,128)}, f32[1,32,64,128]{3,2,1,0:T(8,128)S(1)}, s32[]{:T(128)}) %tuple.75), condition=%wide.region_6.7_spmd, body=%wide.region_5.6_spmd.sunk | while | flops 524290 | bytes 7340261 | solution.py:123
  203.3 1.8 multiply_add_fusion.8
  205.1 1.9 collective-permute-start.1
  207.0 12.6 %collective-permute-done.1 = f32[1,32,64,128]{3,2,1,0:T(8,128)S(1)} collective-permute-done((f32[1,32,64,128]{3,2,1,0:T(8,128)}, f32[1,32,64,128]{3,2,1,0:T(8,128)S(1)}, u32[]{:S(2)}, u32[]{:S(2)}) %collective-permute-start.1) | collective-permute-done | bytes 1048608 | tf_op jit(solution)/shard_map/while/body/eval_jaxpr/ppermute | solution.py:15
  219.6 1.8 multiply_add_fusion.8
  221.4 3.7 collective-permute-start.1
  225.2 12.6 %collective-permute-done.1 = f32[1,32,64,128]{3,2,1,0:T(8,128)S(1)} collective-permute-done((f32[1,32,64,128]{3,2,1,0:T(8,128)}, f32[1,32,64,128]{3,2,1,0:T(8,128)S(1)}, u32[]{:S(2)}, u32[]{:S(2)}) %collective-permute-start.1) | collective-permute-done | bytes 1048608 | tf_op jit(solution)/shard_map/while/body/eval_jaxpr/ppermute | solution.py:15
  237.8 1.8 multiply_add_fusion.8
  239.6 3.7 collective-permute-start.1
  243.3 12.6 %collective-permute-done.1 = f32[1,32,64,128]{3,2,1,0:T(8,128)S(1)} collective-permute-done((f32[1,32,64,128]{3,2,1,0:T(8,128)}, f32[1,32,64,128]{3,2,1,0:T(8,128)S(1)}, u32[]{:S(2)}, u32[]{:S(2)}) %collective-permute-start.1) | collective-permute-done | bytes 1048608 | tf_op jit(solution)/shard_map/while/body/eval_jaxpr/ppermute | solution.py:15
  256.1 0.9 multiply_reduce_fusion.3
  257.3 2.6 multiply_reduce_fusion.1
  259.9 1.3 copy.91
  261.2 1.3 copy.94
  262.5 1.4 fusion.83
  263.9 1.3 copy.87
  265.2 6.6 fusion.9
  272.1 2.5 fusion.12
  274.6 3.4 fusion.6
  278.1 2.6 copy.88
  280.7 2.8 fusion.18
  283.6 0.7 multiply_reduce_fusion.2
  284.9 1.1 reduce_window_sum.41
  286.4 1.1 reduce_window_sum.39
  288.0 1.4 convolution_bitcast_fusion.2
  289.5 8.1 convolution_bitcast_fusion
  297.6 17.5 %copy.115 = f32[1024,4096]{1,0:T(8,128)} copy(f32[1024,4096]{0,1:T(8,128)} %convolution_bitcast_fusion) | data formatting | bytes 33554432
  315.1 6.4 fusion.52
  321.5 1.1 fusion.11
  322.6 113.0 %all-reduce.10.cloned.1.call-done = f32[1024,288]{0,1:T(8,128)} async-done(((f32[1024,288]{0,1:T(8,128)}), f32[1024,288]{0,1:T(8,128)}) %all-reduce.10.cloned.1.call-update) | async-done | bytes 1179664
  435.6 1.0 constant_dynamic-slice_fusion
  436.7 0.7 copy.100
  437.4 745.4 %reduce-scatter.5.cloned.1.call-done = f32[8,4096]{1,0:T(8,128)} async-done(((f32[1024,4096]{1,0:T(8,128)}), f32[8,4096]{1,0:T(8,128)}) %reduce-scatter.5.cloned.1.call-update) | async-done | bytes 131088
  (122 shorter events, 6.5 us)
Async XLA Ops:
  7.2 103.4 %copy-start = (bf16[1,128,1024]{2,1,0:T(8,128)(2,1)S(1)}, bf16[1,128,1024]{2,1,0:T(8,128)(2,1)}, u32[]{:S(2)}) copy-start(bf16[1,128,1024]{2,1,0:T(8,128)(2,1)} %param.14) | copy-start | bytes 786436
  7.2 103.8 %copy-start.39 = (f32[32]{0:T(128)S(1)}, f32[32]{0:T(128)}, u32[]{:S(2)}) copy-start(f32[32]{0:T(128)} %param.19) | copy-start | bytes 388
  7.2 103.8 %copy-start.43 = (f32[32]{0:T(128)S(1)}, f32[32]{0:T(128)}, u32[]{:S(2)}) copy-start(f32[32]{0:T(128)} %param.18) | copy-start | bytes 388
  7.2 111.9 %all-gather.2.cloned.1.call-start = ((), (), s32[]{:S(2)}) async-start(), calls=%async_computation.1 | async-start | bytes 8650752 | tf_op jit(solution)/shard_map/all_gather | solution.py:70
  7.9 427.7 %all-reduce.10.cloned.1.call-start = ((), (), s32[]{:S(2)}) async-start(), calls=%async_computation.3 | async-start | bytes 2359296
  110.6 2.3 copy-start.9
  111.4 6.0 copy-start.18
  111.5 6.0 copy-start.27
  114.3 9.4 copy-start.41
  117.4 8.2 copy-start.12
  123.7 1.3 copy-start.1
  125.7 6.6 copy-start.4
  135.4 16.1 %collective-permute-start = (f32[1,32,64,128]{3,2,1,0:T(8,128)S(1)}, f32[1,32,64,128]{3,2,1,0:T(8,128)S(1)}, u32[]{:S(2)}, u32[]{:S(2)}) collective-permute-start(f32[1,32,64,128]{3,2,1,0:T(8,128)S(1)} %multiply_add_fusion.7), channel_id=1, source_target_pairs={{0,32},{32,64},{64,96},{1,33},{33,65},{65,97},{2,34},{34,66},{66,9... | collective-permute-start | bytes 3145736 | tf_op jit(solution)/shard_map/while/body/eval_jaxpr/ppermute | solution.py:15
  152.4 16.1 %collective-permute-start = (f32[1,32,64,128]{3,2,1,0:T(8,128)S(1)}, f32[1,32,64,128]{3,2,1,0:T(8,128)S(1)}, u32[]{:S(2)}, u32[]{:S(2)}) collective-permute-start(f32[1,32,64,128]{3,2,1,0:T(8,128)S(1)} %multiply_add_fusion.7), channel_id=1, source_target_pairs={{0,32},{32,64},{64,96},{1,33},{33,65},{65,97},{2,34},{34,66},{66,9... | collective-permute-start | bytes 3145736 | tf_op jit(solution)/shard_map/while/body/eval_jaxpr/ppermute | solution.py:15
  169.3 16.1 %collective-permute-start = (f32[1,32,64,128]{3,2,1,0:T(8,128)S(1)}, f32[1,32,64,128]{3,2,1,0:T(8,128)S(1)}, u32[]{:S(2)}, u32[]{:S(2)}) collective-permute-start(f32[1,32,64,128]{3,2,1,0:T(8,128)S(1)} %multiply_add_fusion.7), channel_id=1, source_target_pairs={{0,32},{32,64},{64,96},{1,33},{33,65},{65,97},{2,34},{34,66},{66,9... | collective-permute-start | bytes 3145736 | tf_op jit(solution)/shard_map/while/body/eval_jaxpr/ppermute | solution.py:15
  185.4 5.8 copy-start.2
  191.3 2.7 copy-start.14
  191.3 2.7 copy-start.17
  191.3 2.7 copy-start.33
  205.1 14.5 %collective-permute-start.1 = (f32[1,32,64,128]{3,2,1,0:T(8,128)}, f32[1,32,64,128]{3,2,1,0:T(8,128)S(1)}, u32[]{:S(2)}, u32[]{:S(2)}) collective-permute-start(f32[1,32,64,128]{3,2,1,0:T(8,128)} %multiply_add_fusion.8), channel_id=1, source_target_pairs={{32,0},{64,32},{96,64},{33,1},{65,33},{97,65},{34,2},{66,34},{98,6... | collective-permute-start | bytes 3145736 | tf_op jit(solution)/shard_map/while/body/eval_jaxpr/ppermute | solution.py:15
  221.4 16.3 %collective-permute-start.1 = (f32[1,32,64,128]{3,2,1,0:T(8,128)}, f32[1,32,64,128]{3,2,1,0:T(8,128)S(1)}, u32[]{:S(2)}, u32[]{:S(2)}) collective-permute-start(f32[1,32,64,128]{3,2,1,0:T(8,128)} %multiply_add_fusion.8), channel_id=1, source_target_pairs={{32,0},{64,32},{96,64},{33,1},{65,33},{97,65},{34,2},{66,34},{98,6... | collective-permute-start | bytes 3145736 | tf_op jit(solution)/shard_map/while/body/eval_jaxpr/ppermute | solution.py:15
  239.6 16.3 %collective-permute-start.1 = (f32[1,32,64,128]{3,2,1,0:T(8,128)}, f32[1,32,64,128]{3,2,1,0:T(8,128)S(1)}, u32[]{:S(2)}, u32[]{:S(2)}) collective-permute-start(f32[1,32,64,128]{3,2,1,0:T(8,128)} %multiply_add_fusion.8), channel_id=1, source_target_pairs={{32,0},{64,32},{96,64},{33,1},{65,33},{97,65},{34,2},{66,34},{98,6... | collective-permute-start | bytes 3145736 | tf_op jit(solution)/shard_map/while/body/eval_jaxpr/ppermute | solution.py:15
  256.1 1.2 copy-start.5
  257.3 6.6 copy-start.6
  265.2 6.9 copy-start.28
  271.9 6.2 copy-start.25
  271.9 2.7 copy-start.15
  271.9 2.7 copy-start.19
  271.9 2.7 copy-start.21
  271.9 2.7 copy-start.30
  271.9 2.7 copy-start.37
  271.9 2.7 copy-start.38
  274.6 6.0 copy-start.3
  280.7 2.9 copy-start.11
  280.7 2.9 copy-start.13
  280.7 2.9 copy-start.16
  283.5 0.8 copy-start.20
  283.5 0.9 copy-start.29
  283.5 0.9 copy-start.40
  283.5 0.9 copy-start.42
  283.5 1.2 copy-start.31
  283.5 1.2 copy-start.35
  283.5 1.2 copy-start.36
  283.5 2.5 copy-start.32
  283.5 4.1 copy-start.23
  283.5 4.1 copy-start.24
  283.5 4.1 copy-start.26
  283.6 4.3 copy-start.34
  283.6 4.3 copy-start.44
  283.6 4.4 copy-start.22
  284.3 5.1 copy-start.7
  284.4 5.1 copy-start.8
  289.4 893.3 %reduce-scatter.5.cloned.1.call-start = ((), (), s32[]{:S(2)}) async-start(), calls=%async_computation.2 | async-start | bytes 16908288
  315.1 6.4 copy-start.10
Sparse Core Ops, SparseCore 0:
  11.2 107.8 all-gather.1
  289.5 146.0 all-reduce.9
  438.7 743.9 reduce-scatter.4
where the time goes:
time: 1200 us; the launch traced here: 1190 us
  waiting for transfers between devices  941 us (78%)
  blocking collectives  101 us (8%)
  matrix products  54.8 us (5%)
  local copies, waits for them, and re-layouts  37.9 us (3%)
  other arithmetic  23.9 us (2%)
  starting transfers between devices  15.2 us (1%)
  between operations  14.6 us (1%)
    unnamed x5, waiting for transfers between devices  859 us
    all_gather x1, blocking collectives, body(): lax.all_gather(w_bcdt, 'fsdp', axis=0, tiled=True)  101 us
    ppermute x6, waiting for transfers between devices, shifted(): return lax.ppermute(shard, axis, pairs)  80.4 us
  transfers between devices with their start and end apart: 9, of which 9 were waited for; matrix products, arithmetic and copies ran while one was open for 4% of the time, Pallas kernels for 0%

commit v1 on v0

v1 whole, which is shorter than its diff:
```python
import jax
import jax.numpy as jnp
from jax import lax
from jax.experimental import pallas as pl
from jax.experimental.pallas import tpu as pltpu
from jax.sharding import Mesh, PartitionSpec as P

f32 = jnp.float32
bf16 = jnp.bfloat16
norm_eps = 1e-05
lanes = 128
NN = (((1,), (0,)), ((), ()))
NT = (((1,), (1,)), ((), ()))
TN = (((0,), (0,)), ((), ()))

whole = ("yl", "core", "yh", "x", "z")
rows_axes = ("yh", "x", "z")
group_axes = ("yl", "core", "yh")
vmem = 56 * 2**20


def dot1(a, b, dims):
    return lax.dot_general(a.astype(bf16), b.astype(bf16), dims, preferred_element_type=f32)


def halves(a):
    high = a.astype(bf16)
    return (high, (a - high.astype(f32)).astype(bf16))


def dot3(a, b, dims):
    a_high, a_low = a if isinstance(a, tuple) else halves(a)
    b_high, b_low = b if isinstance(b, tuple) else halves(b)
    dot = lambda left, right: lax.dot_general(left, right, dims, preferred_element_type=f32)
    return dot(a_high, b_high) + (dot(a_high, b_low) + dot(a_low, b_high))


def thirds(a):
    high = a.astype(bf16)
    rest = a - high.astype(f32)
    mid = rest.astype(bf16)
    return (high, mid, (rest - mid.astype(f32)).astype(bf16))


def dot_exact(a, ones, dims):
    high, mid, low = thirds(a)
    dot = lambda left: lax.dot_general(left, ones, dims, preferred_element_type=f32)
    return dot(high) + (dot(mid) + dot(low))


def iota(shape, axis):
    return lax.broadcasted_iota(jnp.int32, shape, axis)


def head_expander(inner, width):
    shape = (lanes, inner)
    start = iota(shape, 0) * width
    col = iota(shape, 1)
    return ((col >= start) & (col < start + width)).astype(f32).astype(bf16)


def lower_ones(block):
    shape = (block, block)
    return (iota(shape, 0) >= iota(shape, 1)).astype(f32).astype(bf16)


def cumulated(steps, rate, lower):
    log_decay = -steps * rate
    high, mid, low = thirds(log_decay)
    dot = lambda right: lax.dot_general(lower, right, NN, preferred_element_type=f32)
    return dot(high) + (dot(mid) + dot(low))


def softplus(a):
    return jnp.maximum(a, 0.0) + jnp.log1p(jnp.exp(-jnp.abs(a)))


def pair_halves(a, block, width):
    left = iota(a.shape, 1) < width
    zero = jnp.zeros_like(a)
    return jnp.concatenate([jnp.where(left, a, zero), jnp.where(left, zero, a)], axis=0)


def forward_kernel(tok, weights, par, cot, xv_o, g_o, bc_o, y_o, st_o, stat_o, state, *, seqs, block, width, inner):
    heads = inner // width
    step = pl.program_id(0)

    @pl.when(step == 0)
    def _():
        state[...] = jnp.zeros_like(state)

    rows = seqs * block
    proj = lax.dot_general(tok[0].reshape(rows, -1), weights[...], NN, preferred_element_type=f32)
    expander = head_expander(inner, width)
    lower = lower_ones(block)
    causal = iota((block, block), 0) >= iota((block, block), 1)
    skip, gain = par[0:1, :], par[1:2, :]
    bias, rate = par[2:3, :lanes], par[3:4, :lanes]
    for s in range(seqs):
        part = proj[s * block : (s + 1) * block]
        xv, gate = part[:, :inner], part[:, inner : 2 * inner]
        b_in, c_out = part[:, 2 * inner : 2 * inner + lanes], part[:, 2 * inner + lanes : 2 * inner + 2 * lanes]
        raw = part[:, 2 * inner + 2 * lanes :] + bias
        xv_o[0, s] = xv
        g_o[0, s] = gate
        bc_o[0, s] = jnp.concatenate([b_in, c_out, raw], axis=1)
        values = xv * jax.nn.sigmoid(xv)
        steps = softplus(raw)
        cumul = cumulated(steps, rate, lower)
        cumul_t = cumul.T
        wide = dot_exact(jnp.concatenate([steps, cumul], axis=0), expander, NN)
        step_wide, cumul_wide = wide[:block], wide[block:]
        last_wide = cumul_wide[block - 1 : block]
        scaled = values * step_wide
        b_two, c_two = halves(b_in), halves(c_out)
        scores = dot3(c_two, b_two, NT)
        old = state[s]
        st_o[0, s] = old
        carried = jnp.exp(cumul_wide) * dot3(c_two, old, NN)
        inners = []
        for pair in range(heads // 2):
            both = []
            for h in (2 * pair, 2 * pair + 1):
                gap = jnp.where(causal, cumul[:, h : h + 1] - cumul_t[h : h + 1, :], -1e30)
                both.append((scores * jnp.exp(gap)).astype(bf16))
            cols = scaled[:, 2 * pair * width : (2 * pair + 2) * width]
            inners.append(
                lax.dot_general(
                    jnp.concatenate(both, axis=1),
                    pair_halves(cols, block, width).astype(bf16),
                    NN,
                    preferred_element_type=f32,
                )
            )
        y = carried + jnp.concatenate(inners, axis=1)
        y_o[0, s] = y
        state[s] = jnp.exp(last_wide) * old + dot3(b_two, scaled * jnp.exp(last_wide - cumul_wide), TN)
        mixed = (y + skip * values) * (gate * jax.nn.sigmoid(gate))
        weighted = cot[0, s].astype(f32) * gain * mixed
        both = jnp.concatenate([mixed * mixed, weighted], axis=1)
        row, col = iota((8, 2 * inner), 0), iota((8, 2 * inner), 1)
        chooser = ((row < 2) & ((col >= inner) == (row == 1))).astype(f32).astype(bf16)
        high, mid, low = thirds(both)
        dot = lambda right: lax.dot_general(chooser, right, NT, preferred_element_type=f32)
        stat_o[0, :, s * block : (s + 1) * block] = dot(high) + (dot(mid) + dot(low))


def backward_kernel(
    xv_i, g_i, bc_i, y_i, st_i, cot, stat, par, out_o, d_o, grad_state, next_state, *, seqs, block, width, inner, total
):
    heads = inner // width
    step = pl.program_id(0)

    @pl.when(step == 0)
    def _():
        grad_state[...] = jnp.zeros_like(grad_state)
        next_state[...] = jnp.zeros_like(next_state)

    expander = head_expander(inner, width)
    lower = lower_ones(block)
    later = iota((block, block), 1) >= iota((block, block), 0)
    upper = (iota((block, block), 1) >= iota((block, block), 0)).astype(f32).astype(bf16)
    skip, gain = par[0:1, :], par[1:2, :]
    bias_rate = par[3:4, :lanes]
    sums = stat[0]
    scale_row = lax.rsqrt(sums[0:1] * (1.0 / total) + norm_eps)
    pull_row = scale_row * scale_row * scale_row * sums[1:2] * (1.0 / total)
    packed = jnp.concatenate([scale_row, pull_row, jnp.zeros((6, scale_row.shape[1]), f32)], axis=0)
    row, col = iota((8, 2 * inner), 0), iota((8, 2 * inner), 1)
    chooser = ((row < 2) & ((col >= inner) == (row == 1))).astype(f32).astype(bf16)
    spread = dot_exact(packed, chooser, TN)
    for s in range(seqs):
        span = slice(s * block, (s + 1) * block)
        scale, pull = spread[span, :inner], spread[span, inner:]
        xv, gate, y = xv_i[0, s], g_i[0, s], y_i[0, s]
        b_in, c_out = bc_i[0, s, :, :lanes], bc_i[0, s, :, lanes : 2 * lanes]
        raw = bc_i[0, s, :, 2 * lanes :]
        sig = jax.nn.sigmoid(xv)
        values = xv * sig
        gate_sig = jax.nn.sigmoid(gate)
        gate_silu = gate * gate_sig
        full = y + skip * values
        mixed = full * gate_silu
        out_o[0, s] = (mixed * scale * gain).astype(bf16)
        d_mixed = cot[0, s].astype(f32) * gain * scale - mixed * pull
        d_y = d_mixed * gate_silu
        d_gate = d_mixed * full * (gate_sig * (1.0 + gate * (1.0 - gate_sig)))

        steps = softplus(raw)
        cumul = cumulated(steps, bias_rate, lower)
        cumul_t = cumul.T
        wide = dot_exact(jnp.concatenate([steps, cumul], axis=0), expander, NN)
        step_wide, cumul_wide = wide[:block], wide[block:]
        last_wide = cumul_wide[block - 1 : block]
        tail = jnp.exp(last_wide - cumul_wide)
        scaled = values * step_wide
        b_two, c_two = halves(b_in), halves(c_out)
        scores_t = dot3(b_two, c_two, NT)
        old = st_i[0, s]
        grad = grad_state[s]
        grad_two = halves(grad)
        back = tail * dot3(b_two, grad_two, NN)
        inners = []
        d_scores_t = jnp.zeros((block, block), f32)
        for pair in range(heads // 2):
            cols = slice(2 * pair * width, (2 * pair + 2) * width)
            dy_pair = d_y[:, cols].astype(bf16)
            products = lax.dot_general(
                pair_halves(scaled[:, cols], block, width).astype(bf16), dy_pair, NT, preferred_element_type=f32
            )
            both = []
            for k in range(2):
                h = 2 * pair + k
                gap = jnp.where(later, cumul_t[h : h + 1, :] - cumul[:, h : h + 1], -1e30)
                decay = jnp.exp(gap)
                both.append((scores_t * decay).astype(bf16))
                d_scores_t += products[k * block : (k + 1) * block] * decay
            inners.append(
                lax.dot_general(
                    jnp.concatenate(both, axis=1),
                    pair_halves(d_y[:, cols], block, width).astype(bf16),
                    NN,
                    preferred_element_type=f32,
                )
            )
        back = back + jnp.concatenate(inners, axis=1)
        lifted = halves(d_y * jnp.exp(cumul_wide))
        ds_two = halves(d_scores_t)
        d_c = dot3(ds_two, b_two, TN) + dot3(lifted, old, NT)
        d_b = dot3(ds_two, c_two, NN) + dot3(scaled * tail, grad_two, NT)
        through = jnp.sum(next_state[s] * grad, axis=0, keepdims=True)
        grad_state[s] = jnp.exp(last_wide) * grad + dot3(c_two, lifted, TN)
        next_state[s] = old
        last_row = iota((block, inner), 0) == block - 1
        reduced = dot_exact(
            jnp.concatenate([values * back, d_y * y + jnp.where(last_row, through, 0.0)], axis=0), expander, NT
        )
        d_steps = reduced[:block]
        d_cumul = reduced[block:] - steps * d_steps
        high, mid, low = thirds(d_cumul)
        dot = lambda right: lax.dot_general(upper, right, NN, preferred_element_type=f32)
        d_log = dot(high) + (dot(mid) + dot(low))
        d_raw = (d_steps - d_log * bias_rate) * jax.nn.sigmoid(raw)
        d_values = back * step_wide + skip * d_y
        d_xv = d_values * (sig * (1.0 + xv * (1.0 - sig)))
        d_o[0, s] = jnp.concatenate([d_xv, d_gate, d_b, d_c, d_raw], axis=1).astype(bf16)


def chunk_spec(shape, count=None):
    blank = (0,) * (len(shape) - 1)
    if count is None:
        return pl.BlockSpec((1,) + shape[1:], lambda i: (i,) + blank)
    return pl.BlockSpec((1,) + shape[1:], lambda i: (count - 1 - i,) + blank)


def fixed_spec(shape):
    return pl.BlockSpec(shape, lambda i: (0,) * len(shape))


def forward_call(tok, weights, par, cot, width):
    chunks, seqs, block, model = tok.shape
    inner = cot.shape[3]
    shapes = [
        (chunks, seqs, block, inner),
        (chunks, seqs, block, inner),
        (chunks, seqs, block, 3 * lanes),
        (chunks, seqs, block, inner),
        (chunks, seqs, lanes, inner),
        (chunks, 8, seqs * block),
    ]

    def kernel(*refs):
        forward_kernel(*refs, seqs=seqs, block=block, width=width, inner=inner)

    return pl.pallas_call(
        kernel,
        grid=(chunks,),
        in_specs=[chunk_spec(tok.shape), fixed_spec(weights.shape), fixed_spec(par.shape), chunk_spec(cot.shape)],
        out_specs=[chunk_spec(s) for s in shapes],
        out_shape=[jax.ShapeDtypeStruct(s, f32) for s in shapes],
        scratch_shapes=[pltpu.VMEM((seqs, lanes, inner), f32)],
        compiler_params=pltpu.CompilerParams(vmem_limit_bytes=vmem),
        name="forward_scan",
    )(tok, weights, par, cot)


def backward_call(xv, gate, bc, y, states, cot, stats, par, width, total):
    chunks, seqs, block, inner = xv.shape
    ins = (xv, gate, bc, y, states, cot, stats)
    out_shapes = [(chunks, seqs, block, inner), (chunks, seqs, block, 2 * inner + 3 * lanes)]

    def kernel(*refs):
        backward_kernel(*refs, seqs=seqs, block=block, width=width, inner=inner, total=total)

    return pl.pallas_call(
        kernel,
        grid=(chunks,),
        in_specs=[chunk_spec(a.shape, chunks) for a in ins] + [fixed_spec(par.shape)],
        out_specs=[chunk_spec(s, chunks) for s in out_shapes],
        out_shape=[jax.ShapeDtypeStruct(s, bf16) for s in out_shapes],
        scratch_shapes=[pltpu.VMEM((seqs, lanes, inner), f32), pltpu.VMEM((seqs, lanes, inner), f32)],
        compiler_params=pltpu.CompilerParams(vmem_limit_bytes=vmem),
        name="backward_scan",
    )(*ins, par)


def body(tokens, cotangent, w_xz, w_bcdt, rate, dt_bias, skip, gain):
    group = lax.axis_size(group_axes)
    devices = lax.axis_size(whole)
    mine = lax.axis_index(group_axes)
    chunks = lax.axis_size("yl") * lax.axis_size("core")
    seqs = group // chunks
    owners = lax.axis_size(rows_axes)
    block, model = tokens.shape[1:]
    total = cotangent.shape[2]
    inner = total // group
    heads = rate.shape[0] // group
    width = inner // heads
    states = (w_bcdt.shape[1] - rate.shape[0]) // 2

    def picked(target):
        w_dt = lax.dynamic_slice_in_dim(w_bcdt[:, 2 * states :], target * heads, heads, 1)
        return jnp.concatenate(
            [
                lax.dynamic_slice_in_dim(w_xz, target * inner, inner, 1),
                lax.dynamic_slice_in_dim(w_xz, total + target * inner, inner, 1),
                w_bcdt[:, : 2 * states],
                jnp.pad(w_dt, ((0, 0), (0, lanes - heads))),
            ],
            axis=1,
        )

    w_picked = jnp.stack([picked(lax.axis_index(("yl", "core")) * seqs + k) for k in range(seqs)])
    copies = jnp.broadcast_to(w_picked[:, None], (seqs, owners // seqs) + w_picked.shape[1:])
    copies = copies.reshape((owners,) + w_picked.shape[1:])
    weights = lax.all_to_all(copies, rows_axes, 0, 0, tiled=True).reshape(model, -1)

    tok = lax.all_gather(tokens[0], group_axes, axis=0).reshape(chunks, seqs, block, model)
    cot = lax.all_to_all(
        cotangent[0].reshape(block, group, inner).transpose(1, 0, 2), group_axes, 0, 0, tiled=True
    ).reshape(chunks, seqs, block, inner)

    own = lambda a: lax.dynamic_slice_in_dim(a, mine * heads, heads, 0)
    padded = lambda a: jnp.pad(own(a), (0, inner - heads))
    par = jnp.stack(
        [jnp.repeat(own(skip), width), lax.dynamic_slice_in_dim(gain, mine * inner, inner, 0)]
        + [padded(dt_bias), padded(rate)]
        + [jnp.zeros((inner,), f32)] * 4
    )
    xv, gate, bc, y, chunk_states, stats = forward_call(tok, weights, par, cot, width)
    stats = lax.all_gather(stats[:, :2], group_axes, axis=0).sum(axis=0)
    stats = jnp.pad(stats, ((0, 0), (0, 6), (0, 0)))
    out, d_all = backward_call(xv, gate, bc, y, chunk_states, cot, stats, par, width, float(total))

    flat_d = d_all.reshape(group * block, -1)
    term = lax.dot_general(tok.reshape(group * block, model), flat_d, TN, preferred_element_type=f32).astype(bf16)
    shares = lax.all_to_all(term.reshape(devices, model // devices, -1), whole, 0, 0, tiled=True)
    partial_input = lax.dot_general(flat_d, weights, NT, preferred_element_type=f32).astype(bf16)
    pieces = lax.all_to_all(partial_input.reshape(group, block, model), group_axes, 0, 0, tiled=True)
    grad_input = pieces.astype(f32).sum(axis=0).astype(bf16)[None]
    layer_out = lax.all_to_all(out.reshape(group, block, inner), group_axes, 0, 0, tiled=True)
    layer_out = layer_out.transpose(1, 0, 2).reshape(1, block, total)

    summed = shares.reshape(group, devices // group, model // devices, -1).astype(f32).sum(axis=1)
    spread = lambda a: a.transpose(1, 0, 2).reshape(model // devices, -1)
    grad_xz = jnp.concatenate([spread(summed[..., :inner]), spread(summed[..., inner : 2 * inner])], axis=1)
    grad_bcdt = jnp.concatenate(
        [
            summed[..., 2 * inner : 2 * inner + 2 * states].sum(axis=0),
            spread(summed[..., 2 * inner + 2 * states : 2 * inner + 2 * states + heads]),
        ],
        axis=1,
    )
    return (layer_out, grad_input, grad_xz, grad_bcdt)


def solution(mesh):
    split = Mesh(mesh.devices.reshape(2, 2, 2, 4, 4), whole)
    ctx, fsdp = ("yl", "core"), rows_axes
    placed = (P(fsdp, ctx, None), P(fsdp, ctx, None), P(fsdp, None), P(fsdp, None), P(), P(), P(), P())
    return jax.shard_map(
        body,
        mesh=split,
        in_specs=placed,
        out_specs=(P(fsdp, ctx, None), P(fsdp, ctx, None), P(ctx + fsdp, None), P(ctx + fsdp, None)),
        check_vma=False,
    )
```

time: 1200 us -> 241 us (0.20)
  the two profiles are of different devices: /device:TPU:24 before, /device:TPU:1 now
where the time goes in v1:
time: 241 us; the launch traced here: 240 us
  waiting for transfers between devices  105 us (44%)
  starting transfers between devices  37.8 us (16%)
  blocking collectives  29.6 us (12%)
  Pallas kernels  26.5 us (11%)
  between operations  14.2 us (6%)
  local copies, waits for them, and re-layouts  12.8 us (5%)
  matrix products  10.1 us (4%)
  other arithmetic  4.21 us (2%)
    all_gather x1, blocking collectives, body(): stats = lax.all_gather(stats[:, :2], group_axes, axis=0).sum(axis=0)  29.6 us
    all_to_all x1, waiting for transfers between devices, body(): lax.all_to_all(copies, rows_axes, 0, 0, tiled=True).reshape(model, -1)  24.4 us
    all_to_all x1, waiting for transfers between devices, body(): lax.all_to_all(partial_input.reshape(group, block, model), group_axes, 0,...  21.7 us
    all_to_all x1, waiting for transfers between devices, body(): lax.all_to_all(term.reshape(devices, model // devices, -1), whole, 0, 0,...  20.7 us
    all_gather x1, waiting for transfers between devices, body(): lax.all_gather(tokens[0], group_axes, axis=0)  19.6 us
    all_to_all x1, waiting for transfers between devices, body(): lax.all_to_all(cotangent[0].reshape(block, group, inner).transpose(1, 0,...  17 us
    pallas_call x1, Pallas kernels, backward_call(): pl.pallas_call(kernel, grid=(chunks,), in_specs=[chunk_spec(a.shape, chun...  14.8 us
    all_to_all x1, starting transfers between devices, body(): lax.all_to_all(term.reshape(devices, model // devices, -1), whole, 0, 0,...  12.9 us
  transfers between devices with their start and end apart: 6, of which 6 were waited for; matrix products, arithmetic and copies ran while one was open for 10% of the time, Pallas kernels for 0%

profile of v1, /device:TPU:1, one launch (start us, length us, event | category | flops | bytes accessed | tf_op | source)
XLA Modules:
  0.0 239.9 jit_solution(5074182155047053718)
XLA Ops:
  7.2 0.0 slice-start
  7.2 0.0 slice-start.1
  7.2 0.0 all-gather.3.cloned.1.call-start
  7.2 0.7 all-gather.3.cloned.1.call-update
  7.9 1.2 copy.34
  9.1 0.9 copy.36
  10.0 6.0 %all-to-all-start.1 = ((bf16[8,128,256]{2,1,0:T(8,128)(2,1)}), bf16[8,128,256]{2,1,0:T(8,128)(2,1)S(1)}, u32[]{:S(2)}, u32[]{:S(2)}) async-start(bf16[8,128,256]{2,1,0:T(8,128)(2,1)} %bitcast.42), calls=%async_computation.1 | async-start | bytes 1048576 | tf_op jit(solution)/shard_map/all_to_all | solution.py:339
  15.9 0.0 slice-done
  15.9 0.1 constant_dynamic-slice_fusion.3
  16.0 0.8 constant_dynamic-slice_fusion.5
  16.8 0.0 slice-done.1
  16.8 17.0 %all-to-all-done.1 = bf16[8,128,256]{2,1,0:T(8,128)(2,1)S(1)} async-done(((bf16[8,128,256]{2,1,0:T(8,128)(2,1)}), bf16[8,128,256]{2,1,0:T(8,128)(2,1)S(1)}, u32[]{:S(2)}, u32[]{:S(2)}) %all-to-all-start.1) | async-done | bytes 524320 | tf_op jit(solution)/shard_map/all_to_all | solution.py:339
  33.9 0.0 copy-start.2
  33.9 1.4 broadcast_in_dim.12
  35.3 0.0 copy-start.4
  35.3 0.0 copy-start.5
  35.3 0.0 copy-start.6
  35.3 0.0 copy-done.2
  35.3 8.9 %all-to-all-start = ((bf16[32,32,896]{2,1,0:T(8,128)(2,1)}), bf16[32,32,896]{2,1,0:T(8,128)(2,1)S(1)}, u32[]{:S(2)}, u32[]{:S(2)}) async-start(bf16[32,32,896]{2,1,0:T(8,128)(2,1)} %bitcast.45), calls=%async_computation | async-start | bytes 3670016 | tf_op jit(solution)/shard_map/all_to_all | solution.py:336
  44.2 0.0 copy-done.4
  44.3 0.1 dynamic_slice.39
  44.3 0.0 copy-done.5
  44.3 0.1 dynamic_slice.38
  44.4 0.0 copy-done.6
  44.4 0.1 dynamic_slice.36
  44.5 0.1 broadcast_in_dim.13
  44.6 0.1 stack_reshape.3
  44.7 0.8 dynamic_slice.37
  45.4 0.6 stack.31.refs_2_.refs_7_
  46.0 24.4 %all-to-all-done = bf16[32,32,896]{2,1,0:T(8,128)(2,1)S(1)} async-done(((bf16[32,32,896]{2,1,0:T(8,128)(2,1)}), bf16[32,32,896]{2,1,0:T(8,128)(2,1)S(1)}, u32[]{:S(2)}, u32[]{:S(2)}) %all-to-all-start) | async-done | bytes 1835040 | tf_op jit(solution)/shard_map/all_to_all | solution.py:336
  70.5 0.0 copy-start
  70.5 19.6 %all-gather.3.cloned.1.call-done = bf16[8,128,1024]{2,1,0:T(8,128)(2,1)} async-done(((bf16[1,128,1024]{2,1,0:T(8,128)(2,1)}), bf16[8,128,1024]{2,1,0:T(8,128)(2,1)}) %all-gather.3.cloned.1.call-update) | async-done | bytes 2097168 | tf_op jit(solution)/shard_map/all_gather | solution.py:338
  90.1 0.0 copy-done
  90.1 11.7 %forward_scan.1 = (f32[4,2,128,256]{3,2,1,0:T(8,128)}, f32[4,2,128,256]{3,2,1,0:T(8,128)}, f32[4,2,128,384]{3,2,1,0:T(8,128)}, f32[4,2,128,256]{3,2,1,0:T(8,128)...) custom-call(bf16[4,2,128,1024]{3,2,1,0:T(8,128)(2,1)} %bitcast.48, bf16[1024,896]{1,0:T(8,128)(2,1)} %bitcast.43, ...), custom_call_target="tpu_custom_call" | custom-call | tf_op jit(solution)/shard_map/forward_scan/pallas_call | solution.py:275
  101.8 0.8 slice.25
  102.5 29.6 %all-gather = f32[32,2,256]{2,1,0:T(2,128)S(1)} all-gather(f32[4,2,256]{2,1,0:T(2,128)S(1)} %slice.25), channel_id=2, replica_groups=mesh['yl'=2,'core'=2,'yh'=2,'x'=4,'z'=4] {'yl','core','yh'}, dimensions={0}, use_global_device_ids=true | all-gather | bytes 73728 | tf_op jit(solution)/shard_map/all_gather | solution.py:351
  132.1 0.6 pad.22.refs_6_
  132.8 0.0 copy-start.3
  132.8 14.8 %backward_scan.1 = (bf16[4,2,128,256]{3,2,1,0:T(8,128)(2,1)}, bf16[4,2,128,896]{3,2,1,0:T(8,128)(2,1)}) custom-call(f32[4,2,128,256]{3,2,1,0:T(8,128)} %get-tuple-element.12.refs_0_, f32[4,2,128,256]{3,2,1,0:T(8,128)} %get-tuple-element.13.refs_1_, f32[4,2,128,384]{3,2,1,0:T(8,128)} %get-tuple-element.14.refs_2_, ...), custom_call_target="tpu_custom_call" | custom-call | tf_op jit(solution)/shard_map/backward_scan/pallas_call | solution.py:295
  147.5 5.3 %all-to-all-start.2 = ((bf16[8,128,256]{2,1,0:T(8,128)(2,1)}), bf16[8,128,256]{2,1,0:T(8,128)(2,1)S(1)}, u32[]{:S(2)}, u32[]{:S(2)}) async-start(bf16[8,128,256]{2,1,0:T(8,128)(2,1)} %bitcast.54), calls=%async_computation.2 | async-start | bytes 1048576 | tf_op jit(solution)/shard_map/all_to_all | solution.py:361
  152.8 0.0 copy-done.3
  152.8 4.9 %convert_bitcast_fusion = bf16[1024,896]{0,1:T(8,128)(2,1)} fusion(bf16[1024,896]{1,0:T(8,128)(2,1)} %bitcast.63, bf16[1024,1024]{1,0:T(8,128)(2,1)S(1)} %bitcast.49), kind=kOutput, calls=%fused_computation.2 | convolution fusion | flops 1879965696 | bytes 5767168 | tf_op jit(solution)/shard_map/dot_general | solution.py:356
  157.7 3.8 %copy.28 = bf16[1024,896]{1,0:T(8,128)(2,1)} copy(bf16[1024,896]{0,1:T(8,128)(2,1)} %convert_bitcast_fusion) | data formatting | bytes 3670016 | tf_op jit(solution)/shard_map/convert_element_type | solution.py:356
  161.5 0.7 all-to-all-done.2
  162.2 0.0 copy-start.1
  162.2 12.9 %all-to-all-start.4 = ((bf16[128,8,896]{2,1,0:T(8,128)(2,1)}), bf16[128,8,896]{2,1,0:T(8,128)(2,1)}, u32[]{:S(2)}, u32[]{:S(2)}) async-start(bf16[128,8,896]{2,1,0:T(8,128)(2,1)} %bitcast.18), calls=%async_computation.4 | async-start | bytes 3670016 | tf_op jit(solution)/shard_map/all_to_all | solution.py:357
  175.1 0.0 copy-done.1
  175.1 5.2 %convolution_convert_fusion = bf16[1024,1024]{1,0:T(8,128)(2,1)} fusion(bf16[1024,896]{1,0:T(8,128)(2,1)} %bitcast.64, bf16[1024,896]{1,0:T(8,128)(2,1)S(1)} %bitcast.44), kind=kOutput, calls=%fused_computation.1 | convolution fusion | flops 1880096768 | bytes 5767168 | tf_op jit(solution)/shard_map/dot_general | solution.py:358
  180.3 20.7 %all-to-all-done.4 = bf16[128,8,896]{2,1,0:T(8,128)(2,1)} async-done(((bf16[128,8,896]{2,1,0:T(8,128)(2,1)}), bf16[128,8,896]{2,1,0:T(8,128)(2,1)}, u32[]{:S(2)}, u32[]{:S(2)}) %all-to-all-start.4) | async-done | bytes 1835040 | tf_op jit(solution)/shard_map/all_to_all | solution.py:357
  201.0 4.7 %all-to-all-start.3 = ((bf16[8,128,1024]{2,1,0:T(8,128)(2,1)}), bf16[8,128,1024]{2,1,0:T(8,128)(2,1)S(1)}, u32[]{:S(2)}, u32[]{:S(2)}) async-start(bf16[8,128,1024]{2,1,0:T(8,128)(2,1)} %bitcast.50), calls=%async_computation.3 | async-start | bytes 4194304 | tf_op jit(solution)/shard_map/all_to_all | solution.py:359
  205.7 0.3 copy.27
  206.0 1.0 reshape.53
  207.0 1.8 convert_reduce_fusion
  208.8 0.1 copy.30
  208.9 0.1 copy.32
  209.0 0.6 pad_maximum_fusion.4
  209.6 0.7 pad_maximum_fusion
  210.3 21.7 %all-to-all-done.3 = bf16[8,128,1024]{2,1,0:T(8,128)(2,1)S(1)} async-done(((bf16[8,128,1024]{2,1,0:T(8,128)(2,1)}), bf16[8,128,1024]{2,1,0:T(8,128)(2,1)S(1)}, u32[]{:S(2)}, u32[]{:S(2)}) %all-to-all-start.3) | async-done | bytes 2097184 | tf_op jit(solution)/shard_map/all_to_all | solution.py:359
  231.9 1.1 reduce_sum.40
  (8 shorter events, 0.1 us)
Async XLA Ops:
  7.2 8.8 %slice-start = ((bf16[32,288]{1,0:T(8,128)(2,1)}), bf16[32,32]{1,0:T(8,128)(2,1)S(1)}, s32[]{:S(2)}) async-start(bf16[32,288]{1,0:T(8,128)(2,1)} %param.11), calls=%async_computation.6 | async-start | bytes 16384 | tf_op jit(solution)/shard_map/slice | solution.py:322
  7.2 9.6 %slice-start.1 = ((bf16[32,288]{1,0:T(8,128)(2,1)}), bf16[32,256]{1,0:T(8,128)(2,1)S(1)}, s32[]{:S(2)}) async-start(bf16[32,288]{1,0:T(8,128)(2,1)} %param.11), calls=%async_computation.7 | async-start | bytes 32768 | tf_op jit(solution)/shard_map/slice | solution.py:327
  7.2 82.9 %all-gather.3.cloned.1.call-start = ((), (), s32[]{:S(2)}) async-start(), calls=%async_computation.5 | async-start | bytes 2359296 | tf_op jit(solution)/shard_map/all_gather | solution.py:338
  10.0 23.9 %all-to-all-start.1 = ((bf16[8,128,256]{2,1,0:T(8,128)(2,1)}), bf16[8,128,256]{2,1,0:T(8,128)(2,1)S(1)}, u32[]{:S(2)}, u32[]{:S(2)}) async-start(bf16[8,128,256]{2,1,0:T(8,128)(2,1)} %bitcast.42), calls=%async_computation.1 | async-start | bytes 1048576 | tf_op jit(solution)/shard_map/all_to_all | solution.py:339
  33.9 1.4 copy-start.2
  35.3 9.0 %copy-start.4 = (f32[32]{0:T(128)S(1)}, f32[32]{0:T(128)}, u32[]{:S(2)}) copy-start(f32[32]{0:T(128)} %param.12) | copy-start | bytes 388
  35.3 9.1 %copy-start.5 = (f32[32]{0:T(128)S(1)}, f32[32]{0:T(128)}, u32[]{:S(2)}) copy-start(f32[32]{0:T(128)} %param.13) | copy-start | bytes 388
  35.3 9.1 %copy-start.6 = (f32[32]{0:T(128)S(1)}, f32[32]{0:T(128)}, u32[]{:S(2)}) copy-start(f32[32]{0:T(128)} %param.14) | copy-start | bytes 388
  35.3 35.2 %all-to-all-start = ((bf16[32,32,896]{2,1,0:T(8,128)(2,1)}), bf16[32,32,896]{2,1,0:T(8,128)(2,1)S(1)}, u32[]{:S(2)}, u32[]{:S(2)}) async-start(bf16[32,32,896]{2,1,0:T(8,128)(2,1)} %bitcast.45), calls=%async_computation | async-start | bytes 3670016 | tf_op jit(solution)/shard_map/all_to_all | solution.py:336
  70.5 19.6 %copy-start = (bf16[32,32,896]{2,1,0:T(8,128)(2,1)}, bf16[32,32,896]{2,1,0:T(8,128)(2,1)S(1)}, u32[]{:S(2)}) copy-start(bf16[32,32,896]{2,1,0:T(8,128)(2,1)S(1)} %all-to-all-done) | copy-start | bytes 5505028
  132.8 20.1 %copy-start.3 = (bf16[8,128,1024]{2,1,0:T(8,128)(2,1)S(1)}, bf16[8,128,1024]{2,1,0:T(8,128)(2,1)}, u32[]{:S(2)}) copy-start(bf16[8,128,1024]{2,1,0:T(8,128)(2,1)} %all-gather.3.cloned.1.call-done) | copy-start | bytes 6291460
  147.5 14.6 %all-to-all-start.2 = ((bf16[8,128,256]{2,1,0:T(8,128)(2,1)}), bf16[8,128,256]{2,1,0:T(8,128)(2,1)S(1)}, u32[]{:S(2)}, u32[]{:S(2)}) async-start(bf16[8,128,256]{2,1,0:T(8,128)(2,1)} %bitcast.54), calls=%async_computation.2 | async-start | bytes 1048576 | tf_op jit(solution)/shard_map/all_to_all | solution.py:361
  162.2 12.9 %copy-start.1 = (bf16[32,32,896]{2,1,0:T(8,128)(2,1)S(1)}, bf16[32,32,896]{2,1,0:T(8,128)(2,1)}, u32[]{:S(2)}) copy-start(bf16[32,32,896]{2,1,0:T(8,128)(2,1)} %copy-done) | copy-start | bytes 5505028
  162.2 38.8 %all-to-all-start.4 = ((bf16[128,8,896]{2,1,0:T(8,128)(2,1)}), bf16[128,8,896]{2,1,0:T(8,128)(2,1)}, u32[]{:S(2)}, u32[]{:S(2)}) async-start(bf16[128,8,896]{2,1,0:T(8,128)(2,1)} %bitcast.18), calls=%async_computation.4 | async-start | bytes 3670016 | tf_op jit(solution)/shard_map/all_to_all | solution.py:357
  201.0 30.9 %all-to-all-start.3 = ((bf16[8,128,1024]{2,1,0:T(8,128)(2,1)}), bf16[8,128,1024]{2,1,0:T(8,128)(2,1)S(1)}, u32[]{:S(2)}, u32[]{:S(2)}) async-start(bf16[8,128,1024]{2,1,0:T(8,128)(2,1)} %bitcast.50), calls=%async_computation.3 | async-start | bytes 4194304 | tf_op jit(solution)/shard_map/all_to_all | solution.py:359
Sparse Core Ops, SparseCore 0:
  9.7 80.3 all-gather.2

commit v2 on v1

--- a/solution.py
+++ b/solution.py
@@ -146,10 +146,13 @@
 
 
 def backward_kernel(
-    xv_i, g_i, bc_i, y_i, st_i, cot, stat, par, out_o, d_o, grad_state, next_state, *, seqs, block, width, inner, total
+    xv_i, g_i, bc_i, y_i, st_i, cot, stat_0, stat_1, stat_2, stat_3, par, tok, weights,
+    out_o, near_o, far_o, term_o, grad_state, next_state, d_all, *, seqs, block, width, inner, total, chunks
 ):
     heads = inner // width
     step = pl.program_id(0)
+    chunk = chunks - 1 - step
+    rows = seqs * block
 
     @pl.when(step == 0)
     def _():
@@ -162,7 +165,7 @@
     upper = (iota((block, block), 1) >= iota((block, block), 0)).astype(f32).astype(bf16)
     skip, gain = par[0:1, :], par[1:2, :]
     bias_rate = par[3:4, :lanes]
-    sums = stat[0]
+    sums = (stat_0[0] + stat_1[0]) + (stat_2[0] + stat_3[0])
     scale_row = lax.rsqrt(sums[0:1] * (1.0 / total) + norm_eps)
     pull_row = scale_row * scale_row * scale_row * sums[1:2] * (1.0 / total)
     packed = jnp.concatenate([scale_row, pull_row, jnp.zeros((6, scale_row.shape[1]), f32)], axis=0)
@@ -243,7 +246,23 @@
         d_raw = (d_steps - d_log * bias_rate) * jax.nn.sigmoid(raw)
         d_values = back * step_wide + skip * d_y
         d_xv = d_values * (sig * (1.0 + xv * (1.0 - sig)))
-        d_o[0, s] = jnp.concatenate([d_xv, d_gate, d_b, d_c, d_raw], axis=1).astype(bf16)
+        start = pl.multiple_of(chunk * rows + s * block, block)
+        d_all[pl.ds(start, block), :] = jnp.concatenate([d_xv, d_gate, d_b, d_c, d_raw], axis=1).astype(bf16)
+
+    here = d_all[pl.ds(pl.multiple_of(chunk * rows, rows), rows), :]
+    partial = lax.dot_general(here, weights[...], NT, preferred_element_type=f32)
+    partial = partial.reshape(near_o.shape)
+    near_o[...] = partial
+    far_o[...] = partial.astype(bf16)
+
+    @pl.when(step == chunks - 1)
+    def _():
+        slab = 256
+        for first in range(0, term_o.shape[0], slab):
+            left = tok[:, :, :, first : first + slab].reshape(chunks * rows, slab)
+            term_o[first : first + slab, :] = lax.dot_general(
+                left, d_all[...], TN, preferred_element_type=f32
+            ).astype(bf16)
 
 
 def chunk_spec(shape, count=None):
@@ -284,24 +303,59 @@
     )(tok, weights, par, cot)
 
 
-def backward_call(xv, gate, bc, y, states, cot, stats, par, width, total):
+def backward_call(xv, gate, bc, y, states, cot, stats, par, tok, weights, width, total):
     chunks, seqs, block, inner = xv.shape
-    ins = (xv, gate, bc, y, states, cot, stats)
-    out_shapes = [(chunks, seqs, block, inner), (chunks, seqs, block, 2 * inner + 3 * lanes)]
+    model, columns = weights.shape
+    ins = (xv, gate, bc, y, states, cot) + tuple(stats)
+    fixed = (par, tok, weights)
+    split_spec = pl.BlockSpec((1, 1, seqs, block, model), lambda i: ((chunks - 1 - i) % 2, (chunks - 1 - i) // 2, 0, 0, 0))
+    split_shape = (2, chunks // 2, seqs, block, model)
 
     def kernel(*refs):
-        backward_kernel(*refs, seqs=seqs, block=block, width=width, inner=inner, total=total)
+        backward_kernel(*refs, seqs=seqs, block=block, width=width, inner=inner, total=total, chunks=chunks)
 
     return pl.pallas_call(
         kernel,
         grid=(chunks,),
-        in_specs=[chunk_spec(a.shape, chunks) for a in ins] + [fixed_spec(par.shape)],
-        out_specs=[chunk_spec(s, chunks) for s in out_shapes],
-        out_shape=[jax.ShapeDtypeStruct(s, bf16) for s in out_shapes],
-        scratch_shapes=[pltpu.VMEM((seqs, lanes, inner), f32), pltpu.VMEM((seqs, lanes, inner), f32)],
+        in_specs=[chunk_spec(a.shape, chunks) for a in ins] + [fixed_spec(a.shape) for a in fixed],
+        out_specs=[chunk_spec(xv.shape, chunks), split_spec, split_spec, fixed_spec((model, columns))],
+        out_shape=[
+            jax.ShapeDtypeStruct(xv.shape, bf16),
+            jax.ShapeDtypeStruct(split_shape, f32),
+            jax.ShapeDtypeStruct(split_shape, bf16),
+            jax.ShapeDtypeStruct((model, columns), bf16),
+        ],
+        scratch_shapes=[
+            pltpu.VMEM((seqs, lanes, inner), f32),
+            pltpu.VMEM((seqs, lanes, inner), f32),
+            pltpu.VMEM((chunks * seqs * block, columns), bf16),
+        ],
         compiler_params=pltpu.CompilerParams(vmem_limit_bytes=vmem),
         name="backward_scan",
-    )(*ins, par)
+    )(*ins, *fixed)
+
+
+def partner(a):
+    return lax.ppermute(a, "core", [(0, 1), (1, 0)])
+
+
+def around(give, mine):
+    came = [give(mine)]
+    spot = lambda y: (y % 2) * 2 + y // 2
+    for shift in (1, 3, 2):
+        pairs = [(spot(y), spot((y + shift) % 4)) for y in range(4)]
+        came.append(lax.ppermute(give((mine + shift) % 4), ("yl", "yh"), pairs))
+    return [came[0], came[1], came[3], came[2]]
+
+
+def in_order(came, mine):
+    turned = [came[0], came[3], came[2], came[1]]
+    return lax.dynamic_slice_in_dim(jnp.stack(turned + turned), 4 - mine, 4, 0)
+
+
+def by_core(own, other, core):
+    first = core == 0
+    return jnp.stack([jnp.where(first, own, other), jnp.where(first, other, own)])
 
 
 def body(tokens, cotangent, w_xz, w_bcdt, rate, dt_bias, skip, gain):
@@ -335,10 +389,19 @@
     copies = copies.reshape((owners,) + w_picked.shape[1:])
     weights = lax.all_to_all(copies, rows_axes, 0, 0, tiled=True).reshape(model, -1)
 
-    tok = lax.all_gather(tokens[0], group_axes, axis=0).reshape(chunks, seqs, block, model)
-    cot = lax.all_to_all(
-        cotangent[0].reshape(block, group, inner).transpose(1, 0, 2), group_axes, 0, 0, tiled=True
-    ).reshape(chunks, seqs, block, inner)
+    core = lax.axis_index("core")
+    here = lax.axis_index(("yh", "yl"))
+    at = lambda a, index: lax.dynamic_index_in_dim(a, index, 0, keepdims=False)
+
+    tok = in_order(around(lambda y: tokens[0], here), here)
+    tok = by_core(tok, partner(tok), core)
+    tok = tok.reshape(2, 2, 2, block, model).transpose(2, 0, 1, 3, 4).reshape(chunks, seqs, block, model)
+
+    cut = cotangent[0].reshape(block, 2, 2, 2, inner).transpose(2, 3, 1, 0, 4)
+    cut = cut.reshape(2, 4, block, inner)
+    cut = by_core(at(cut, core), partner(at(cut, 1 - core)), core)
+    cot = in_order(around(lambda y: lax.dynamic_index_in_dim(cut, y, 1, keepdims=False), here), here)
+    cot = cot.reshape(2, 2, 2, block, inner).transpose(1, 2, 0, 3, 4).reshape(chunks, seqs, block, inner)
 
     own = lambda a: lax.dynamic_slice_in_dim(a, mine * heads, heads, 0)
     padded = lambda a: jnp.pad(own(a), (0, inner - heads))
@@ -348,18 +411,23 @@
         + [jnp.zeros((inner,), f32)] * 4
     )
     xv, gate, bc, y, chunk_states, stats = forward_call(tok, weights, par, cot, width)
-    stats = lax.all_gather(stats[:, :2], group_axes, axis=0).sum(axis=0)
-    stats = jnp.pad(stats, ((0, 0), (0, 6), (0, 0)))
-    out, d_all = backward_call(xv, gate, bc, y, chunk_states, cot, stats, par, width, float(total))
-
-    flat_d = d_all.reshape(group * block, -1)
-    term = lax.dot_general(tok.reshape(group * block, model), flat_d, TN, preferred_element_type=f32).astype(bf16)
+    stats = stats + partner(stats)
+    stats = around(lambda y: stats, here)
+    out, near, far, term = backward_call(
+        xv, gate, bc, y, chunk_states, cot, stats, par, tok, weights, width, float(total)
+    )
     shares = lax.all_to_all(term.reshape(devices, model // devices, -1), whole, 0, 0, tiled=True)
-    partial_input = lax.dot_general(flat_d, weights, NT, preferred_element_type=f32).astype(bf16)
-    pieces = lax.all_to_all(partial_input.reshape(group, block, model), group_axes, 0, 0, tiled=True)
-    grad_input = pieces.astype(f32).sum(axis=0).astype(bf16)[None]
-    layer_out = lax.all_to_all(out.reshape(group, block, inner), group_axes, 0, 0, tiled=True)
-    layer_out = layer_out.transpose(1, 0, 2).reshape(1, block, total)
+
+    both = at(near, core) + partner(at(far, 1 - core)).astype(f32)
+    both = both.astype(bf16).transpose(1, 0, 2, 3).reshape(4, block, model)
+    came = around(lambda y: at(both, y), here)
+    grad_input = sum(a.astype(f32) for a in came).astype(bf16)[None]
+
+    given = out.reshape(2, 2, 2, block, inner).transpose(2, 0, 1, 3, 4).reshape(4, 2, block, inner)
+    came = in_order(around(lambda y: at(given, y), here), here)
+    pick = lambda index: lax.dynamic_index_in_dim(came, index, 1, keepdims=False)
+    layer_out = by_core(pick(core), partner(pick(1 - core)), core)
+    layer_out = layer_out.reshape(2, 2, 2, block, inner).transpose(3, 2, 0, 1, 4).reshape(1, block, total)
 
     summed = shares.reshape(group, devices // group, model // devices, -1).astype(f32).sum(axis=1)
     spread = lambda a: a.transpose(1, 0, 2).reshape(model // devices, -1)

time: 241 us -> 159 us (0.66)
  waiting for transfers between devices: 105 us -> 58 us
  blocking collectives: 29.6 us -> 0 us
  between operations: 14.2 us -> 1.12 us
  matrix products: 10.1 us -> 0 us
  Pallas kernels: 26.5 us -> 33.9 us
  starting transfers between devices: 37.8 us -> 43.7 us
  local copies, waits for them, and re-layouts: 12.8 us -> 15.4 us
    ppermute x0 -> x20, waiting for transfers between devices: none -> 57.9 us  [the longest x15 56.9 us: around(): came.append(lax.ppermute(give((mine + shift) % 4), ('yl', 'yh'), pairs))]
    all_to_all x3 -> x0, waiting for transfers between devices: 39.4 us -> none  [the longest x1 21.7 us: body(): lax.all_to_all(partial_input.reshape(group, block, model), group_axes, 0,...]
    all_gather x1 -> x0, blocking collectives: 29.6 us -> none  [body(): stats = lax.all_gather(stats[:, :2], group_axes, axis=0).sum(axis=0)]
    ppermute x0 -> x20, starting transfers between devices: none -> 27.9 us  [the longest x15 23 us: around(): came.append(lax.ppermute(give((mine + shift) % 4), ('yl', 'yh'), pairs))]
    all_to_all x1, waiting for transfers between devices: 24.4 us -> 0.01 us  [body(): lax.all_to_all(copies, rows_axes, 0, 0, tiled=True).reshape(model, -1)]
    all_to_all x1, waiting for transfers between devices: 20.7 us -> 0.01 us  [body(): lax.all_to_all(term.reshape(devices, model // devices, -1), whole, 0, 0,...]
    all_gather x1 -> x0, waiting for transfers between devices: 19.6 us -> none  [body(): lax.all_gather(tokens[0], group_axes, axis=0)]
    all_to_all x3 -> x0, starting transfers between devices: 15.9 us -> none  [the longest x1 5.97 us: body(): lax.all_to_all(cotangent[0].reshape(block, group, inner).transpose(1, 0,...]
  transfers between devices with their start and end apart: 6 -> 22, of which waited for: 6 -> 12; matrix products, arithmetic and copies ran while one was open for 10% -> 11% of each run, Pallas kernels for 0% -> 0%
where the time goes in v2:
time: 159 us; the launch traced here: 158 us
  waiting for transfers between devices  58 us (36%)
  starting transfers between devices  43.7 us (27%)
  Pallas kernels  33.9 us (21%)
  local copies, waits for them, and re-layouts  15.4 us (10%)
  other arithmetic  6.17 us (4%)
    ppermute x15, waiting for transfers between devices, around(): came.append(lax.ppermute(give((mine + shift) % 4), ('yl', 'yh'), pairs))  56.9 us
    ppermute x15, starting transfers between devices, around(): came.append(lax.ppermute(give((mine + shift) % 4), ('yl', 'yh'), pairs))  23 us
    pallas_call x1, Pallas kernels, backward_call(): pl.pallas_call(kernel, grid=(chunks,), in_specs=[chunk_spec(a.shape, chun...  22.3 us
    pallas_call x1, Pallas kernels, forward_call(): pl.pallas_call(kernel, grid=(chunks,), in_specs=[chunk_spec(tok.shape), f...  11.7 us
    all_to_all x1, starting transfers between devices, body(): lax.all_to_all(copies, rows_axes, 0, 0, tiled=True).reshape(model, -1)  9.4 us
    all_to_all x1, starting transfers between devices, body(): lax.all_to_all(term.reshape(devices, model // devices, -1), whole, 0, 0,...  6.39 us
    unnamed x44, local copies, waits for them, and re-layouts  5.49 us
    ppermute x5, starting transfers between devices, partner(): return lax.ppermute(a, 'core', [(0, 1), (1, 0)])  4.91 us
  transfers between devices with their start and end apart: 22, of which 12 were waited for; matrix products, arithmetic and copies ran while one was open for 11% of the time, Pallas kernels for 0%

profile of v2, /device:TPU:1, one launch (start us, length us, event | category | flops | bytes accessed | tf_op | source)
XLA Modules:
  0.0 158.3 jit_solution(13007610508884458679)
XLA Ops:
  0.7 3.6 %collective-permute-start = (bf16[128,1024]{1,0:T(8,128)(2,1)}, bf16[128,1024]{1,0:T(8,128)(2,1)S(1)}, u32[]{:S(2)}, u32[]{:S(2)}) collective-permute-start(bf16[128,1024]{1,0:T(8,128)(2,1)} %bitcast.149), channel_id=1, source_target_pairs={{0,80},{64,0},{16,64},{80,16},{1,81},{65,1},{17,65},{81,17},{2,82}... | collective-permute-start | bytes 786440 | tf_op jit(solution)/shard_map/ppermute | solution.py:347
  4.3 0.3 collective-permute-start.1
  4.6 0.7 collective-permute-start.2
  5.3 1.3 copy.47
  6.6 0.2 copy.48
  6.9 0.7 dynamic-slice_bitcast_fusion.5
  7.6 1.5 collective-permute-start.4
  9.1 0.1 constant_dynamic-slice_fusion.4
  9.2 0.8 constant_dynamic-slice_fusion.6
  10.0 1.4 broadcast_in_dim.12
  11.4 9.4 %all-to-all-start = ((bf16[32,32,896]{2,1,0:T(8,128)(2,1)}), bf16[32,32,896]{2,1,0:T(8,128)(2,1)S(1)}, u32[]{:S(2)}, u32[]{:S(2)}) async-start(bf16[32,32,896]{2,1,0:T(8,128)(2,1)} %bitcast.134), calls=%async_computation | async-start | bytes 3670016 | tf_op jit(solution)/shard_map/all_to_all | solution.py:390
  20.9 0.1 dynamic_slice.107
  21.1 0.1 stack_reshape.3
  21.1 0.1 dynamic_slice.109
  21.2 0.1 dynamic_slice.110
  21.3 0.8 dynamic_slice.108
  22.1 0.6 stack.116.refs_2_.refs_10_
  22.7 1.0 fusion.6
  23.8 3.1 %collective-permute-start.5 = (bf16[2,128,256]{2,1,0:T(8,128)(2,1)S(1)}, bf16[2,128,256]{2,1,0:T(8,128)(2,1)S(1)}, u32[]{:S(2)}, u32[]{:S(2)}) collective-permute-start(bf16[2,128,256]{2,1,0:T(8,128)(2,1)S(1)} %get-tuple-element.50), channel_id=1, source_target_pairs={{0,80},{64,0},{16,64},{80,16},{1,81},{65,1},{17,65},{81,17},{2,82}... | collective-permute-start | bytes 393224 | tf_op jit(solution)/shard_map/ppermute | solution.py:347
  26.9 0.7 collective-permute-start.7
  27.8 0.1 constant_dynamic-slice_fusion.7
  27.9 1.3 collective-permute-start.3
  29.2 16.3 %collective-permute-done.5 = bf16[2,128,256]{2,1,0:T(8,128)(2,1)S(1)} collective-permute-done((bf16[2,128,256]{2,1,0:T(8,128)(2,1)S(1)}, bf16[2,128,256]{2,1,0:T(8,128)(2,1)S(1)}, u32[]{:S(2)}, u32[]{:S(2)}) %collective-permute-start.5) | collective-permute-done | bytes 131104 | tf_op jit(solution)/shard_map/ppermute | solution.py:347
  45.5 1.7 %collective-permute-done.6 = bf16[2,128,256]{2,1,0:T(8,128)(2,1)S(1)} collective-permute-done((bf16[2,128,256]{2,1,0:T(8,128)(2,1)S(1)}, bf16[2,128,256]{2,1,0:T(8,128)(2,1)S(1)}, u32[]{:S(2)}, u32[]{:S(2)}) %collective-permute-start.6) | collective-permute-done | bytes 131104 | tf_op jit(solution)/shard_map/ppermute | solution.py:347
  47.2 2.9 %collective-permute-done.7 = bf16[2,128,256]{2,1,0:T(8,128)(2,1)S(1)} collective-permute-done((bf16[2,128,256]{2,1,0:T(8,128)(2,1)S(1)}, bf16[2,128,256]{2,1,0:T(8,128)(2,1)S(1)}, u32[]{:S(2)}, u32[]{:S(2)}) %collective-permute-start.7) | collective-permute-done | bytes 131104 | tf_op jit(solution)/shard_map/ppermute | solution.py:347
  50.2 0.8 copy.49
  51.1 0.1 broadcast_select_fusion.1
  51.2 0.2 pad_maximum_fusion
  51.4 1.5 copy.58
  53.0 1.2 copy-done
  54.2 11.7 %forward_scan.1 = (f32[4,2,128,256]{3,2,1,0:T(8,128)}, f32[4,2,128,256]{3,2,1,0:T(8,128)}, f32[4,2,128,384]{3,2,1,0:T(8,128)}, f32[4,2,128,256]{3,2,1,0:T(8,128)...) custom-call(bf16[4,2,128,1024]{3,2,1,0:T(8,128)(2,1)} %bitcast.130, bf16[1024,896]{1,0:T(8,128)(2,1)} %bitcast.132, ...), custom_call_target="tpu_custom_call" | custom-call | tf_op jit(solution)/shard_map/forward_scan/pallas_call | solution.py:294
  65.9 0.6 collective-permute-start.8
  66.5 1.1 collective-permute-done.8
  67.6 0.8 add.186.refs_6_
  68.3 3.2 %collective-permute-start.10 = (f32[4,8,256]{2,1,0:T(8,128)S(1)}, f32[4,8,256]{2,1,0:T(8,128)S(1)}, u32[]{:S(2)}, u32[]{:S(2)}) collective-permute-start(f32[4,8,256]{2,1,0:T(8,128)S(1)} %add.186.refs_6_), channel_id=1, source_target_pairs={{0,16},{64,80},{16,0},{80,64},{1,17},{65,81},{17,1},{81,65},{2,18}... | collective-permute-start | bytes 98312 | tf_op jit(solution)/shard_map/ppermute | solution.py:347
  71.6 3.9 %collective-permute-start.11 = (f32[4,8,256]{2,1,0:T(8,128)S(1)}, f32[4,8,256]{2,1,0:T(8,128)S(1)}, u32[]{:S(2)}, u32[]{:S(2)}) collective-permute-start(f32[4,8,256]{2,1,0:T(8,128)S(1)} %add.186.refs_6_), channel_id=1, source_target_pairs={{0,80},{64,0},{16,64},{80,16},{1,81},{65,1},{17,65},{81,17},{2,82}... | collective-permute-start | bytes 98312 | tf_op jit(solution)/shard_map/ppermute | solution.py:347
  75.5 1.0 collective-permute-done.11.refs_9_
  76.5 2.9 %collective-permute-done.9.refs_7_ = f32[4,8,256]{2,1,0:T(8,128)S(1)} collective-permute-done((f32[4,8,256]{2,1,0:T(8,128)S(1)}, f32[4,8,256]{2,1,0:T(8,128)S(1)}, u32[]{:S(2)}, u32[]{:S(2)}) %collective-permute-start.9) | collective-permute-done | bytes 32800 | tf_op jit(solution)/shard_map/ppermute | solution.py:347
  79.4 0.6 copy-done.8
  80.0 22.3 %backward_scan.1 = (bf16[4,2,128,256]{3,2,1,0:T(8,128)(2,1)}, f32[2,2,2,128,1024]{4,3,2,1,0:T(8,128)}, bf16[2,2,2,128,1024]{4,3,2,1,0:T(8,128)(2,1)}, bf16[1024,896]{1,0:T(8,128)(2,1)}) custom-call(f32[4,2,128,256]{3,2,1,0:T(8,128)} %get-tuple-element.14.refs_0_, f32[4,2,128,256]{3,2,1,0:T(8,128)} %get-tuple-element.15.refs_1_, ...), custom_call_target="tpu_custom_call" | custom-call | tf_op jit(solution)/shard_map/backward_scan/pallas_call | solution.py:317
  102.3 6.4 %all-to-all-start.1 = ((bf16[128,8,896]{2,1,0:T(8,128)(2,1)}), bf16[128,8,896]{2,1,0:T(8,128)(2,1)S(1)}, u32[]{:S(2)}, u32[]{:S(2)}) async-start(bf16[128,8,896]{2,1,0:T(8,128)(2,1)} %bitcast.148), calls=%async_computation.1 | async-start | bytes 3670016 | tf_op jit(solution)/shard_map/all_to_all | solution.py:419
  108.8 2.7 %collective-permute-start.12 = (bf16[2,128,256]{2,1,0:T(8,128)(2,1)S(1)}, bf16[2,128,256]{2,1,0:T(8,128)(2,1)S(1)}, u32[]{:S(2)}, u32[]{:S(2)}) collective-permute-start(bf16[2,128,256]{2,1,0:T(8,128)(2,1)S(1)} %get-tuple-element.48), channel_id=1, source_target_pairs={{0,80},{64,0},{16,64},{80,16},{1,81},{65,1},{17,65},{81,17},{2,82}... | collective-permute-start | bytes 393224 | tf_op jit(solution)/shard_map/ppermute | solution.py:347
  111.6 0.7 collective-permute-start.16
  112.4 1.4 collective-permute-start.13
  113.7 0.3 collective-permute-start.14
  114.1 18.6 %collective-permute-done.12 = bf16[2,128,256]{2,1,0:T(8,128)(2,1)S(1)} collective-permute-done((bf16[2,128,256]{2,1,0:T(8,128)(2,1)S(1)}, bf16[2,128,256]{2,1,0:T(8,128)(2,1)S(1)}, u32[]{:S(2)}, u32[]{:S(2)}) %collective-permute-start.12) | collective-permute-done | bytes 131104 | tf_op jit(solution)/shard_map/ppermute | solution.py:347
  132.7 1.8 %collective-permute-done.13 = bf16[2,128,256]{2,1,0:T(8,128)(2,1)S(1)} collective-permute-done((bf16[2,128,256]{2,1,0:T(8,128)(2,1)S(1)}, bf16[2,128,256]{2,1,0:T(8,128)(2,1)S(1)}, u32[]{:S(2)}, u32[]{:S(2)}) %collective-permute-start.13) | collective-permute-done | bytes 131104 | tf_op jit(solution)/shard_map/ppermute | solution.py:347
  134.5 2.5 %collective-permute-done.14 = bf16[2,128,256]{2,1,0:T(8,128)(2,1)S(1)} collective-permute-done((bf16[2,128,256]{2,1,0:T(8,128)(2,1)S(1)}, bf16[2,128,256]{2,1,0:T(8,128)(2,1)S(1)}, u32[]{:S(2)}, u32[]{:S(2)}) %collective-permute-start.14) | collective-permute-done | bytes 131104 | tf_op jit(solution)/shard_map/ppermute | solution.py:347
  137.1 0.8 collective-permute-start.15
  137.8 0.4 fusion.1
  138.3 0.9 dynamic-slice_bitcast_fusion.3
  139.2 0.6 collective-permute-start.17
  139.8 1.7 %collective-permute-start.18 = (bf16[128,1024]{1,0:T(8,128)(2,1)}, bf16[128,1024]{1,0:T(8,128)(2,1)}, u32[]{:S(2)}, u32[]{:S(2)}) collective-permute-start(bf16[128,1024]{1,0:T(8,128)(2,1)} %get-tuple-element.42), channel_id=1, source_target_pairs={{0,16},{64,80},{16,0},{80,64},{1,17},{65,81},{17,1},{81,65},{2,18}... | collective-permute-start | bytes 786440 | tf_op jit(solution)/shard_map/ppermute | solution.py:347
  141.6 0.7 collective-permute-start.19
  142.3 1.0 copy.51
  143.3 2.0 %copy.57 = bf16[1,128,2048]{2,1,0:T(8,128)(2,1)} copy(bf16[1,128,2048]{1,2,0:T(8,128)(2,1)} %bitcast.146) | data formatting | bytes 1048576
  145.4 3.6 %collective-permute-done.17 = bf16[128,1024]{1,0:T(8,128)(2,1)} collective-permute-done((bf16[128,1024]{1,0:T(8,128)(2,1)}, bf16[128,1024]{1,0:T(8,128)(2,1)}, u32[]{:S(2)}, u32[]{:S(2)}) %collective-permute-start.17) | collective-permute-done | bytes 262176 | tf_op jit(solution)/shard_map/ppermute | solution.py:347
  149.0 5.0 %collective-permute-done.18 = bf16[128,1024]{1,0:T(8,128)(2,1)} collective-permute-done((bf16[128,1024]{1,0:T(8,128)(2,1)}, bf16[128,1024]{1,0:T(8,128)(2,1)}, u32[]{:S(2)}, u32[]{:S(2)}) %collective-permute-start.18) | collective-permute-done | bytes 262176 | tf_op jit(solution)/shard_map/ppermute | solution.py:347
  154.0 0.6 collective-permute-done.19
  154.6 2.0 %fusion.5 = bf16[1,128,1024]{2,1,0:T(8,128)(2,1)} fusion(bf16[128,1024]{1,0:T(8,128)(2,1)} %collective-permute-done.19, bf16[128,1024]{1,0:T(8,128)(2,1)} %collective-permute-done.18, bf16[128,1024]{1,0:T(8,128)(2,1)} %collective-permute-done.17, bf16[4,128,1024]{2,1,0:T(8,128)(2,1)S(1)} %bitcast.138, s32[]{:T(128)S(6)} %select_n.150), kind=kLoop, calls=%fused_computation.21 | loop fusion | flops 1048576 | bytes 1310724 | tf_op jit(solution)/shard_map/broadcast_in_dim | solution.py:424
  156.5 0.2 convert_reduce_fusion
  156.8 0.1 copy.54
  157.0 0.6 pad_maximum_fusion.5
  157.6 0.7 pad_maximum_fusion.1
  (79 shorter events, 1.0 us)
Async XLA Ops:
  0.6 8.5 %slice-start = ((bf16[32,288]{1,0:T(8,128)(2,1)}), bf16[32,32]{1,0:T(8,128)(2,1)S(1)}, s32[]{:S(2)}) async-start(bf16[32,288]{1,0:T(8,128)(2,1)} %param.11), calls=%async_computation.2 | async-start | bytes 16384 | tf_op jit(solution)/shard_map/slice | solution.py:376
  0.6 9.3 %slice-start.1 = ((bf16[32,288]{1,0:T(8,128)(2,1)}), bf16[32,256]{1,0:T(8,128)(2,1)S(1)}, s32[]{:S(2)}) async-start(bf16[32,288]{1,0:T(8,128)(2,1)} %param.11), calls=%async_computation.3 | async-start | bytes 32768 | tf_op jit(solution)/shard_map/slice | solution.py:381
  0.7 26.3 %collective-permute-start = (bf16[128,1024]{1,0:T(8,128)(2,1)}, bf16[128,1024]{1,0:T(8,128)(2,1)S(1)}, u32[]{:S(2)}, u32[]{:S(2)}) collective-permute-start(bf16[128,1024]{1,0:T(8,128)(2,1)} %bitcast.149), channel_id=1, source_target_pairs={{0,80},{64,0},{16,64},{80,16},{1,81},{65,1},{17,65},{81,17},{2,82}... | collective-permute-start | bytes 786440 | tf_op jit(solution)/shard_map/ppermute | solution.py:347
  4.3 23.3 %collective-permute-start.1 = (bf16[128,1024]{1,0:T(8,128)(2,1)}, bf16[128,1024]{1,0:T(8,128)(2,1)S(1)}, u32[]{:S(2)}, u32[]{:S(2)}) collective-permute-start(bf16[128,1024]{1,0:T(8,128)(2,1)} %bitcast.150), channel_id=1, source_target_pairs={{0,16},{64,80},{16,0},{80,64},{1,17},{65,81},{17,1},{81,65},{2,18}... | collective-permute-start | bytes 786440 | tf_op jit(solution)/shard_map/ppermute | solution.py:347
  4.6 23.0 %collective-permute-start.2 = (bf16[128,1024]{1,0:T(8,128)(2,1)}, bf16[128,1024]{1,0:T(8,128)(2,1)S(1)}, u32[]{:S(2)}, u32[]{:S(2)}) collective-permute-start(bf16[128,1024]{1,0:T(8,128)(2,1)} %bitcast.151), channel_id=1, source_target_pairs={{0,64},{64,16},{16,80},{80,0},{1,65},{65,17},{17,81},{81,1},{2,66}... | collective-permute-start | bytes 786440 | tf_op jit(solution)/shard_map/ppermute | solution.py:347
  7.6 15.1 %collective-permute-start.4 = (bf16[4,128,256]{2,1,0:T(8,128)(2,1)}, bf16[4,128,256]{2,1,0:T(8,128)(2,1)}, u32[]{:S(2)}, u32[]{:S(2)}) collective-permute-start(bf16[4,128,256]{2,1,0:T(8,128)(2,1)} %dynamic-slice_bitcast_fusion.5), channel_id=1, source_target_pairs={{0,32},{32,0},{1,33},{33,1},{2,34},{34,2},{3,35},{35,3},{4,36},{36... | collective-permute-start | bytes 786440 | tf_op jit(solution)/shard_map/ppermute | solution.py:339
  11.4 9.5 %copy-start.9 = (f32[32]{0:T(128)S(1)}, f32[32]{0:T(128)}, u32[]{:S(2)}) copy-start(f32[32]{0:T(128)} %param.14) | copy-start | bytes 388
  11.4 9.7 %copy-start.10 = (f32[32]{0:T(128)S(1)}, f32[32]{0:T(128)}, u32[]{:S(2)}) copy-start(f32[32]{0:T(128)} %param.13) | copy-start | bytes 388
  11.4 9.8 %copy-start.11 = (f32[32]{0:T(128)S(1)}, f32[32]{0:T(128)}, u32[]{:S(2)}) copy-start(f32[32]{0:T(128)} %param.12) | copy-start | bytes 388
  11.4 11.3 %copy-start.2 = (bf16[1,128,1024]{2,1,0:T(8,128)(2,1)S(1)}, bf16[1,128,1024]{2,1,0:T(8,128)(2,1)}, u32[]{:S(2)}) copy-start(bf16[1,128,1024]{2,1,0:T(8,128)(2,1)} %param.8) | copy-start | bytes 786436
  11.4 41.5 %all-to-all-start = ((bf16[32,32,896]{2,1,0:T(8,128)(2,1)}), bf16[32,32,896]{2,1,0:T(8,128)(2,1)S(1)}, u32[]{:S(2)}, u32[]{:S(2)}) async-start(bf16[32,32,896]{2,1,0:T(8,128)(2,1)} %bitcast.134), calls=%async_computation | async-start | bytes 3670016 | tf_op jit(solution)/shard_map/all_to_all | solution.py:390
  23.8 21.8 %collective-permute-start.5 = (bf16[2,128,256]{2,1,0:T(8,128)(2,1)S(1)}, bf16[2,128,256]{2,1,0:T(8,128)(2,1)S(1)}, u32[]{:S(2)}, u32[]{:S(2)}) collective-permute-start(bf16[2,128,256]{2,1,0:T(8,128)(2,1)S(1)} %get-tuple-element.50), channel_id=1, source_target_pairs={{0,80},{64,0},{16,64},{80,16},{1,81},{65,1},{17,65},{81,17},{2,82}... | collective-permute-start | bytes 393224 | tf_op jit(solution)/shard_map/ppermute | solution.py:347
  26.9 20.3 %collective-permute-start.6 = (bf16[2,128,256]{2,1,0:T(8,128)(2,1)S(1)}, bf16[2,128,256]{2,1,0:T(8,128)(2,1)S(1)}, u32[]{:S(2)}, u32[]{:S(2)}) collective-permute-start(bf16[2,128,256]{2,1,0:T(8,128)(2,1)S(1)} %get-tuple-element.51), channel_id=1, source_target_pairs={{0,16},{64,80},{16,0},{80,64},{1,17},{65,81},{17,1},{81,65},{2,18}... | collective-permute-start | bytes 393224 | tf_op jit(solution)/shard_map/ppermute | solution.py:347
  26.9 23.2 %collective-permute-start.7 = (bf16[2,128,256]{2,1,0:T(8,128)(2,1)S(1)}, bf16[2,128,256]{2,1,0:T(8,128)(2,1)S(1)}, u32[]{:S(2)}, u32[]{:S(2)}) collective-permute-start(bf16[2,128,256]{2,1,0:T(8,128)(2,1)S(1)} %get-tuple-element.49), channel_id=1, source_target_pairs={{0,64},{64,16},{16,80},{80,0},{1,65},{65,17},{17,81},{81,1},{2,66}... | collective-permute-start | bytes 393224 | tf_op jit(solution)/shard_map/ppermute | solution.py:347
  27.9 23.2 %collective-permute-start.3 = (bf16[4,128,1024]{2,1,0:T(8,128)(2,1)S(1)}, bf16[4,128,1024]{2,1,0:T(8,128)(2,1)S(1)}, u32[]{:S(2)}, u32[]{:S(2)}) collective-permute-start(bf16[4,128,1024]{2,1,0:T(8,128)(2,1)S(1)} %constant_dynamic-slice_fusion.7), channel_id=1, source_target_pairs={{0,32},{32,0},{1,33},{33,1},{2,34},{34,2},{3,35},{35,3},{4,36},{36... | collective-permute-start | bytes 3145736 | tf_op jit(solution)/shard_map/ppermute | solution.py:339
  53.0 1.2 copy-start
  65.9 1.6 %collective-permute-start.8 = (f32[4,8,256]{2,1,0:T(8,128)}, f32[4,8,256]{2,1,0:T(8,128)S(1)}, u32[]{:S(2)}, u32[]{:S(2)}) collective-permute-start(f32[4,8,256]{2,1,0:T(8,128)} %get-tuple-element.19), channel_id=1, source_target_pairs={{0,32},{32,0},{1,33},{33,1},{2,34},{34,2},{3,35},{35,3},{4,36},{36... | collective-permute-start | bytes 98312 | tf_op jit(solution)/shard_map/ppermute | solution.py:339
  68.3 11.1 %copy-start.5 = (f32[4,8,256]{2,1,0:T(8,128)}, f32[4,8,256]{2,1,0:T(8,128)S(1)}, u32[]{:S(2)}) copy-start(f32[4,8,256]{2,1,0:T(8,128)S(1)} %add.186.refs_6_) | copy-start | bytes 98308
  68.3 7.1 %collective-permute-start.10 = (f32[4,8,256]{2,1,0:T(8,128)S(1)}, f32[4,8,256]{2,1,0:T(8,128)S(1)}, u32[]{:S(2)}, u32[]{:S(2)}) collective-permute-start(f32[4,8,256]{2,1,0:T(8,128)S(1)} %add.186.refs_6_), channel_id=1, source_target_pairs={{0,16},{64,80},{16,0},{80,64},{1,17},{65,81},{17,1},{81,65},{2,18}... | collective-permute-start | bytes 98312 | tf_op jit(solution)/shard_map/ppermute | solution.py:347
  71.6 4.9 %collective-permute-start.11 = (f32[4,8,256]{2,1,0:T(8,128)S(1)}, f32[4,8,256]{2,1,0:T(8,128)S(1)}, u32[]{:S(2)}, u32[]{:S(2)}) collective-permute-start(f32[4,8,256]{2,1,0:T(8,128)S(1)} %add.186.refs_6_), channel_id=1, source_target_pairs={{0,80},{64,0},{16,64},{80,16},{1,81},{65,1},{17,65},{81,17},{2,82}... | collective-permute-start | bytes 98312 | tf_op jit(solution)/shard_map/ppermute | solution.py:347
  75.5 4.0 %collective-permute-start.9 = (f32[4,8,256]{2,1,0:T(8,128)S(1)}, f32[4,8,256]{2,1,0:T(8,128)S(1)}, u32[]{:S(2)}, u32[]{:S(2)}) collective-permute-start(f32[4,8,256]{2,1,0:T(8,128)S(1)} %add.186.refs_6_), channel_id=1, source_target_pairs={{0,64},{64,16},{16,80},{80,0},{1,65},{65,17},{17,81},{81,1},{2,66}... | collective-permute-start | bytes 98312 | tf_op jit(solution)/shard_map/ppermute | solution.py:347
  75.5 4.0 %copy-start.6 = (f32[4,8,256]{2,1,0:T(8,128)}, f32[4,8,256]{2,1,0:T(8,128)S(1)}, u32[]{:S(2)}) copy-start(f32[4,8,256]{2,1,0:T(8,128)S(1)} %collective-permute-done.10.refs_8_) | copy-start | bytes 98308
  76.5 3.0 %copy-start.7 = (f32[4,8,256]{2,1,0:T(8,128)}, f32[4,8,256]{2,1,0:T(8,128)S(1)}, u32[]{:S(2)}) copy-start(f32[4,8,256]{2,1,0:T(8,128)S(1)} %collective-permute-done.11.refs_9_) | copy-start | bytes 98308
  79.4 0.6 copy-start.8
  102.3 6.4 %copy-start.4 = (bf16[4,2,128,256]{3,2,1,0:T(8,128)(2,1)S(1)}, bf16[4,2,128,256]{3,2,1,0:T(8,128)(2,1)}, u32[]{:S(2)}) copy-start(bf16[4,2,128,256]{3,2,1,0:T(8,128)(2,1)} %get-tuple-element.20) | copy-start | bytes 1572868
  102.3 54.2 %all-to-all-start.1 = ((bf16[128,8,896]{2,1,0:T(8,128)(2,1)}), bf16[128,8,896]{2,1,0:T(8,128)(2,1)S(1)}, u32[]{:S(2)}, u32[]{:S(2)}) async-start(bf16[128,8,896]{2,1,0:T(8,128)(2,1)} %bitcast.148), calls=%async_computation.1 | async-start | bytes 3670016 | tf_op jit(solution)/shard_map/all_to_all | solution.py:419
  108.7 2.8 %copy-start.3 = (bf16[2,2,2,128,1024]{4,3,2,1,0:T(8,128)(2,1)S(1)}, bf16[2,2,2,128,1024]{4,3,2,1,0:T(8,128)(2,1)}, u32[]{:S(2)}) copy-start(bf16[2,2,2,128,1024]{4,3,2,1,0:T(8,128)(2,1)} %get-tuple-element.22) | copy-start | bytes 6291460
  108.8 23.8 %collective-permute-start.12 = (bf16[2,128,256]{2,1,0:T(8,128)(2,1)S(1)}, bf16[2,128,256]{2,1,0:T(8,128)(2,1)S(1)}, u32[]{:S(2)}, u32[]{:S(2)}) collective-permute-start(bf16[2,128,256]{2,1,0:T(8,128)(2,1)S(1)} %get-tuple-element.48), channel_id=1, source_target_pairs={{0,80},{64,0},{16,64},{80,16},{1,81},{65,1},{17,65},{81,17},{2,82}... | collective-permute-start | bytes 393224 | tf_op jit(solution)/shard_map/ppermute | solution.py:347
  111.6 26.3 %copy-start.1 = (f32[2,2,2,128,1024]{4,3,2,1,0:T(8,128)S(1)}, f32[2,2,2,128,1024]{4,3,2,1,0:T(8,128)}, u32[]{:S(2)}) copy-start(f32[2,2,2,128,1024]{4,3,2,1,0:T(8,128)} %get-tuple-element.21) | copy-start | bytes 12582916
  111.6 26.2 %collective-permute-start.16 = (bf16[2,2,128,1024]{3,2,1,0:T(8,128)(2,1)S(1)}, bf16[2,2,128,1024]{3,2,1,0:T(8,128)(2,1)S(1)}, u32[]{:S(2)}, u32[]{:S(2)}) collective-permute-start(bf16[2,2,128,1024]{3,2,1,0:T(8,128)(2,1)S(1)} %dynamic-slice_bitcast_fusion), channel_id=1, source_target_pairs={{0,32},{32,0},{1,33},{33,1},{2,34},{34,2},{3,35},{35,3},{4,36},{36... | collective-permute-start | bytes 3145736 | tf_op jit(solution)/shard_map/ppermute | solution.py:339
  112.4 22.1 %collective-permute-start.13 = (bf16[2,128,256]{2,1,0:T(8,128)(2,1)S(1)}, bf16[2,128,256]{2,1,0:T(8,128)(2,1)S(1)}, u32[]{:S(2)}, u32[]{:S(2)}) collective-permute-start(bf16[2,128,256]{2,1,0:T(8,128)(2,1)S(1)} %get-tuple-element.47), channel_id=1, source_target_pairs={{0,16},{64,80},{16,0},{80,64},{1,17},{65,81},{17,1},{81,65},{2,18}... | collective-permute-start | bytes 393224 | tf_op jit(solution)/shard_map/ppermute | solution.py:347
  113.7 23.2 %collective-permute-start.14 = (bf16[2,128,256]{2,1,0:T(8,128)(2,1)S(1)}, bf16[2,128,256]{2,1,0:T(8,128)(2,1)S(1)}, u32[]{:S(2)}, u32[]{:S(2)}) collective-permute-start(bf16[2,128,256]{2,1,0:T(8,128)(2,1)S(1)} %get-tuple-element.45), channel_id=1, source_target_pairs={{0,64},{64,16},{16,80},{80,0},{1,65},{65,17},{17,81},{81,1},{2,66}... | collective-permute-start | bytes 393224 | tf_op jit(solution)/shard_map/ppermute | solution.py:347
  137.1 5.1 %collective-permute-start.15 = (bf16[4,128,256]{2,1,0:T(8,128)(2,1)S(1)}, bf16[4,128,256]{2,1,0:T(8,128)(2,1)S(1)}, u32[]{:S(2)}, u32[]{:S(2)}) collective-permute-start(bf16[4,128,256]{2,1,0:T(8,128)(2,1)S(1)} %dynamic-slice_bitcast_fusion.4), channel_id=1, source_target_pairs={{0,32},{32,0},{1,33},{33,1},{2,34},{34,2},{3,35},{35,3},{4,36},{36... | collective-permute-start | bytes 786440 | tf_op jit(solution)/shard_map/ppermute | solution.py:339
  139.2 9.8 %collective-permute-start.17 = (bf16[128,1024]{1,0:T(8,128)(2,1)}, bf16[128,1024]{1,0:T(8,128)(2,1)}, u32[]{:S(2)}, u32[]{:S(2)}) collective-permute-start(bf16[128,1024]{1,0:T(8,128)(2,1)} %get-tuple-element.40), channel_id=1, source_target_pairs={{0,64},{64,16},{16,80},{80,0},{1,65},{65,17},{17,81},{81,1},{2,66}... | collective-permute-start | bytes 786440 | tf_op jit(solution)/shard_map/ppermute | solution.py:347
  139.8 14.2 %collective-permute-start.18 = (bf16[128,1024]{1,0:T(8,128)(2,1)}, bf16[128,1024]{1,0:T(8,128)(2,1)}, u32[]{:S(2)}, u32[]{:S(2)}) collective-permute-start(bf16[128,1024]{1,0:T(8,128)(2,1)} %get-tuple-element.42), channel_id=1, source_target_pairs={{0,16},{64,80},{16,0},{80,64},{1,17},{65,81},{17,1},{81,65},{2,18}... | collective-permute-start | bytes 786440 | tf_op jit(solution)/shard_map/ppermute | solution.py:347
  141.6 13.0 %collective-permute-start.19 = (bf16[128,1024]{1,0:T(8,128)(2,1)}, bf16[128,1024]{1,0:T(8,128)(2,1)}, u32[]{:S(2)}, u32[]{:S(2)}) collective-permute-start(bf16[128,1024]{1,0:T(8,128)(2,1)} %get-tuple-element.41), channel_id=1, source_target_pairs={{0,80},{64,0},{16,64},{80,16},{1,81},{65,1},{17,65},{81,17},{2,82}... | collective-permute-start | bytes 786440 | tf_op jit(solution)/shard_map/ppermute | solution.py:347

commit v3 on v1

v3 whole, which is shorter than its diff:
```python
import jax
import jax.numpy as jnp
from jax import lax
from jax.experimental import pallas as pl
from jax.experimental.pallas import tpu as pltpu
from jax.sharding import Mesh, PartitionSpec as P

f32 = jnp.float32
bf16 = jnp.bfloat16
norm_eps = 1e-05
lanes = 128
NN = (((1,), (0,)), ((), ()))
NT = (((1,), (1,)), ((), ()))
TN = (((0,), (0,)), ((), ()))

whole = ("yl", "core", "yh", "x", "z")
rows_axes = ("yh", "x", "z")
group_axes = ("yl", "core", "yh")
vmem = 32 * 2**20


def dot1(a, b, dims):
    return lax.dot_general(a.astype(bf16), b.astype(bf16), dims, preferred_element_type=f32)


def halves(a):
    high = a.astype(bf16)
    return (high, (a - high.astype(f32)).astype(bf16))


def dot3(a, b, dims):
    a_high, a_low = a if isinstance(a, tuple) else halves(a)
    b_high, b_low = b if isinstance(b, tuple) else halves(b)
    dot = lambda left, right: lax.dot_general(left, right, dims, preferred_element_type=f32)
    (ca,), (cb,) = dims[0]
    both = dot(jnp.concatenate([a_high, a_low], axis=ca), jnp.concatenate([b_high, b_high], axis=cb))
    return both + dot(a_high, b_low)


def thirds(a):
    high = a.astype(bf16)
    rest = a - high.astype(f32)
    mid = rest.astype(bf16)
    return (high, mid, (rest - mid.astype(f32)).astype(bf16))


def dot_ones(pieces, ones, dims):
    first, *rest = [lax.dot_general(a, ones, dims, preferred_element_type=f32) for a in pieces]
    return first + sum(rest[1:], rest[0])


def spread_out(steps, cumul, expander):
    block = steps.shape[0]
    (s_high, s_low), (c_high, c_mid, c_low) = halves(steps), thirds(cumul)
    stacked = jnp.concatenate([s_high, s_low, c_high, c_mid, c_low], axis=0)
    wide = lax.dot_general(stacked, expander, NN, preferred_element_type=f32)
    at = lambda k: wide[k * block : (k + 1) * block]
    return at(0) + at(1), at(2) + (at(3) + at(4))


def iota(shape, axis):
    return lax.broadcasted_iota(jnp.int32, shape, axis)


def head_expander(inner, width, units):
    shape = (lanes, units * inner)
    start = iota(shape, 0) * width
    col = iota(shape, 1)
    return ((col >= start) & (col < start + width)).astype(f32).astype(bf16)


def packed(parts, heads):
    keep = iota(parts[0].shape, 1) < heads
    kept = [jnp.where(keep, a, 0.0) for a in parts]
    return sum(a if u == 0 else pltpu.roll(a, u * heads, 1) for u, a in enumerate(kept))


def unpacked(a, unit, heads):
    moved = a if unit == 0 else pltpu.roll(a, lanes - unit * heads, 1)
    return jnp.where(iota(a.shape, 1) < heads, moved, 0.0)


def beside(parts):
    return jnp.concatenate(list(parts), axis=1)


def lower_ones(block):
    shape = (block, block)
    return (iota(shape, 0) >= iota(shape, 1)).astype(f32).astype(bf16)


def ones_dot(ones, pieces):
    width = pieces[0].shape[1]
    wide = lax.dot_general(ones, jnp.concatenate(pieces, axis=1), NN, preferred_element_type=f32)
    parts = [wide[:, k * width : (k + 1) * width] for k in range(len(pieces))]
    return parts[0] + sum(parts[2:], parts[1])


def softplus(a):
    return jnp.maximum(a, 0.0) + jnp.log1p(jnp.exp(-jnp.abs(a)))


def pair_halves(a, block, width):
    left = iota(a.shape, 1) < width
    zero = jnp.zeros_like(a)
    return jnp.concatenate([jnp.where(left, a, zero), jnp.where(left, zero, a)], axis=0)


def forward_kernel(tok, weights, par, cot, xv_o, g_o, bc_o, low_o, y_o, st_o, stat_o, state, *, width, inner):
    _, seqs, block, _ = tok.shape
    units = [(j, s) for j in range(tok.shape[0]) for s in range(seqs)]
    count = len(units)
    heads = inner // width

    @pl.when(pl.program_id(0) == 0)
    def _():
        state[...] = jnp.zeros_like(state)

    proj = lax.dot_general(tok[...].reshape(count * block, -1), weights[...], NN, preferred_element_type=f32)
    cut = lambda u, first, size: proj[u * block : (u + 1) * block, first : first + size]
    part = lambda a, u: a[:, u * inner : (u + 1) * inner]
    expander = head_expander(inner, width, count)
    causal = iota((block, block), 0) >= iota((block, block), 1)
    skip, gain = beside([par[0:1, :]] * count), beside([par[1:2, :]] * count)
    bias, rate = par[2:3, :lanes], par[3:4, :lanes]

    raw = packed([cut(u, 2 * inner + 2 * lanes, lanes) for u in range(count)], heads) + bias
    steps = softplus(raw)
    cumul = ones_dot(lower_ones(block), thirds(-steps * rate))
    cumul_t = cumul.T
    low_o[0, 0], low_o[0, 1], low_o[0, 2] = raw, steps, cumul
    b_two, c_two = [], []
    for u, (j, s) in enumerate(units):
        b_in, c_out = cut(u, 2 * inner, lanes), cut(u, 2 * inner + lanes, lanes)
        bc_o[j, s] = beside([b_in, c_out])
        xv_o[j, s] = cut(u, 0, inner)
        g_o[j, s] = cut(u, inner, inner)
        b_two.append(halves(b_in))
        c_two.append(halves(c_out))
    scores = [dot3(c_two[u], b_two[u], NT) for u in range(count)]
    step_wide, cumul_wide = spread_out(steps, cumul, expander)
    last_wide = cumul_wide[block - 1 : block]
    xv = beside(cut(u, 0, inner) for u in range(count))
    gate = beside(cut(u, inner, inner) for u in range(count))
    values = xv * jax.nn.sigmoid(xv)
    scaled = values * step_wide
    tailed = scaled * jnp.exp(last_wide - cumul_wide)
    last_decay = jnp.exp(last_wide)
    updates = [dot3(b_two[u], part(tailed, u), TN) for u in range(count)]
    inners = []
    for u in range(count):
        for pair in range(heads // 2):
            both = []
            for h in (u * heads + 2 * pair, u * heads + 2 * pair + 1):
                gap = jnp.where(causal, cumul[:, h : h + 1] - cumul_t[h : h + 1, :], -1e30)
                both.append((scores[u] * jnp.exp(gap)).astype(bf16))
            first = u * inner + 2 * pair * width
            cols = scaled[:, first : first + 2 * width]
            inners.append(
                lax.dot_general(
                    beside(both), pair_halves(cols, block, width).astype(bf16), NN, preferred_element_type=f32
                )
            )
    carried = []
    for u, (j, s) in enumerate(units):
        old = state[s]
        st_o[j, s] = old
        carried.append(dot3(c_two[u], old, NN))
        state[s] = part(last_decay, u) * old + updates[u]
    y = jnp.exp(cumul_wide) * beside(carried) + beside(inners) + skip * values
    mixed = y * (gate * jax.nn.sigmoid(gate))
    weighted = beside(cot[j, s] for j, s in units).astype(f32) * gain * mixed
    squared = mixed * mixed
    row, col = iota((8, 2 * inner), 0), iota((8, 2 * inner), 1)
    chooser = ((row < 2) & ((col >= inner) == (row == 1))).astype(f32).astype(bf16)
    for u, (j, s) in enumerate(units):
        y_o[j, s] = part(y, u)
        high, low = halves(beside([part(squared, u), part(weighted, u)]))
        dot = lambda right: lax.dot_general(chooser, right, NT, preferred_element_type=f32)
        stat_o[0, :, u * block : (u + 1) * block] = dot(high) + dot(low)


def norm_kernel(y_i, g_i, cot, stat_0, stat_1, stat_2, stat_3, par, out_o, dy_o, dg_o, *, total):
    _, seqs, block, inner = y_i.shape
    gain = par[1:2, :]
    sums = (stat_0[0] + stat_1[0]) + (stat_2[0] + stat_3[0])
    scale_row = lax.rsqrt(sums[0:1] * (1.0 / total) + norm_eps)
    pull_row = scale_row * scale_row * scale_row * sums[1:2] * (1.0 / total)
    stacked = jnp.concatenate([scale_row, pull_row, jnp.zeros((6, scale_row.shape[1]), f32)], axis=0)
    row, col = iota((8, 2 * inner), 0), iota((8, 2 * inner), 1)
    chooser = ((row < 2) & ((col >= inner) == (row == 1))).astype(f32).astype(bf16)
    spread = dot_ones(halves(stacked), chooser, TN)
    for u in range(y_i.shape[0] * seqs):
        j, s = u // seqs, u % seqs
        span = slice(u * block, (u + 1) * block)
        scale, pull = spread[span, :inner], spread[span, inner:]
        gate, full = g_i[j, s], y_i[j, s]
        gate_sig = jax.nn.sigmoid(gate)
        gate_silu = gate * gate_sig
        mixed = full * gate_silu
        out_o[j, s] = (mixed * scale * gain).astype(bf16)
        d_mixed = cot[j, s].astype(f32) * gain * scale - mixed * pull
        dy_o[j, s] = d_mixed * gate_silu
        dg_o[j, s] = (d_mixed * full * (gate_sig * (1.0 + gate * (1.0 - gate_sig)))).astype(bf16)


def backward_kernel(
    core, xv_i, bc_i, low_i, y_i, st_i, dy_i, dg_i, tok, par, weights,
    near_o, far_o, term_o, give_o, grad_state, next_state, term, *, width, inner
):
    per_step, seqs, block, model = tok.shape
    units = [(j, s) for j in range(per_step) for s in range(seqs)]
    count = len(units)
    heads = inner // width
    step = pl.program_id(0)

    @pl.when(step == 0)
    def _():
        grad_state[...] = jnp.zeros_like(grad_state)
        next_state[...] = jnp.zeros_like(next_state)
        term[...] = jnp.zeros_like(term)

    part = lambda a, u: a[:, u * inner : (u + 1) * inner]
    expander = head_expander(inner, width, count)
    later = iota((block, block), 1) >= iota((block, block), 0)
    upper = (iota((block, block), 1) >= iota((block, block), 0)).astype(f32).astype(bf16)
    skip, rate = beside([par[0:1, :]] * count), par[3:4, :lanes]
    raw, steps, cumul = low_i[0, 0], low_i[0, 1], low_i[0, 2]
    cumul_t = cumul.T
    step_wide, cumul_wide = spread_out(steps, cumul, expander)
    last_wide = cumul_wide[block - 1 : block]
    tail, last_decay = jnp.exp(last_wide - cumul_wide), jnp.exp(last_wide)
    b_two = [halves(bc_i[j, s, :, :lanes]) for j, s in units]
    c_two = [halves(bc_i[j, s, :, lanes:]) for j, s in units]
    scores_t = [dot3(b_two[u], c_two[u], NT) for u in range(count)]
    xv = beside(xv_i[j, s] for j, s in units)
    d_y = beside(dy_i[j, s] for j, s in units)
    sig = jax.nn.sigmoid(xv)
    values = xv * sig
    y = beside(y_i[j, s] for j, s in units) - skip * values
    scaled = values * step_wide
    tailed = scaled * tail
    lifted = halves(d_y * jnp.exp(cumul_wide))
    lifted = [(part(lifted[0], u), part(lifted[1], u)) for u in range(count)]
    updates = [dot3(c_two[u], lifted[u], TN) for u in range(count)]

    back, through, from_state = [None] * count, [None] * count, [None] * count
    for u in reversed(range(count)):
        j, s = units[u]
        grad = grad_state[s]
        grad_two = halves(grad)
        back[u] = dot3(b_two[u], grad_two, NN)
        from_state[u] = dot3(part(tailed, u), grad_two, NT)
        through[u] = jnp.sum(next_state[s] * grad, axis=0, keepdims=True)
        grad_state[s] = part(last_decay, u) * grad + updates[u]
        next_state[s] = st_i[j, s]

    inners, d_scores = [], []
    for u in range(count):
        d_scores_t = jnp.zeros((block, block), f32)
        for pair in range(heads // 2):
            first = u * inner + 2 * pair * width
            cols = slice(first, first + 2 * width)
            products = lax.dot_general(
                pair_halves(scaled[:, cols], block, width).astype(bf16),
                d_y[:, cols].astype(bf16),
                NT,
                preferred_element_type=f32,
            )
            both = []
            for k in range(2):
                h = u * heads + 2 * pair + k
                gap = jnp.where(later, cumul_t[h : h + 1, :] - cumul[:, h : h + 1], -1e30)
                decay = jnp.exp(gap)
                both.append((scores_t[u] * decay).astype(bf16))
                d_scores_t += products[k * block : (k + 1) * block] * decay
            inners.append(
                lax.dot_general(
                    beside(both), pair_halves(d_y[:, cols], block, width).astype(bf16), NN, preferred_element_type=f32
                )
            )
        d_scores.append(halves(d_scores_t))
    d_c = [
        dot3(d_scores[u], b_two[u], TN) + dot3(lifted[u], st_i[j, s], NT) for u, (j, s) in enumerate(units)
    ]
    d_b = [dot3(d_scores[u], c_two[u], NN) + from_state[u] for u in range(count)]
    back = tail * beside(back) + beside(inners)
    last_row = iota((block, count * inner), 0) == block - 1
    products = jnp.concatenate([values * back, d_y * y + jnp.where(last_row, beside(through), 0.0)], axis=0)
    reduced = dot_ones(halves(products), expander, NT)
    d_steps = reduced[:block]
    d_log = ones_dot(upper, halves(reduced[block:] - steps * d_steps))
    d_raw = (d_steps - d_log * rate) * jax.nn.sigmoid(raw)
    d_values = back * step_wide + skip * d_y
    d_xv = (d_values * (sig * (1.0 + xv * (1.0 - sig)))).astype(bf16)
    here = jnp.concatenate(
        [
            beside([part(d_xv, u), dg_i[j, s], d_b[u].astype(bf16), d_c[u].astype(bf16)]
                   + [unpacked(d_raw, u, heads).astype(bf16)])
            for u, (j, s) in enumerate(units)
        ],
        axis=0,
    )
    term[...] += lax.dot_general(tok[...].reshape(count * block, model), here, TN, preferred_element_type=f32)
    partial = lax.dot_general(here, weights[...], NT, preferred_element_type=f32)
    partial = partial.reshape(per_step, seqs, block, model)
    first = core[0] == 0

    @pl.when(first)
    def _():
        near_o[0] = partial[0]
        far_o[0] = partial[1].astype(bf16)

    @pl.when(jnp.logical_not(first))
    def _():
        near_o[0] = partial[1]
        far_o[0] = partial[0].astype(bf16)

    @pl.when(step == pl.num_programs(0) - 1)
    def _():
        wide = 2 * inner
        term_o[:, :wide] = term[:, :wide].astype(bf16)
        term_o[:, wide + lanes :] = term[:, wide + 2 * lanes :].astype(bf16)
        b_part, c_part = term[:, wide : wide + lanes], term[:, wide + lanes : wide + 2 * lanes]
        term_o[:, wide : wide + lanes] = jnp.where(first, b_part, c_part).astype(bf16)
        give_o[...] = jnp.where(first, c_part, b_part).astype(bf16)


def join_kernel(_, near, far, term, got, out_0, out_1, out_2, out_3, term_o):
    step = pl.program_id(0)
    both = (near[0, 0] + far[0, 0].astype(f32)).astype(bf16)
    for k, out in enumerate((out_0, out_1, out_2, out_3)):

        @pl.when(step == k)
        def _(out=out):
            out[...] = both

    @pl.when(step == 0)
    def _():
        term_o[...] = (term[...].astype(f32) + got[...].astype(f32)).astype(bf16)


def total_kernel(shares, xz_o, bcdt_o, *, inner, heads, group):
    step = pl.program_id(0)
    half = group * inner

    @pl.when(step == 0)
    def _():
        bcdt_o[...] = jnp.zeros_like(bcdt_o)

    summed = jnp.sum(shares[0].astype(f32), axis=0)
    at = pl.multiple_of(step * inner, inner)
    xz_o[:, pl.ds(at, inner)] = summed[:, :inner]
    xz_o[:, pl.ds(pl.multiple_of(half + at, inner), inner)] = summed[:, inner : 2 * inner]
    core = lax.rem(lax.div(step, 2), 2)
    bc = summed[:, 2 * inner : 2 * inner + lanes]
    bcdt_o[:, :lanes] += jnp.where(core == 0, bc, 0.0)
    bcdt_o[:, lanes : 2 * lanes] += jnp.where(core == 0, 0.0, bc)
    steps = summed[:, 2 * inner + lanes :]
    lane = iota(steps.shape, 1)
    moved = pltpu.roll(jnp.where(lane < heads, steps, 0.0), step * heads, 1)
    bcdt_o[:, 2 * lanes :] += moved[:, : group * heads]


def cost(micros):
    return pl.CostEstimate(flops=int(micros * 1.1e9), bytes_accessed=int(micros * 3.5e6), transcendentals=0)


def chunk_spec(shape, count=None, per_step=1):
    blank = (0,) * (len(shape) - 1)
    if count is None:
        return pl.BlockSpec((per_step,) + shape[1:], lambda i: (i,) + blank)
    return pl.BlockSpec((per_step,) + shape[1:], lambda i: (count - 1 - i,) + blank)


def fixed_spec(shape):
    return pl.BlockSpec(shape, lambda i: (0,) * len(shape))


chunks_per_step = 2


def forward_call(tok, weights, par, cot, width):
    chunks, seqs, block, model = tok.shape
    inner = cot.shape[3]
    steps = chunks // chunks_per_step
    wide = (chunks, seqs, block, inner)
    by_chunk = lambda a: chunk_spec(a, per_step=chunks_per_step)
    outs = [
        (wide, by_chunk),
        (wide, by_chunk),
        ((chunks, seqs, block, 2 * lanes), by_chunk),
        ((steps, 3, block, lanes), chunk_spec),
        (wide, by_chunk),
        ((chunks, seqs, lanes, inner), by_chunk),
        ((steps, 8, chunks_per_step * seqs * block), chunk_spec),
    ]

    def kernel(*refs):
        forward_kernel(*refs, width=width, inner=inner)

    return pl.pallas_call(
        kernel,
        grid=(steps,),
        in_specs=[by_chunk(tok.shape), fixed_spec(weights.shape), fixed_spec(par.shape), by_chunk(cot.shape)],
        out_specs=[spec(a) for a, spec in outs],
        out_shape=[jax.ShapeDtypeStruct(a, f32) for a, _ in outs],
        scratch_shapes=[pltpu.VMEM((seqs, lanes, inner), f32)],
        compiler_params=pltpu.CompilerParams(vmem_limit_bytes=vmem),
        cost_estimate=cost(12),
        name="forward_scan",
    )(tok, weights, par, cot)


def norm_call(y, gate, cot, stats, par, total):
    chunks = y.shape[0]
    by_chunk = lambda a: chunk_spec(a.shape, per_step=chunks_per_step)

    def kernel(*refs):
        norm_kernel(*refs, total=total)

    return pl.pallas_call(
        kernel,
        grid=(chunks // chunks_per_step,),
        in_specs=[by_chunk(a) for a in (y, gate, cot)] + [chunk_spec(a.shape) for a in stats] + [fixed_spec(par.shape)],
        out_specs=[by_chunk(y)] * 3,
        out_shape=[jax.ShapeDtypeStruct(y.shape, kind) for kind in (bf16, f32, bf16)],
        compiler_params=pltpu.CompilerParams(vmem_limit_bytes=vmem),
        cost_estimate=cost(5),
        name="gated_norm",
    )(y, gate, cot, *stats, par)


def backward_call(core, xv, bc, low, y, states, d_y, d_gate, tok, par, weights, width):
    chunks, seqs, block, inner = xv.shape
    model, columns = weights.shape
    steps = chunks // chunks_per_step
    half = (steps, seqs, block, model)
    half_spec = chunk_spec(half, steps)
    by_chunk = lambda a: chunk_spec(a.shape, steps, chunks_per_step)

    def kernel(*refs):
        backward_kernel(*refs, width=width, inner=inner)

    return pl.pallas_call(
        kernel,
        grid=(steps,),
        in_specs=[pl.BlockSpec(memory_space=pltpu.SMEM), by_chunk(xv), by_chunk(bc), chunk_spec(low.shape, steps)]
        + [by_chunk(a) for a in (y, states, d_y, d_gate, tok)]
        + [fixed_spec(par.shape), fixed_spec(weights.shape)],
        out_specs=[half_spec, half_spec, fixed_spec((model, columns - lanes)), fixed_spec((model, lanes))],
        out_shape=[
            jax.ShapeDtypeStruct(half, f32),
            jax.ShapeDtypeStruct(half, bf16),
            jax.ShapeDtypeStruct((model, columns - lanes), bf16),
            jax.ShapeDtypeStruct((model, lanes), bf16),
        ],
        scratch_shapes=[
            pltpu.VMEM((seqs, lanes, inner), f32),
            pltpu.VMEM((seqs, lanes, inner), f32),
            pltpu.VMEM((model, columns), f32),
        ],
        compiler_params=pltpu.CompilerParams(vmem_limit_bytes=vmem),
        cost_estimate=cost(20),
        name="backward_scan",
    )(core, xv, bc, low, y, states, d_y, d_gate, tok, par, weights)


def join_call(here, near, far, term, got, inner):
    halves_of, seqs, block, model = near.shape
    count = halves_of * seqs
    bc_spec = pl.BlockSpec((term.shape[0], lanes), lambda k, here: (0, 2 * inner // lanes))

    def place(k, here):
        y = lax.rem(here[0] + k, count)
        return (lax.rem(y, 2), lax.div(y, 2), 0, 0)

    spec = pl.BlockSpec((1, 1, block, model), place)
    return pl.pallas_call(
        join_kernel,
        grid_spec=pltpu.PrefetchScalarGridSpec(
            num_scalar_prefetch=1,
            grid=(count,),
            in_specs=[spec, spec, bc_spec, pl.BlockSpec(got.shape, lambda k, here: (0, 0))],
            out_specs=[pl.BlockSpec((block, model), lambda k, here: (0, 0))] * count + [bc_spec],
        ),
        out_shape=[jax.ShapeDtypeStruct((block, model), bf16)] * count + [jax.ShapeDtypeStruct(term.shape, bf16)],
        input_output_aliases={3: count},
        compiler_params=pltpu.CompilerParams(vmem_limit_bytes=vmem),
        cost_estimate=cost(3),
        name="join_halves",
    )(here, near, far, term, got)


def total_call(shares, inner, heads):
    group, _, rows, columns = shares.shape
    shapes = [(rows, 2 * group * inner), (rows, 2 * lanes + group * heads)]

    def kernel(*refs):
        total_kernel(*refs, inner=inner, heads=heads, group=group)

    return pl.pallas_call(
        kernel,
        grid=(group,),
        in_specs=[chunk_spec(shares.shape)],
        out_specs=[fixed_spec(a) for a in shapes],
        out_shape=[jax.ShapeDtypeStruct(a, f32) for a in shapes],
        compiler_params=pltpu.CompilerParams(vmem_limit_bytes=vmem),
        cost_estimate=cost(2),
        name="total_shares",
    )(shares)


def partner(a):
    return lax.ppermute(a, "core", [(0, 1), (1, 0)])


def around(give, mine):
    came = [give(0 if mine is None else mine)]
    spot = lambda y: (y % 2) * 2 + y // 2
    for shift in (1, 3, 2):
        pairs = [(spot(y), spot((y + shift) % 4)) for y in range(4)]
        came.append(lax.ppermute(give(shift if mine is None else (mine + shift) % 4), ("yl", "yh"), pairs))
    return [came[0], came[1], came[3], came[2]]


def in_order(came, mine):
    turned = [came[0], came[3], came[2], came[1]]
    return lax.dynamic_slice_in_dim(jnp.stack(turned + turned), 4 - mine, 4, 0)


def by_core(own, other, core):
    first = core == 0
    return jnp.stack([jnp.where(first, own, other), jnp.where(first, other, own)])


def body(tokens, cotangent, w_xz, w_bcdt, rate, dt_bias, skip, gain):
    group = lax.axis_size(group_axes)
    devices = lax.axis_size(whole)
    mine = lax.axis_index(group_axes)
    chunks = lax.axis_size("yl") * lax.axis_size("core")
    seqs = group // chunks
    owners = lax.axis_size(rows_axes)
    block, model = tokens.shape[1:]
    total = cotangent.shape[2]
    inner = total // group
    heads = rate.shape[0] // group
    width = inner // heads
    states = (w_bcdt.shape[1] - rate.shape[0]) // 2

    def picked(target):
        w_dt = lax.dynamic_slice_in_dim(w_bcdt[:, 2 * states :], target * heads, heads, 1)
        return jnp.concatenate(
            [
                lax.dynamic_slice_in_dim(w_xz, target * inner, inner, 1),
                lax.dynamic_slice_in_dim(w_xz, total + target * inner, inner, 1),
                w_bcdt[:, : 2 * states],
                jnp.pad(w_dt, ((0, 0), (0, lanes - heads))),
            ],
            axis=1,
        )

    yl, yh, core = lax.axis_index("yl"), lax.axis_index("yh"), lax.axis_index("core")
    w_picked = jnp.stack([picked((((yl + yh + k) % 2) * 2 + core) * seqs + k) for k in range(seqs)])
    copies = jnp.broadcast_to(w_picked[:, None], (seqs, owners // seqs) + w_picked.shape[1:])
    copies = copies.reshape((owners,) + w_picked.shape[1:])
    rest = owners // seqs
    traders = [
        [(((start + k) % 2) * seqs + k) * rest + i for k in range(seqs) for i in range(rest)] for start in range(2)
    ]
    weights = lax.all_to_all(copies, ("yl",) + rows_axes, 0, 0, axis_index_groups=traders, tiled=True)
    weights = weights.reshape(model, -1)

    here = lax.axis_index(("yh", "yl"))
    at = lambda a, index: lax.dynamic_index_in_dim(a, index, 0, keepdims=False)

    tok = in_order(around(lambda y: tokens[0], here), here)
    tok = by_core(tok, partner(tok), core)
    tok = tok.reshape(2, 2, 2, block, model).transpose(2, 0, 1, 3, 4).reshape(chunks, seqs, block, model)

    cut = cotangent[0].reshape(block, 2, 2, 2, inner).transpose(2, 3, 1, 0, 4)
    cut = cut.reshape(2, 4, block, inner)
    cut = by_core(at(cut, core), partner(at(cut, 1 - core)), core)
    cot = in_order(around(lambda y: lax.dynamic_index_in_dim(cut, y, 1, keepdims=False), here), here)
    cot = cot.reshape(2, 2, 2, block, inner).transpose(1, 2, 0, 3, 4).reshape(chunks, seqs, block, inner)

    own = lambda a: lax.dynamic_slice_in_dim(a, mine * heads, heads, 0)
    padded = lambda a: jnp.pad(jnp.tile(own(a), lanes // heads), (0, inner - lanes))
    par = jnp.stack(
        [jnp.repeat(own(skip), width), lax.dynamic_slice_in_dim(gain, mine * inner, inner, 0)]
        + [padded(dt_bias), padded(rate)]
        + [jnp.zeros((inner,), f32)] * 4
    )
    xv, gate, bc, low, y, chunk_states, stats = forward_call(tok, weights, par, cot, width)
    stats = stats + partner(stats)
    stats = around(lambda y: stats, here)
    out, d_y, d_gate = norm_call(y, gate, cot, stats, par, float(total))
    layer_out = lax.all_to_all(out.reshape(group, block, inner), group_axes, 0, 0, tiled=True)
    layer_out = layer_out.transpose(1, 0, 2).reshape(1, block, total)
    scalar = lambda a: jnp.full((1,), a, jnp.int32)
    near, far, term, give = backward_call(
        scalar(core), xv, bc, low, y, chunk_states, d_y, d_gate, tok, par, weights, width
    )
    *sums, term = join_call(scalar(here), near, partner(far), term, partner(give), inner)
    shares = lax.all_to_all(term.reshape(devices, model // devices, -1), whole, 0, 0, tiled=True)
    came = around(lambda shift: sums[shift], None)
    grad_input = sum(a.astype(f32) for a in came).astype(bf16)[None]
    grad_xz, grad_bcdt = total_call(
        shares.reshape(group, devices // group, model // devices, -1), inner, heads
    )
    return (layer_out, grad_input, grad_xz, grad_bcdt)


def solution(mesh):
    split = Mesh(mesh.devices.reshape(2, 2, 2, 4, 4), whole)
    ctx, fsdp = ("yl", "core"), rows_axes
    placed = (P(fsdp, ctx, None), P(fsdp, ctx, None), P(fsdp, None), P(fsdp, None), P(), P(), P(), P())
    return jax.shard_map(
        body,
        mesh=split,
        in_specs=placed,
        out_specs=(P(fsdp, ctx, None), P(fsdp, ctx, None), P(ctx + fsdp, None), P(ctx + fsdp, None)),
        check_vma=False,
    )
```

time: 241 us -> 139 us (0.58)
  waiting for transfers between devices: 105 us -> 48.9 us
  blocking collectives: 29.6 us -> 0 us
  between operations: 14.2 us -> 1.07 us
  matrix products: 10.1 us -> 0 us
  local copies, waits for them, and re-layouts: 12.8 us -> 18.6 us
  starting transfers between devices: 37.8 us -> 40.9 us
    all_to_all x3 -> x1, waiting for transfers between devices: 63.1 us -> 0.01 us  [body(): lax.all_to_all(copies, ('yl',) + rows_axes, 0, 0, axis_index_groups=trade...]
    ppermute x0 -> x17, waiting for transfers between devices: none -> 44.4 us  [the longest x12 43.5 us: around(): lax.ppermute(give(shift if mine is None else (mine + shift) % 4), ('yl',...]
    all_gather x1 -> x0, blocking collectives: 29.6 us -> none  [body(): stats = lax.all_gather(stats[:, :2], group_axes, axis=0).sum(axis=0)]
    all_to_all x1, waiting for transfers between devices: 20.7 us -> 0.01 us  [body(): lax.all_to_all(term.reshape(devices, model // devices, -1), whole, 0, 0,...]
    all_gather x1 -> x0, waiting for transfers between devices: 19.6 us -> none  [body(): lax.all_gather(tokens[0], group_axes, axis=0)]
    ppermute x0 -> x17, starting transfers between devices: none -> 19 us  [the longest x12 14.3 us: around(): lax.ppermute(give(shift if mine is None else (mine + shift) % 4), ('yl',...]
    dot_general x2 -> x0, matrix products: 10.1 us -> none  [the longest x1 5.2 us: body(): lax.dot_general(flat_d, weights, NT, preferred_element_type=f32)]
    all_to_all x3 -> x1, starting transfers between devices: 19.6 us -> 9.83 us  [body(): lax.all_to_all(copies, ('yl',) + rows_axes, 0, 0, axis_index_groups=trade...]
  transfers between devices with their start and end apart: 6 -> 20, of which waited for: 6 -> 10; matrix products, arithmetic and copies ran while one was open for 10% -> 11% of each run, Pallas kernels for 0% -> 0%
where the time goes in v3:
time: 139 us; the launch traced here: 138 us
  waiting for transfers between devices  48.9 us (35%)
  starting transfers between devices  40.9 us (29%)
  Pallas kernels  25.2 us (18%)
  local copies, waits for them, and re-layouts  18.6 us (13%)
  other arithmetic  3.34 us (2%)
    ppermute x12, waiting for transfers between devices, around(): lax.ppermute(give(shift if mine is None else (mine + shift) % 4), ('yl',...  43.5 us
    ppermute x12, starting transfers between devices, around(): lax.ppermute(give(shift if mine is None else (mine + shift) % 4), ('yl',...  14.3 us
    pallas_call x1, Pallas kernels, backward_call(): pl.pallas_call(kernel, grid=(steps,), in_specs=[pl.BlockSpec(memory_space...  13.6 us
    all_to_all x1, starting transfers between devices, body(): lax.all_to_all(copies, ('yl',) + rows_axes, 0, 0, axis_index_groups=trade...  9.83 us
    unnamed x33, local copies, waits for them, and re-layouts  8.11 us
    all_to_all x1, starting transfers between devices, body(): lax.all_to_all(term.reshape(devices, model // devices, -1), whole, 0, 0,...  7.83 us
    pallas_call x1, Pallas kernels, forward_call(): pl.pallas_call(kernel, grid=(steps,), in_specs=[by_chunk(tok.shape), fixe...  7.66 us
    ppermute x5, starting transfers between devices, partner(): return lax.ppermute(a, 'core', [(0, 1), (1, 0)])  4.73 us
  transfers between devices with their start and end apart: 20, of which 10 were waited for; matrix products, arithmetic and copies ran while one was open for 11% of the time, Pallas kernels for 0%

profile of v3, /device:TPU:1, one launch (start us, length us, event | category | flops | bytes accessed | tf_op | source)
XLA Modules:
  0.0 138.0 jit_solution(1446483392424178048)
XLA Ops:
  0.6 3.6 %collective-permute-start = (bf16[128,1024]{1,0:T(8,128)(2,1)}, bf16[128,1024]{1,0:T(8,128)(2,1)S(1)}, u32[]{:S(2)}, u32[]{:S(2)}) collective-permute-start(bf16[128,1024]{1,0:T(8,128)(2,1)} %bitcast.87), channel_id=1, source_target_pairs={{0,80},{64,0},{16,64},{80,16},{1,81},{65,1},{17,65},{81,17},{2,82}... | collective-permute-start | bytes 786440 | tf_op jit(solution)/shard_map/ppermute | solution.py:523
  4.3 0.3 collective-permute-start.1
  4.6 0.7 collective-permute-start.2
  5.3 0.7 slice.8
  6.0 0.7 slice.9
  6.7 0.1 constant_dynamic-slice_fusion.4
  6.8 0.8 constant_dynamic-slice_fusion.6
  7.6 1.4 broadcast_in_dim.18
  9.0 9.8 %all-to-all-start = ((bf16[32,32,896]{2,1,0:T(8,128)(2,1)}), bf16[32,32,896]{2,1,0:T(8,128)(2,1)}, u32[]{:S(2)}, u32[]{:S(2)}) async-start(bf16[32,32,896]{2,1,0:T(8,128)(2,1)} %bitcast.10), calls=%async_computation | async-start | bytes 3670016 | tf_op jit(solution)/shard_map/all_to_all | solution.py:571
  18.8 0.0 copy-start.5
  18.9 0.3 copy.22
  19.2 0.2 copy.23
  19.4 0.7 dynamic-slice_bitcast_fusion
  20.1 1.8 %collective-permute-start.4 = (bf16[4,128,256]{2,1,0:T(8,128)(2,1)}, bf16[4,128,256]{2,1,0:T(8,128)(2,1)}, u32[]{:S(2)}, u32[]{:S(2)}) collective-permute-start(bf16[4,128,256]{2,1,0:T(8,128)(2,1)} %dynamic-slice_bitcast_fusion), channel_id=1, source_target_pairs={{0,32},{32,0},{1,33},{33,1},{2,34},{34,2},{3,35},{35,3},{4,36},{36... | collective-permute-start | bytes 786440 | tf_op jit(solution)/shard_map/ppermute | solution.py:515
  22.0 0.1 dynamic_slice.63
  22.1 0.1 broadcast_in_dim.19
  22.2 0.1 stack_reshape.3
  22.2 0.1 dynamic_slice.65
  22.3 0.1 tile.9
  22.4 0.1 dynamic_slice.66
  22.5 0.1 tile.21
  22.7 0.8 dynamic_slice.64
  23.5 1.0 bitcast_dynamic-update-slice_fusion
  24.5 1.0 fusion.1
  25.6 2.7 %collective-permute-start.5 = (bf16[2,128,256]{2,1,0:T(8,128)(2,1)S(1)}, bf16[2,128,256]{2,1,0:T(8,128)(2,1)S(1)}, u32[]{:S(2)}, u32[]{:S(2)}) collective-permute-start(bf16[2,128,256]{2,1,0:T(8,128)(2,1)S(1)} %get-tuple-element.51), channel_id=1, source_target_pairs={{0,80},{64,0},{16,64},{80,16},{1,81},{65,1},{17,65},{81,17},{2,82}... | collective-permute-start | bytes 393224 | tf_op jit(solution)/shard_map/ppermute | solution.py:523
  28.4 1.0 bitcast_dynamic-update-slice_fusion.1
  29.4 0.1 constant_dynamic-slice_fusion.7
  29.4 0.4 collective-permute-start.3
  29.8 0.4 collective-permute-start.7
  30.2 13.3 %collective-permute-done.5 = bf16[2,128,256]{2,1,0:T(8,128)(2,1)S(1)} collective-permute-done((bf16[2,128,256]{2,1,0:T(8,128)(2,1)S(1)}, bf16[2,128,256]{2,1,0:T(8,128)(2,1)S(1)}, u32[]{:S(2)}, u32[]{:S(2)}) %collective-permute-start.5) | collective-permute-done | bytes 131104 | tf_op jit(solution)/shard_map/ppermute | solution.py:523
  43.5 3.6 %collective-permute-done.7 = bf16[2,128,256]{2,1,0:T(8,128)(2,1)S(1)} collective-permute-done((bf16[2,128,256]{2,1,0:T(8,128)(2,1)S(1)}, bf16[2,128,256]{2,1,0:T(8,128)(2,1)S(1)}, u32[]{:S(2)}, u32[]{:S(2)}) %collective-permute-start.7) | collective-permute-done | bytes 131104 | tf_op jit(solution)/shard_map/ppermute | solution.py:523
  47.3 0.1 broadcast_select_fusion.1
  47.5 0.2 pad_maximum_fusion
  47.7 0.2 copy.26
  47.8 7.7 %forward_scan.1 = (f32[4,2,128,256]{3,2,1,0:T(8,128)S(1)}, f32[4,2,128,256]{3,2,1,0:T(8,128)S(1)}, f32[4,2,128,256]{3,2,1,0:T(8,128)S(1)}, f32[2,3,128,128]{3,2,...) custom-call(bf16[4,2,128,1024]{3,2,1,0:T(8,128)(2,1)S(1)} %bitcast.74, ...), custom_call_target="tpu_custom_call" | custom-call | flops 13200000000 | bytes 42000000 | tf_op jit(solution)/shard_map/forward_scan/pallas_call | solution.py:402
  55.5 1.1 collective-permute-start.8
  56.6 0.9 collective-permute-done.8
  57.5 1.4 %collective-permute-start.10 = (f32[2,8,512]{2,1,0:T(8,128)S(1)}, f32[2,8,512]{2,1,0:T(8,128)S(1)}, u32[]{:S(2)}, u32[]{:S(2)}) collective-permute-start(f32[2,8,512]{2,1,0:T(8,128)S(1)} %add.165.refs_3_), channel_id=1, source_target_pairs={{0,16},{64,80},{16,0},{80,64},{1,17},{65,81},{17,1},{81,65},{2,18}... | collective-permute-start | bytes 98312 | tf_op jit(solution)/shard_map/ppermute | solution.py:523
  58.9 1.3 collective-permute-start.11
  60.2 1.3 collective-permute-done.9.refs_4_
  61.5 0.4 collective-permute-done.10.refs_5_
  61.8 0.8 collective-permute-done.11.refs_6_
  62.7 2.0 %gated_norm.1 = (bf16[4,2,128,256]{3,2,1,0:T(8,128)(2,1)}, f32[4,2,128,256]{3,2,1,0:T(8,128)S(1)}, bf16[4,2,128,256]{3,2,1,0:T(8,128)(2,1)S(1)}) custom-call(f32[4,2,128,256]{3,2,1,0:T(8,128)S(1)} %get-tuple-element.25.refs_0_.refs_4_, f32[4,2,128,256]{3,2,1,0:T(8,128)S(1)} %get-tuple-element.26.refs_1_, bf16[4,2,128,256]{3,2,1,0:T(8,128)(2,1)S(1)} %bitcast.79, ...), custom_call_target="tpu_custom_call" | custom-call | flops 5500000256 | bytes 17500000 | tf_op jit(solution)/shard_map/gated_norm/pallas_call | solution.py:422
  64.6 13.6 %backward_scan.1 = (f32[2,2,128,1024]{3,2,1,0:T(8,128)S(1)}, bf16[2,2,128,1024]{3,2,1,0:T(8,128)(2,1)}, bf16[1024,768]{1,0:T(8,128)(2,1)S(1)}, bf16[1024,128]{1,0:T(8,128)(2,1)S(1)}) custom-call(s32[1]{0:T(128)} %bitcast.35.refs_0_, f32[4,2,128,256]{3,2,1,0:T(8,128)S(1)} %get-tuple-element.29.refs_1_, f32[4,2,128,256]{3,2,1,0:T(8,128)S(1)} %get-tuple-element.30.refs_2_, ...), custom_call_target="tpu_custom_call" | custom-call | flops 22000001024 | bytes 70000000 | tf_op jit(solution)/shard_map/backward_scan/pallas_call | solution.py:445
  78.3 1.2 copy-done
  79.4 1.4 copy-done.3
  80.8 1.4 %collective-permute-start.12 = (bf16[2,2,128,1024]{3,2,1,0:T(8,128)(2,1)}, bf16[2,2,128,1024]{3,2,1,0:T(8,128)(2,1)S(1)}, u32[]{:S(2)}, u32[]{:S(2)}) collective-permute-start(bf16[2,2,128,1024]{3,2,1,0:T(8,128)(2,1)} %get-tuple-element.36), channel_id=1, source_target_pairs={{0,32},{32,0},{1,33},{33,1},{2,34},{34,2},{3,35},{35,3},{4,36},{36... | collective-permute-start | bytes 3145736 | tf_op jit(solution)/shard_map/ppermute | solution.py:515
  82.2 4.2 %all-to-all-start.1 = ((bf16[8,128,256]{2,1,0:T(8,128)(2,1)}), bf16[8,128,256]{2,1,0:T(8,128)(2,1)S(1)}, u32[]{:S(2)}, u32[]{:S(2)}) async-start(bf16[8,128,256]{2,1,0:T(8,128)(2,1)} %bitcast.32), calls=%async_computation.1 | async-start | bytes 1048576 | tf_op jit(solution)/shard_map/all_to_all | solution.py:598
  86.4 1.4 %copy-done.1 = bf16[1024,768]{1,0:T(8,128)(2,1)S(1)} copy-done((bf16[1024,768]{1,0:T(8,128)(2,1)S(1)}, bf16[1024,768]{1,0:T(8,128)(2,1)}, u32[]{:S(2)}) %copy-start.1) | copy-done | bytes 1572888
  87.8 1.6 %copy-done.4 = f32[2,2,128,1024]{3,2,1,0:T(8,128)S(1)} copy-done((f32[2,2,128,1024]{3,2,1,0:T(8,128)S(1)}, f32[2,2,128,1024]{3,2,1,0:T(8,128)}, u32[]{:S(2)}) %copy-start.4) | copy-done | bytes 2097176
  89.4 0.6 join_halves.1
  90.1 1.2 copy-done.2
  91.2 4.5 %all-to-all-done.1 = bf16[8,128,256]{2,1,0:T(8,128)(2,1)S(1)} async-done(((bf16[8,128,256]{2,1,0:T(8,128)(2,1)}), bf16[8,128,256]{2,1,0:T(8,128)(2,1)S(1)}, u32[]{:S(2)}, u32[]{:S(2)}) %all-to-all-start.1) | async-done | bytes 524320 | tf_op jit(solution)/shard_map/all_to_all | solution.py:598
  95.8 7.8 %all-to-all-start.2 = ((bf16[128,8,768]{2,1,0:T(8,128)(2,1)}), bf16[128,8,768]{2,1,0:T(8,128)(2,1)S(1)}, u32[]{:S(2)}, u32[]{:S(2)}) async-start(bf16[128,8,768]{2,1,0:T(8,128)(2,1)} %bitcast.77), calls=%async_computation.2 | async-start | bytes 3145728 | tf_op jit(solution)/shard_map/all_to_all | solution.py:605
  103.6 2.7 %collective-permute-start.16 = (bf16[128,1024]{1,0:T(8,128)(2,1)S(1)}, bf16[128,1024]{1,0:T(8,128)(2,1)S(1)}, u32[]{:S(2)}, u32[]{:S(2)}) collective-permute-start(bf16[128,1024]{1,0:T(8,128)(2,1)S(1)} %get-tuple-element.42), channel_id=1, source_target_pairs={{0,80},{64,0},{16,64},{80,16},{1,81},{65,1},{17,65},{81,17},{2,82}... | collective-permute-start | bytes 786440 | tf_op jit(solution)/shard_map/ppermute | solution.py:523
  106.3 0.5 collective-permute-start.15
  106.8 0.6 collective-permute-start.14
  107.4 1.1 copy.25
  108.5 2.1 %reshape.54 = bf16[1,128,2048]{2,1,0:T(8,128)(2,1)} reshape(bf16[128,8,256]{2,1,0:T(8,128)(2,1)} %copy.25) | data formatting | bytes 1048576 | tf_op jit(solution)/shard_map/reshape | solution.py:599
  110.6 17.1 %collective-permute-done.16 = bf16[128,1024]{1,0:T(8,128)(2,1)S(1)} collective-permute-done((bf16[128,1024]{1,0:T(8,128)(2,1)S(1)}, bf16[128,1024]{1,0:T(8,128)(2,1)S(1)}, u32[]{:S(2)}, u32[]{:S(2)}) %collective-permute-start.16) | collective-permute-done | bytes 262176 | tf_op jit(solution)/shard_map/ppermute | solution.py:523
  127.7 1.9 %collective-permute-done.15 = bf16[128,1024]{1,0:T(8,128)(2,1)} collective-permute-done((bf16[128,1024]{1,0:T(8,128)(2,1)S(1)}, bf16[128,1024]{1,0:T(8,128)(2,1)}, u32[]{:S(2)}, u32[]{:S(2)}) %collective-permute-start.15) | collective-permute-done | bytes 262176 | tf_op jit(solution)/shard_map/ppermute | solution.py:523
  129.5 5.2 %collective-permute-done.14 = bf16[128,1024]{1,0:T(8,128)(2,1)} collective-permute-done((bf16[128,1024]{1,0:T(8,128)(2,1)S(1)}, bf16[128,1024]{1,0:T(8,128)(2,1)}, u32[]{:S(2)}, u32[]{:S(2)}) %collective-permute-start.14) | collective-permute-done | bytes 262176 | tf_op jit(solution)/shard_map/ppermute | solution.py:523
  134.7 1.9 %fusion = bf16[1,128,1024]{2,1,0:T(8,128)(2,1)} fusion(bf16[128,1024]{1,0:T(8,128)(2,1)S(1)} %collective-permute-done.16, bf16[128,1024]{1,0:T(8,128)(2,1)} %collective-permute-done.15, bf16[128,1024]{1,0:T(8,128)(2,1)} %collective-permute-done.14, bf16[128,1024]{1,0:T(8,128)(2,1)S(1)} %get-tuple-element.39), kind=kLoop, calls=%fused_computation.12 | loop fusion | flops 1048576 | bytes 1310720 | tf_op jit(solution)/shard_map/broadcast_in_dim | solution.py:607
  136.6 1.4 total_shares.1
  (53 shorter events, 0.5 us)
Async XLA Ops:
  0.6 22.8 %collective-permute-start = (bf16[128,1024]{1,0:T(8,128)(2,1)}, bf16[128,1024]{1,0:T(8,128)(2,1)S(1)}, u32[]{:S(2)}, u32[]{:S(2)}) collective-permute-start(bf16[128,1024]{1,0:T(8,128)(2,1)} %bitcast.87), channel_id=1, source_target_pairs={{0,80},{64,0},{16,64},{80,16},{1,81},{65,1},{17,65},{81,17},{2,82}... | collective-permute-start | bytes 786440 | tf_op jit(solution)/shard_map/ppermute | solution.py:523
  4.3 19.2 %collective-permute-start.1 = (bf16[128,1024]{1,0:T(8,128)(2,1)}, bf16[128,1024]{1,0:T(8,128)(2,1)S(1)}, u32[]{:S(2)}, u32[]{:S(2)}) collective-permute-start(bf16[128,1024]{1,0:T(8,128)(2,1)} %bitcast.88), channel_id=1, source_target_pairs={{0,16},{64,80},{16,0},{80,64},{1,17},{65,81},{17,1},{81,65},{2,18}... | collective-permute-start | bytes 786440 | tf_op jit(solution)/shard_map/ppermute | solution.py:523
  4.6 18.9 %collective-permute-start.2 = (bf16[128,1024]{1,0:T(8,128)(2,1)}, bf16[128,1024]{1,0:T(8,128)(2,1)}, u32[]{:S(2)}, u32[]{:S(2)}) collective-permute-start(bf16[128,1024]{1,0:T(8,128)(2,1)} %bitcast.89), channel_id=1, source_target_pairs={{0,64},{64,16},{16,80},{80,0},{1,65},{65,17},{17,81},{81,1},{2,66}... | collective-permute-start | bytes 786440 | tf_op jit(solution)/shard_map/ppermute | solution.py:523
  9.0 9.9 %copy-start.6 = (bf16[1,128,2048]{2,1,0:T(8,128)(2,1)S(1)}, bf16[1,128,2048]{2,1,0:T(8,128)(2,1)}, u32[]{:S(2)}) copy-start(bf16[1,128,2048]{2,1,0:T(8,128)(2,1)} %param.9) | copy-start | bytes 1572868
  9.0 38.8 %all-to-all-start = ((bf16[32,32,896]{2,1,0:T(8,128)(2,1)}), bf16[32,32,896]{2,1,0:T(8,128)(2,1)}, u32[]{:S(2)}, u32[]{:S(2)}) async-start(bf16[32,32,896]{2,1,0:T(8,128)(2,1)} %bitcast.10), calls=%async_computation | async-start | bytes 3670016 | tf_op jit(solution)/shard_map/all_to_all | solution.py:571
  18.8 3.1 %copy-start.5 = (bf16[1,128,1024]{2,1,0:T(8,128)(2,1)S(1)}, bf16[1,128,1024]{2,1,0:T(8,128)(2,1)}, u32[]{:S(2)}) copy-start(bf16[1,128,1024]{2,1,0:T(8,128)(2,1)} %param.8) | copy-start | bytes 786436
  18.8 3.2 %copy-start.7 = (f32[32]{0:T(128)S(1)}, f32[32]{0:T(128)}, u32[]{:S(2)}) copy-start(f32[32]{0:T(128)} %param.14) | copy-start | bytes 388
  18.9 3.4 %copy-start.8 = (f32[32]{0:T(128)S(1)}, f32[32]{0:T(128)}, u32[]{:S(2)}) copy-start(f32[32]{0:T(128)} %param.13) | copy-start | bytes 388
  18.9 3.6 %copy-start.9 = (f32[32]{0:T(128)S(1)}, f32[32]{0:T(128)}, u32[]{:S(2)}) copy-start(f32[32]{0:T(128)} %param.12) | copy-start | bytes 388
  20.1 4.4 %collective-permute-start.4 = (bf16[4,128,256]{2,1,0:T(8,128)(2,1)}, bf16[4,128,256]{2,1,0:T(8,128)(2,1)}, u32[]{:S(2)}, u32[]{:S(2)}) collective-permute-start(bf16[4,128,256]{2,1,0:T(8,128)(2,1)} %dynamic-slice_bitcast_fusion), channel_id=1, source_target_pairs={{0,32},{32,0},{1,33},{33,1},{2,34},{34,2},{3,35},{35,3},{4,36},{36... | collective-permute-start | bytes 786440 | tf_op jit(solution)/shard_map/ppermute | solution.py:515
  25.6 17.9 %collective-permute-start.5 = (bf16[2,128,256]{2,1,0:T(8,128)(2,1)S(1)}, bf16[2,128,256]{2,1,0:T(8,128)(2,1)S(1)}, u32[]{:S(2)}, u32[]{:S(2)}) collective-permute-start(bf16[2,128,256]{2,1,0:T(8,128)(2,1)S(1)} %get-tuple-element.51), channel_id=1, source_target_pairs={{0,80},{64,0},{16,64},{80,16},{1,81},{65,1},{17,65},{81,17},{2,82}... | collective-permute-start | bytes 393224 | tf_op jit(solution)/shard_map/ppermute | solution.py:523
  29.4 17.9 %collective-permute-start.3 = (bf16[4,128,1024]{2,1,0:T(8,128)(2,1)S(1)}, bf16[4,128,1024]{2,1,0:T(8,128)(2,1)S(1)}, u32[]{:S(2)}, u32[]{:S(2)}) collective-permute-start(bf16[4,128,1024]{2,1,0:T(8,128)(2,1)S(1)} %constant_dynamic-slice_fusion.7), channel_id=1, source_target_pairs={{0,32},{32,0},{1,33},{33,1},{2,34},{34,2},{3,35},{35,3},{4,36},{36... | collective-permute-start | bytes 3145736 | tf_op jit(solution)/shard_map/ppermute | solution.py:515
  29.8 13.7 %collective-permute-start.6 = (bf16[2,128,256]{2,1,0:T(8,128)(2,1)S(1)}, bf16[2,128,256]{2,1,0:T(8,128)(2,1)S(1)}, u32[]{:S(2)}, u32[]{:S(2)}) collective-permute-start(bf16[2,128,256]{2,1,0:T(8,128)(2,1)S(1)} %get-tuple-element.52), channel_id=1, source_target_pairs={{0,16},{64,80},{16,0},{80,64},{1,17},{65,81},{17,1},{81,65},{2,18}... | collective-permute-start | bytes 393224 | tf_op jit(solution)/shard_map/ppermute | solution.py:523
  29.8 17.3 %collective-permute-start.7 = (bf16[2,128,256]{2,1,0:T(8,128)(2,1)S(1)}, bf16[2,128,256]{2,1,0:T(8,128)(2,1)S(1)}, u32[]{:S(2)}, u32[]{:S(2)}) collective-permute-start(bf16[2,128,256]{2,1,0:T(8,128)(2,1)S(1)} %get-tuple-element.50), channel_id=1, source_target_pairs={{0,64},{64,16},{16,80},{80,0},{1,65},{65,17},{17,81},{81,1},{2,66}... | collective-permute-start | bytes 393224 | tf_op jit(solution)/shard_map/ppermute | solution.py:523
  55.5 2.0 %collective-permute-start.8 = (f32[2,8,512]{2,1,0:T(8,128)S(1)}, f32[2,8,512]{2,1,0:T(8,128)S(1)}, u32[]{:S(2)}, u32[]{:S(2)}) collective-permute-start(f32[2,8,512]{2,1,0:T(8,128)S(1)} %get-tuple-element.27), channel_id=1, source_target_pairs={{0,32},{32,0},{1,33},{33,1},{2,34},{34,2},{3,35},{35,3},{4,36},{36... | collective-permute-start | bytes 98312 | tf_op jit(solution)/shard_map/ppermute | solution.py:515
  57.5 4.0 %collective-permute-start.9 = (f32[2,8,512]{2,1,0:T(8,128)S(1)}, f32[2,8,512]{2,1,0:T(8,128)S(1)}, u32[]{:S(2)}, u32[]{:S(2)}) collective-permute-start(f32[2,8,512]{2,1,0:T(8,128)S(1)} %add.165.refs_3_), channel_id=1, source_target_pairs={{0,64},{64,16},{16,80},{80,0},{1,65},{65,17},{17,81},{81,1},{2,66}... | collective-permute-start | bytes 98312 | tf_op jit(solution)/shard_map/ppermute | solution.py:523
  57.5 4.3 %collective-permute-start.10 = (f32[2,8,512]{2,1,0:T(8,128)S(1)}, f32[2,8,512]{2,1,0:T(8,128)S(1)}, u32[]{:S(2)}, u32[]{:S(2)}) collective-permute-start(f32[2,8,512]{2,1,0:T(8,128)S(1)} %add.165.refs_3_), channel_id=1, source_target_pairs={{0,16},{64,80},{16,0},{80,64},{1,17},{65,81},{17,1},{81,65},{2,18}... | collective-permute-start | bytes 98312 | tf_op jit(solution)/shard_map/ppermute | solution.py:523
  58.9 3.8 %collective-permute-start.11 = (f32[2,8,512]{2,1,0:T(8,128)S(1)}, f32[2,8,512]{2,1,0:T(8,128)S(1)}, u32[]{:S(2)}, u32[]{:S(2)}) collective-permute-start(f32[2,8,512]{2,1,0:T(8,128)S(1)} %add.165.refs_3_), channel_id=1, source_target_pairs={{0,80},{64,0},{16,64},{80,16},{1,81},{65,1},{17,65},{81,17},{2,82}... | collective-permute-start | bytes 98312 | tf_op jit(solution)/shard_map/ppermute | solution.py:523
  78.3 1.2 copy-start
  79.4 1.4 copy-start.3
  80.8 5.6 %collective-permute-start.12 = (bf16[2,2,128,1024]{3,2,1,0:T(8,128)(2,1)}, bf16[2,2,128,1024]{3,2,1,0:T(8,128)(2,1)S(1)}, u32[]{:S(2)}, u32[]{:S(2)}) collective-permute-start(bf16[2,2,128,1024]{3,2,1,0:T(8,128)(2,1)} %get-tuple-element.36), channel_id=1, source_target_pairs={{0,32},{32,0},{1,33},{33,1},{2,34},{34,2},{3,35},{35,3},{4,36},{36... | collective-permute-start | bytes 3145736 | tf_op jit(solution)/shard_map/ppermute | solution.py:515
  82.2 4.2 %collective-permute-start.13 = (bf16[1024,128]{1,0:T(8,128)(2,1)S(1)}, bf16[1024,128]{1,0:T(8,128)(2,1)S(1)}, u32[]{:S(2)}, u32[]{:S(2)}) collective-permute-start(bf16[1024,128]{1,0:T(8,128)(2,1)S(1)} %get-tuple-element.38), channel_id=1, source_target_pairs={{0,32},{32,0},{1,33},{33,1},{2,34},{34,2},{3,35},{35,3},{4,36},{36... | collective-permute-start | bytes 786440 | tf_op jit(solution)/shard_map/ppermute | solution.py:515
  82.2 13.5 %all-to-all-start.1 = ((bf16[8,128,256]{2,1,0:T(8,128)(2,1)}), bf16[8,128,256]{2,1,0:T(8,128)(2,1)S(1)}, u32[]{:S(2)}, u32[]{:S(2)}) async-start(bf16[8,128,256]{2,1,0:T(8,128)(2,1)} %bitcast.32), calls=%async_computation.1 | async-start | bytes 1048576 | tf_op jit(solution)/shard_map/all_to_all | solution.py:598
  86.4 1.4 %copy-start.1 = (bf16[1024,768]{1,0:T(8,128)(2,1)S(1)}, bf16[1024,768]{1,0:T(8,128)(2,1)}, u32[]{:S(2)}) copy-start(bf16[1024,768]{1,0:T(8,128)(2,1)} %copy-done) | copy-start | bytes 4718596
  87.8 1.6 %copy-start.4 = (f32[2,2,128,1024]{3,2,1,0:T(8,128)S(1)}, f32[2,2,128,1024]{3,2,1,0:T(8,128)}, u32[]{:S(2)}) copy-start(f32[2,2,128,1024]{3,2,1,0:T(8,128)} %copy-done.3) | copy-start | bytes 6291460
  90.1 1.2 copy-start.2
  95.8 40.9 %all-to-all-start.2 = ((bf16[128,8,768]{2,1,0:T(8,128)(2,1)}), bf16[128,8,768]{2,1,0:T(8,128)(2,1)S(1)}, u32[]{:S(2)}, u32[]{:S(2)}) async-start(bf16[128,8,768]{2,1,0:T(8,128)(2,1)} %bitcast.77), calls=%async_computation.2 | async-start | bytes 3145728 | tf_op jit(solution)/shard_map/all_to_all | solution.py:605
  103.6 24.1 %collective-permute-start.16 = (bf16[128,1024]{1,0:T(8,128)(2,1)S(1)}, bf16[128,1024]{1,0:T(8,128)(2,1)S(1)}, u32[]{:S(2)}, u32[]{:S(2)}) collective-permute-start(bf16[128,1024]{1,0:T(8,128)(2,1)S(1)} %get-tuple-element.42), channel_id=1, source_target_pairs={{0,80},{64,0},{16,64},{80,16},{1,81},{65,1},{17,65},{81,17},{2,82}... | collective-permute-start | bytes 786440 | tf_op jit(solution)/shard_map/ppermute | solution.py:523
  106.3 23.2 %collective-permute-start.15 = (bf16[128,1024]{1,0:T(8,128)(2,1)S(1)}, bf16[128,1024]{1,0:T(8,128)(2,1)}, u32[]{:S(2)}, u32[]{:S(2)}) collective-permute-start(bf16[128,1024]{1,0:T(8,128)(2,1)S(1)} %get-tuple-element.41), channel_id=1, source_target_pairs={{0,16},{64,80},{16,0},{80,64},{1,17},{65,81},{17,1},{81,65},{2,18}... | collective-permute-start | bytes 786440 | tf_op jit(solution)/shard_map/ppermute | solution.py:523
  106.8 27.9 %collective-permute-start.14 = (bf16[128,1024]{1,0:T(8,128)(2,1)S(1)}, bf16[128,1024]{1,0:T(8,128)(2,1)}, u32[]{:S(2)}, u32[]{:S(2)}) collective-permute-start(bf16[128,1024]{1,0:T(8,128)(2,1)S(1)} %get-tuple-element.40), channel_id=1, source_target_pairs={{0,64},{64,16},{16,80},{80,0},{1,65},{65,17},{17,81},{81,1},{2,66}... | collective-permute-start | bytes 786440 | tf_op jit(solution)/shard_map/ppermute | solution.py:523

commit v4 on v3

--- a/solution.py
+++ b/solution.py
@@ -13,10 +13,12 @@
 NT = (((1,), (1,)), ((), ()))
 TN = (((0,), (0,)), ((), ()))
 
-whole = ("yl", "core", "yh", "x", "z")
-rows_axes = ("yh", "x", "z")
-group_axes = ("yl", "core", "yh")
+whole = ("yl", "core", "yh", "xh", "xl", "z")
+rows_axes = ("yh", "xh", "xl", "z")
+group_axes = ("yl", "core", "xl")
 vmem = 32 * 2**20
+wide_vmem = 60 * 2**20
+stack_cost, sum_cost = 12, 24
 
 
 def dot1(a, b, dims):
@@ -106,17 +108,64 @@
     return jnp.concatenate([jnp.where(left, a, zero), jnp.where(left, zero, a)], axis=0)
 
 
-def forward_kernel(tok, weights, par, cot, xv_o, g_o, bc_o, low_o, y_o, st_o, stat_o, state, *, width, inner):
-    _, seqs, block, _ = tok.shape
-    units = [(j, s) for j in range(tok.shape[0]) for s in range(seqs)]
+def pack_kernel(place, tokens, cot, w_xz, w_bcdt, out_0, out_1, out_2, out_3, copies, *, inner, heads, states):
+    cols = lambda block, count=1: pl.ds(pl.multiple_of(block * inner, inner), count * inner)
+    mine = tokens[...]
+    for k, out in enumerate((out_0, out_1, out_2, out_3)):
+        chip = lax.bitwise_xor(place[0], k)
+        first = lax.rem(chip, 2) * 4 + lax.div(chip, 2)
+        out[...] = jnp.concatenate([mine, cot[:, cols(first)], cot[:, cols(first + 2)]], axis=1)
+
+    low = w_bcdt[...].astype(f32)
+    rows = low.shape[0]
+    filled = jnp.zeros((rows, 2 * lanes - (low.shape[1] - 2 * states)), f32)
+    all_steps = jnp.concatenate([low[:, 2 * states :], filled], axis=1)
+    half = jnp.where(place[1] == 0, low[:, :states], low[:, states : 2 * states]).astype(bf16)
+    group = w_xz.shape[1] // (2 * inner)
+    yh, xh, xl, z = copies.shape[:4]
+    for side in range(yh):
+        for s in range(xl):
+            target = (lax.rem(place[2] + side, 2) * 2 + place[1]) * 2 + s
+            steps = pltpu.roll(all_steps, 2 * lanes - target * heads, 1)[:, :lanes]
+            steps = jnp.where(iota(steps.shape, 1) < heads, steps, 0.0).astype(bf16)
+            row = jnp.concatenate([w_xz[:, cols(target)], w_xz[:, cols(group + target)], half, steps], axis=1)
+            for upper in range(xh):
+                copies[side, upper, s] = jnp.broadcast_to(row[None], (z,) + row.shape)
+
+
+def whole_weights(main, other, first, inner):
+    half, got = main[:, 2 * inner : 2 * inner + lanes], other[...]
+    b_part, c_part = jnp.where(first, half, got), jnp.where(first, got, half)
+    return jnp.concatenate([main[:, : 2 * inner], b_part, c_part, main[:, 2 * inner + lanes :]], axis=1)
+
+
+def forward_kernel(place, own, far, w_main, w_other, par, *rest, width, inner):
+    *outs, state = rest
+    first = place[1] == 0
+    weights = whole_weights(w_main, w_other, first, inner)
+    state[...] = jnp.zeros_like(state)
+    steps = outs[0].shape[0] // chunks_per_step
+    for i in range(steps):
+        came = [
+            [a[lax.bitwise_xor(place[0], 2 * s + i)] for a in (own, far)] for s in range(outs[0].shape[1])
+        ]
+        views = [a.at[pl.ds(i * (a.shape[0] // steps), a.shape[0] // steps)] for a in outs]
+        forward_step(first, came, weights, par, *views, state, width=width, inner=inner)
+
+
+def forward_step(
+    first, came, weights, par, tok, cot, xv_o, g_o, bc_o, low_o, y_o, st_o, stat_o, state, *, width, inner
+):
+    per_step, seqs, block, model = tok.shape
+    units = [(j, s) for j in range(per_step) for s in range(seqs)]
+    for s, (own, far) in enumerate(came):
+        one, two = jnp.where(first, own, far), jnp.where(first, far, own)
+        tok[0, s], tok[1, s] = one[:, :model], two[:, :model]
+        cot[0, s], cot[1, s] = one[:, model:], two[:, model:]
     count = len(units)
     heads = inner // width
 
-    @pl.when(pl.program_id(0) == 0)
-    def _():
-        state[...] = jnp.zeros_like(state)
-
-    proj = lax.dot_general(tok[...].reshape(count * block, -1), weights[...], NN, preferred_element_type=f32)
+    proj = lax.dot_general(tok[...].reshape(count * block, -1), weights, NN, preferred_element_type=f32)
     cut = lambda u, first, size: proj[u * block : (u + 1) * block, first : first + size]
     part = lambda a, u: a[:, u * inner : (u + 1) * inner]
     expander = head_expander(inner, width, count)
@@ -171,29 +220,39 @@
     mixed = y * (gate * jax.nn.sigmoid(gate))
     weighted = beside(cot[j, s] for j, s in units).astype(f32) * gain * mixed
     squared = mixed * mixed
-    row, col = iota((8, 2 * inner), 0), iota((8, 2 * inner), 1)
-    chooser = ((row < 2) & ((col >= inner) == (row == 1))).astype(f32).astype(bf16)
+    sums = []
     for u, (j, s) in enumerate(units):
         y_o[j, s] = part(y, u)
         high, low = halves(beside([part(squared, u), part(weighted, u)]))
-        dot = lambda right: lax.dot_general(chooser, right, NT, preferred_element_type=f32)
-        stat_o[0, :, u * block : (u + 1) * block] = dot(high) + dot(low)
-
-
-def norm_kernel(y_i, g_i, cot, stat_0, stat_1, stat_2, stat_3, par, out_o, dy_o, dg_o, *, total):
+        dot = lambda right: lax.dot_general(stat_rows(u, inner), right, NT, preferred_element_type=f32)
+        sums.append(dot(high) + dot(low))
+    stat_o[0] = (sums[0] + sums[1]) + (sums[2] + sums[3])
+
+
+def stat_rows(unit, inner):
+    row, col = iota((8, 2 * inner), 0), iota((8, 2 * inner), 1)
+    return (((row == 2 * unit) & (col < inner)) | ((row == 2 * unit + 1) & (col >= inner))).astype(f32).astype(bf16)
+
+
+def norm_kernel(y, g, cot, stat_0, stat_1, stat_2, stat_3, par, out, dy, dg, *, total):
+    for i in range(y.shape[0] // chunks_per_step):
+        cut = lambda a: a.at[pl.ds(i * chunks_per_step, chunks_per_step)]
+        sums = (stat_0[i] + stat_1[i]) + (stat_2[i] + stat_3[i])
+        norm_step(cut(y), cut(g), cut(cot), sums, par, cut(out), cut(dy), cut(dg), total=total)
+
+
+def norm_step(y_i, g_i, cot, sums, par, out_o, dy_o, dg_o, *, total):
     _, seqs, block, inner = y_i.shape
     gain = par[1:2, :]
-    sums = (stat_0[0] + stat_1[0]) + (stat_2[0] + stat_3[0])
-    scale_row = lax.rsqrt(sums[0:1] * (1.0 / total) + norm_eps)
-    pull_row = scale_row * scale_row * scale_row * sums[1:2] * (1.0 / total)
-    stacked = jnp.concatenate([scale_row, pull_row, jnp.zeros((6, scale_row.shape[1]), f32)], axis=0)
-    row, col = iota((8, 2 * inner), 0), iota((8, 2 * inner), 1)
-    chooser = ((row < 2) & ((col >= inner) == (row == 1))).astype(f32).astype(bf16)
-    spread = dot_ones(halves(stacked), chooser, TN)
+    mean = sums * (1.0 / total)
+    even = lax.rem(iota(mean.shape, 0), 2) == 0
+    scales = lax.rsqrt(jnp.where(even, mean, 1.0) + norm_eps)
+    before = pltpu.roll(scales, 1, 0)
+    stacked = halves(jnp.where(even, scales, before * before * before * mean))
     for u in range(y_i.shape[0] * seqs):
         j, s = u // seqs, u % seqs
-        span = slice(u * block, (u + 1) * block)
-        scale, pull = spread[span, :inner], spread[span, inner:]
+        spread = dot_ones(stacked, stat_rows(u, inner), TN)
+        scale, pull = spread[:, :inner], spread[:, inner:]
         gate, full = g_i[j, s], y_i[j, s]
         gate_sig = jax.nn.sigmoid(gate)
         gate_silu = gate * gate_sig
@@ -204,22 +263,38 @@
         dg_o[j, s] = (d_mixed * full * (gate_sig * (1.0 + gate * (1.0 - gate_sig)))).astype(bf16)
 
 
-def backward_kernel(
-    core, xv_i, bc_i, low_i, y_i, st_i, dy_i, dg_i, tok, par, weights,
-    near_o, far_o, term_o, give_o, grad_state, next_state, term, *, width, inner
+def backward_kernel(core, *refs, width, inner):
+    ins, (par, w_main, w_other) = refs[:8], refs[8:11]
+    near, far, term_o, give_o, grad_state, next_state, term = refs[11:]
+    grad_state[...] = jnp.zeros_like(grad_state)
+    next_state[...] = jnp.zeros_like(next_state)
+    first = core[0] == 0
+    weights = whole_weights(w_main, w_other, first, inner)
+    steps = near.shape[0]
+    for i in reversed(range(steps)):
+        views = [a.at[pl.ds(i * (a.shape[0] // steps), a.shape[0] // steps)] for a in ins + (near, far)]
+        added = backward_step(first, *views, par, weights, grad_state, next_state, width=width, inner=inner)
+        if i == steps - 1:
+            term[...] = added
+        else:
+            term[...] += added
+
+    wide = 2 * inner
+    term_o[:, :wide] = term[:, :wide].astype(bf16)
+    term_o[:, wide + lanes :] = term[:, wide + 2 * lanes :].astype(bf16)
+    b_part, c_part = term[:, wide : wide + lanes], term[:, wide + lanes : wide + 2 * lanes]
+    term_o[:, wide : wide + lanes] = jnp.where(first, b_part, c_part).astype(bf16)
+    give_o[...] = jnp.where(first, c_part, b_part).astype(bf16)
+
+
+def backward_step(
+    first_core, xv_i, bc_i, low_i, y_i, st_i, dy_i, dg_i, tok, near_o, far_o, par, weights, grad_state, next_state,
+    *, width, inner
 ):
     per_step, seqs, block, model = tok.shape
     units = [(j, s) for j in range(per_step) for s in range(seqs)]
     count = len(units)
     heads = inner // width
-    step = pl.program_id(0)
-
-    @pl.when(step == 0)
-    def _():
-        grad_state[...] = jnp.zeros_like(grad_state)
-        next_state[...] = jnp.zeros_like(next_state)
-        term[...] = jnp.zeros_like(term)
-
     part = lambda a, u: a[:, u * inner : (u + 1) * inner]
     expander = head_expander(inner, width, count)
     later = iota((block, block), 1) >= iota((block, block), 0)
@@ -301,29 +376,12 @@
         ],
         axis=0,
     )
-    term[...] += lax.dot_general(tok[...].reshape(count * block, model), here, TN, preferred_element_type=f32)
-    partial = lax.dot_general(here, weights[...], NT, preferred_element_type=f32)
+    added = lax.dot_general(tok[...].reshape(count * block, model), here, TN, preferred_element_type=f32)
+    partial = lax.dot_general(here, weights, NT, preferred_element_type=f32)
     partial = partial.reshape(per_step, seqs, block, model)
-    first = core[0] == 0
-
-    @pl.when(first)
-    def _():
-        near_o[0] = partial[0]
-        far_o[0] = partial[1].astype(bf16)
-
-    @pl.when(jnp.logical_not(first))
-    def _():
-        near_o[0] = partial[1]
-        far_o[0] = partial[0].astype(bf16)
-
-    @pl.when(step == pl.num_programs(0) - 1)
-    def _():
-        wide = 2 * inner
-        term_o[:, :wide] = term[:, :wide].astype(bf16)
-        term_o[:, wide + lanes :] = term[:, wide + 2 * lanes :].astype(bf16)
-        b_part, c_part = term[:, wide : wide + lanes], term[:, wide + lanes : wide + 2 * lanes]
-        term_o[:, wide : wide + lanes] = jnp.where(first, b_part, c_part).astype(bf16)
-        give_o[...] = jnp.where(first, c_part, b_part).astype(bf16)
+    near_o[0] = jnp.where(first_core, partial[0], partial[1])
+    far_o[0] = jnp.where(first_core, partial[1], partial[0]).astype(bf16)
+    return added
 
 
 def join_kernel(_, near, far, term, got, out_0, out_1, out_2, out_3, term_o):
@@ -348,7 +406,7 @@
     def _():
         bcdt_o[...] = jnp.zeros_like(bcdt_o)
 
-    summed = jnp.sum(shares[0].astype(f32), axis=0)
+    summed = jnp.sum(shares[0, :, 0].astype(f32), axis=(0, 1))
     at = pl.multiple_of(step * inner, inner)
     xz_o[:, pl.ds(at, inner)] = summed[:, :inner]
     xz_o[:, pl.ds(pl.multiple_of(half + at, inner), inner)] = summed[:, inner : 2 * inner]
@@ -378,22 +436,50 @@
 
 
 chunks_per_step = 2
-
-
-def forward_call(tok, weights, par, cot, width):
-    chunks, seqs, block, model = tok.shape
-    inner = cot.shape[3]
+smem_spec = pl.BlockSpec(memory_space=pltpu.SMEM)
+vmem_spec = pl.BlockSpec(memory_space=pltpu.VMEM)
+HBM = pltpu.HBM
+
+
+def pack_call(place, tokens, cot, w_xz, w_bcdt, sides, group, heads):
+    block, total = cot.shape
+    inner = total // group
+    states = (w_bcdt.shape[1] - heads * group) // 2
+    copies = sides + (w_xz.shape[0], 2 * inner + states + lanes)
+    piece = (block, tokens.shape[1] + 2 * inner)
+
+    def kernel(*refs):
+        pack_kernel(*refs, inner=inner, heads=heads, states=states)
+
+    return pl.pallas_call(
+        kernel,
+        in_specs=[pl.BlockSpec(memory_space=pltpu.SMEM)] + [pl.BlockSpec(memory_space=pltpu.VMEM)] * 4,
+        out_specs=[pl.BlockSpec(memory_space=pltpu.VMEM)] * 5,
+        out_shape=[HBM(piece, bf16)] * 4 + [HBM(copies, bf16)],
+        compiler_params=pltpu.CompilerParams(vmem_limit_bytes=wide_vmem),
+        cost_estimate=cost(2),
+        name="pack_pieces",
+    )(place, tokens, cot, w_xz, w_bcdt)
+
+
+def forward_call(place, own, far, weights, w_other, par, width):
+    _, block, columns = own.shape
+    model = weights.shape[0]
+    inner = columns - model
+    chunks, seqs = 4, 2
     steps = chunks // chunks_per_step
     wide = (chunks, seqs, block, inner)
-    by_chunk = lambda a: chunk_spec(a, per_step=chunks_per_step)
+
     outs = [
-        (wide, by_chunk),
-        (wide, by_chunk),
-        ((chunks, seqs, block, 2 * lanes), by_chunk),
-        ((steps, 3, block, lanes), chunk_spec),
-        (wide, by_chunk),
-        ((chunks, seqs, lanes, inner), by_chunk),
-        ((steps, 8, chunks_per_step * seqs * block), chunk_spec),
+        ((chunks, seqs, block, model), bf16),
+        (wide, bf16),
+        (wide, f32),
+        (wide, f32),
+        ((chunks, seqs, block, 2 * lanes), f32),
+        ((steps, 3, block, lanes), f32),
+        (wide, f32),
+        ((chunks, seqs, lanes, inner), f32),
+        ((steps, 8, block), f32),
     ]
 
     def kernel(*refs):
@@ -401,59 +487,50 @@
 
     return pl.pallas_call(
         kernel,
-        grid=(steps,),
-        in_specs=[by_chunk(tok.shape), fixed_spec(weights.shape), fixed_spec(par.shape), by_chunk(cot.shape)],
-        out_specs=[spec(a) for a, spec in outs],
-        out_shape=[jax.ShapeDtypeStruct(a, f32) for a, _ in outs],
+        in_specs=[smem_spec] + [vmem_spec] * 5,
+        out_specs=[vmem_spec] * len(outs),
+        out_shape=[jax.ShapeDtypeStruct(a, kind) for a, kind in outs],
         scratch_shapes=[pltpu.VMEM((seqs, lanes, inner), f32)],
         compiler_params=pltpu.CompilerParams(vmem_limit_bytes=vmem),
         cost_estimate=cost(12),
         name="forward_scan",
-    )(tok, weights, par, cot)
+    )(place, own, far, weights, w_other, par)
 
 
 def norm_call(y, gate, cot, stats, par, total):
-    chunks = y.shape[0]
-    by_chunk = lambda a: chunk_spec(a.shape, per_step=chunks_per_step)
-
     def kernel(*refs):
         norm_kernel(*refs, total=total)
 
     return pl.pallas_call(
         kernel,
-        grid=(chunks // chunks_per_step,),
-        in_specs=[by_chunk(a) for a in (y, gate, cot)] + [chunk_spec(a.shape) for a in stats] + [fixed_spec(par.shape)],
-        out_specs=[by_chunk(y)] * 3,
-        out_shape=[jax.ShapeDtypeStruct(y.shape, kind) for kind in (bf16, f32, bf16)],
+        in_specs=[vmem_spec] * 8,
+        out_specs=[vmem_spec] * 3,
+        out_shape=[HBM(y.shape, bf16), jax.ShapeDtypeStruct(y.shape, f32), jax.ShapeDtypeStruct(y.shape, bf16)],
         compiler_params=pltpu.CompilerParams(vmem_limit_bytes=vmem),
         cost_estimate=cost(5),
         name="gated_norm",
     )(y, gate, cot, *stats, par)
 
 
-def backward_call(core, xv, bc, low, y, states, d_y, d_gate, tok, par, weights, width):
+def backward_call(core, xv, bc, low, y, states, d_y, d_gate, tok, par, weights, w_other, width):
     chunks, seqs, block, inner = xv.shape
     model, columns = weights.shape
+    columns = columns + lanes
     steps = chunks // chunks_per_step
     half = (steps, seqs, block, model)
-    half_spec = chunk_spec(half, steps)
-    by_chunk = lambda a: chunk_spec(a.shape, steps, chunks_per_step)
 
     def kernel(*refs):
         backward_kernel(*refs, width=width, inner=inner)
 
     return pl.pallas_call(
         kernel,
-        grid=(steps,),
-        in_specs=[pl.BlockSpec(memory_space=pltpu.SMEM), by_chunk(xv), by_chunk(bc), chunk_spec(low.shape, steps)]
-        + [by_chunk(a) for a in (y, states, d_y, d_gate, tok)]
-        + [fixed_spec(par.shape), fixed_spec(weights.shape)],
-        out_specs=[half_spec, half_spec, fixed_spec((model, columns - lanes)), fixed_spec((model, lanes))],
+        in_specs=[smem_spec] + [vmem_spec] * 11,
+        out_specs=[vmem_spec] * 4,
         out_shape=[
-            jax.ShapeDtypeStruct(half, f32),
-            jax.ShapeDtypeStruct(half, bf16),
-            jax.ShapeDtypeStruct((model, columns - lanes), bf16),
-            jax.ShapeDtypeStruct((model, lanes), bf16),
+            HBM(half, f32),
+            HBM(half, bf16),
+            HBM((model, columns - lanes), bf16),
+            HBM((model, lanes), bf16),
         ],
         scratch_shapes=[
             pltpu.VMEM((seqs, lanes, inner), f32),
@@ -463,7 +540,7 @@
         compiler_params=pltpu.CompilerParams(vmem_limit_bytes=vmem),
         cost_estimate=cost(20),
         name="backward_scan",
-    )(core, xv, bc, low, y, states, d_y, d_gate, tok, par, weights)
+    )(core, xv, bc, low, y, states, d_y, d_gate, tok, par, weights, w_other)
 
 
 def join_call(here, near, far, term, got, inner):
@@ -472,7 +549,7 @@
     bc_spec = pl.BlockSpec((term.shape[0], lanes), lambda k, here: (0, 2 * inner // lanes))
 
     def place(k, here):
-        y = lax.rem(here[0] + k, count)
+        y = lax.bitwise_xor(here[0], k)
         return (lax.rem(y, 2), lax.div(y, 2), 0, 0)
 
     spec = pl.BlockSpec((1, 1, block, model), place)
@@ -484,16 +561,17 @@
             in_specs=[spec, spec, bc_spec, pl.BlockSpec(got.shape, lambda k, here: (0, 0))],
             out_specs=[pl.BlockSpec((block, model), lambda k, here: (0, 0))] * count + [bc_spec],
         ),
-        out_shape=[jax.ShapeDtypeStruct((block, model), bf16)] * count + [jax.ShapeDtypeStruct(term.shape, bf16)],
+        out_shape=[HBM((block, model), bf16)] * count + [HBM(term.shape, bf16)],
         input_output_aliases={3: count},
-        compiler_params=pltpu.CompilerParams(vmem_limit_bytes=vmem),
+        compiler_params=pltpu.CompilerParams(vmem_limit_bytes=wide_vmem),
         cost_estimate=cost(3),
         name="join_halves",
     )(here, near, far, term, got)
 
 
 def total_call(shares, inner, heads):
-    group, _, rows, columns = shares.shape
+    times, far, seqs, near, rows, columns = shares.shape
+    group = times * seqs
     shapes = [(rows, 2 * group * inner), (rows, 2 * lanes + group * heads)]
 
     def kernel(*refs):
@@ -502,7 +580,7 @@
     return pl.pallas_call(
         kernel,
         grid=(group,),
-        in_specs=[chunk_spec(shares.shape)],
+        in_specs=[pl.BlockSpec((1, far, 1, near, rows, columns), lambda i: (i // seqs, 0, i % seqs, 0, 0, 0))],
         out_specs=[fixed_spec(a) for a in shapes],
         out_shape=[jax.ShapeDtypeStruct(a, f32) for a in shapes],
         compiler_params=pltpu.CompilerParams(vmem_limit_bytes=vmem),
@@ -515,23 +593,58 @@
     return lax.ppermute(a, "core", [(0, 1), (1, 0)])
 
 
-def around(give, mine):
-    came = [give(0 if mine is None else mine)]
-    spot = lambda y: (y % 2) * 2 + y // 2
-    for shift in (1, 3, 2):
-        pairs = [(spot(y), spot((y + shift) % 4)) for y in range(4)]
-        came.append(lax.ppermute(give(shift if mine is None else (mine + shift) % 4), ("yl", "yh"), pairs))
-    return [came[0], came[1], came[3], came[2]]
-
-
-def in_order(came, mine):
-    turned = [came[0], came[3], came[2], came[1]]
-    return lax.dynamic_slice_in_dim(jnp.stack(turned + turned), 4 - mine, 4, 0)
-
-
-def by_core(own, other, core):
-    first = core == 0
-    return jnp.stack([jnp.where(first, own, other), jnp.where(first, other, own)])
+def around(give):
+    came = [give(0)]
+    spot = lambda chip: (chip % 2) * 2 + chip // 2
+    for k in (1, 2, 3):
+        came.append(lax.ppermute(give(k), ("yl", "xl"), [(spot(chip), spot(chip ^ k)) for chip in range(4)]))
+    return came
+
+
+def stack_kernel(place, a, b, c, d, own_o, give_o):
+    inner = own_o.shape[2] // 5
+    model = 4 * inner
+    for k, came in enumerate((a, b, c, d)):
+        tokens = came[:, :model]
+        one, two = came[:, model : model + inner], came[:, model + inner :]
+        first = place[1] == 0
+        own_o[k] = jnp.concatenate([tokens, jnp.where(first, one, two)], axis=1)
+        give_o[k] = jnp.concatenate([tokens, jnp.where(first, two, one)], axis=1)
+
+
+def stack_call(place, came):
+    block, columns = came[0].shape
+    stacked = (4, block, columns // 6 * 5)
+    return pl.pallas_call(
+        stack_kernel,
+        in_specs=[pl.BlockSpec(memory_space=pltpu.SMEM)] + [pl.BlockSpec(memory_space=pltpu.VMEM)] * 4,
+        out_specs=[pl.BlockSpec(memory_space=pltpu.VMEM)] * 2,
+        out_shape=[HBM(stacked, bf16), HBM(stacked, bf16)],
+        compiler_params=pltpu.CompilerParams(vmem_limit_bytes=wide_vmem),
+        cost_estimate=cost(stack_cost),
+        name="stack_pieces",
+    )(place, *came)
+
+
+def sum_kernel(a, b, c, d, heads, out, layer_o):
+    out[...] = ((a[...].astype(f32) + b[...].astype(f32)) + (c[...].astype(f32) + d[...].astype(f32))).astype(bf16)
+    inner = heads.shape[2]
+    for k in range(heads.shape[0]):
+        layer_o[:, k * inner : (k + 1) * inner] = heads[k]
+
+
+def sum_call(arrays, heads):
+    group, block, inner = heads.shape
+    return pl.pallas_call(
+        sum_kernel,
+        out_shape=[
+            jax.ShapeDtypeStruct(arrays[0].shape, bf16),
+            jax.ShapeDtypeStruct((block, group * inner), bf16),
+        ],
+        compiler_params=pltpu.CompilerParams(vmem_limit_bytes=wide_vmem),
+        cost_estimate=cost(sum_cost),
+        name="sum_pieces",
+    )(*arrays, heads)
 
 
 def body(tokens, cotangent, w_xz, w_bcdt, rate, dt_bias, skip, gain):
@@ -548,41 +661,24 @@
     width = inner // heads
     states = (w_bcdt.shape[1] - rate.shape[0]) // 2
 
-    def picked(target):
-        w_dt = lax.dynamic_slice_in_dim(w_bcdt[:, 2 * states :], target * heads, heads, 1)
-        return jnp.concatenate(
-            [
-                lax.dynamic_slice_in_dim(w_xz, target * inner, inner, 1),
-                lax.dynamic_slice_in_dim(w_xz, total + target * inner, inner, 1),
-                w_bcdt[:, : 2 * states],
-                jnp.pad(w_dt, ((0, 0), (0, lanes - heads))),
-            ],
-            axis=1,
-        )
-
-    yl, yh, core = lax.axis_index("yl"), lax.axis_index("yh"), lax.axis_index("core")
-    w_picked = jnp.stack([picked((((yl + yh + k) % 2) * 2 + core) * seqs + k) for k in range(seqs)])
-    copies = jnp.broadcast_to(w_picked[:, None], (seqs, owners // seqs) + w_picked.shape[1:])
-    copies = copies.reshape((owners,) + w_picked.shape[1:])
-    rest = owners // seqs
+    core = lax.axis_index("core")
+    here = lax.axis_index(("xl", "yl"))
+    place = jnp.stack([here, core, lax.axis_index("yl") + lax.axis_index("yh")]).astype(jnp.int32)
+    sides = tuple(lax.axis_size(name) for name in rows_axes)
+    *pieces, copies = pack_call(place, tokens[0], cotangent[0], w_xz, w_bcdt, sides, group, heads)
+    copies = copies.reshape((owners,) + copies.shape[4:])
+
+    own_came, give_came = stack_call(place, around(lambda shift: pieces[shift]))
+    far_came = partner(give_came)
+
+    rest = owners // sides[0]
     traders = [
-        [(((start + k) % 2) * seqs + k) * rest + i for k in range(seqs) for i in range(rest)] for start in range(2)
+        [(((start + k) % 2) * sides[0] + k) * rest + i for k in range(sides[0]) for i in range(rest)]
+        for start in range(2)
     ]
     weights = lax.all_to_all(copies, ("yl",) + rows_axes, 0, 0, axis_index_groups=traders, tiled=True)
     weights = weights.reshape(model, -1)
-
-    here = lax.axis_index(("yh", "yl"))
-    at = lambda a, index: lax.dynamic_index_in_dim(a, index, 0, keepdims=False)
-
-    tok = in_order(around(lambda y: tokens[0], here), here)
-    tok = by_core(tok, partner(tok), core)
-    tok = tok.reshape(2, 2, 2, block, model).transpose(2, 0, 1, 3, 4).reshape(chunks, seqs, block, model)
-
-    cut = cotangent[0].reshape(block, 2, 2, 2, inner).transpose(2, 3, 1, 0, 4)
-    cut = cut.reshape(2, 4, block, inner)
-    cut = by_core(at(cut, core), partner(at(cut, 1 - core)), core)
-    cot = in_order(around(lambda y: lax.dynamic_index_in_dim(cut, y, 1, keepdims=False), here), here)
-    cot = cot.reshape(2, 2, 2, block, inner).transpose(1, 2, 0, 3, 4).reshape(chunks, seqs, block, inner)
+    w_other = partner(weights[:, 2 * inner : 2 * inner + lanes])
 
     own = lambda a: lax.dynamic_slice_in_dim(a, mine * heads, heads, 0)
     padded = lambda a: jnp.pad(jnp.tile(own(a), lanes // heads), (0, inner - lanes))
@@ -591,34 +687,35 @@
         + [padded(dt_bias), padded(rate)]
         + [jnp.zeros((inner,), f32)] * 4
     )
-    xv, gate, bc, low, y, chunk_states, stats = forward_call(tok, weights, par, cot, width)
+    tok, cot, xv, gate, bc, low, y, chunk_states, stats = forward_call(
+        place, own_came, far_came, weights, w_other, par, width
+    )
     stats = stats + partner(stats)
-    stats = around(lambda y: stats, here)
+    stats = around(lambda shift: stats)
     out, d_y, d_gate = norm_call(y, gate, cot, stats, par, float(total))
     layer_out = lax.all_to_all(out.reshape(group, block, inner), group_axes, 0, 0, tiled=True)
-    layer_out = layer_out.transpose(1, 0, 2).reshape(1, block, total)
     scalar = lambda a: jnp.full((1,), a, jnp.int32)
     near, far, term, give = backward_call(
-        scalar(core), xv, bc, low, y, chunk_states, d_y, d_gate, tok, par, weights, width
+        scalar(core), xv, bc, low, y, chunk_states, d_y, d_gate, tok, par, weights, w_other, width
     )
     *sums, term = join_call(scalar(here), near, partner(far), term, partner(give), inner)
     shares = lax.all_to_all(term.reshape(devices, model // devices, -1), whole, 0, 0, tiled=True)
-    came = around(lambda shift: sums[shift], None)
-    grad_input = sum(a.astype(f32) for a in came).astype(bf16)[None]
+    came = around(lambda shift: sums[shift])
+    grad_input, layer_out = sum_call(came, layer_out)
     grad_xz, grad_bcdt = total_call(
-        shares.reshape(group, devices // group, model // devices, -1), inner, heads
+        shares.reshape(chunks, -1, seqs, lax.axis_size("z"), model // devices, shares.shape[-1]), inner, heads
     )
-    return (layer_out, grad_input, grad_xz, grad_bcdt)
+    return (layer_out[None], grad_input[None], grad_xz, grad_bcdt)
 
 
 def solution(mesh):
-    split = Mesh(mesh.devices.reshape(2, 2, 2, 4, 4), whole)
+    split = Mesh(mesh.devices.reshape(2, 2, 2, 2, 2, 4), whole)
     ctx, fsdp = ("yl", "core"), rows_axes
     placed = (P(fsdp, ctx, None), P(fsdp, ctx, None), P(fsdp, None), P(fsdp, None), P(), P(), P(), P())
     return jax.shard_map(
         body,
         mesh=split,
         in_specs=placed,
-        out_specs=(P(fsdp, ctx, None), P(fsdp, ctx, None), P(ctx + fsdp, None), P(ctx + fsdp, None)),
+        out_specs=(P(fsdp, ctx, None), P(fsdp, ctx, None), P(ctx + fsdp, None), P(ctx + fsdp)),
         check_vma=False,
     )

time: 139 us -> 125 us (0.90)
  local copies, waits for them, and re-layouts: 18.6 us -> 6.01 us
  Pallas kernels: 25.2 us -> 34.9 us
  waiting for transfers between devices: 48.9 us -> 44.7 us
  starting transfers between devices: 40.9 us -> 37 us
  other arithmetic: 3.34 us -> 0.58 us
    ppermute x12 -> x9, waiting for transfers between devices: 43.5 us -> 12.2 us  [around(): lax.ppermute(give(k), ('yl', 'xl'), [(spot(chip), spot(chip ^ k)) for chi...]
    all_to_all x1, waiting for transfers between devices: 0.01 us -> 16.2 us  [body(): lax.all_to_all(term.reshape(devices, model // devices, -1), whole, 0, 0,...]
    all_to_all x1, waiting for transfers between devices: 0.01 us -> 14.5 us  [body(): lax.all_to_all(copies, ('yl',) + rows_axes, 0, 0, axis_index_groups=trade...]
    pallas_call x4 -> x7, Pallas kernels: 24.6 us -> 30.9 us  [the longest x1 11.9 us: backward_call(): pl.pallas_call(kernel, in_specs=[smem_spec] + [vmem_spec] * 11, out_specs...]
    ppermute x12 -> x9, starting transfers between devices: 14.3 us -> 8.66 us  [around(): lax.ppermute(give(k), ('yl', 'xl'), [(spot(chip), spot(chip ^ k)) for chi...]
    all_to_all x1, waiting for transfers between devices: 4.53 us -> 0.69 us  [body(): lax.all_to_all(out.reshape(group, block, inner), group_axes, 0, 0, tiled=...]
    unnamed x33 -> x28, local copies, waits for them, and re-layouts: 8.11 us -> 4.6 us
    pallas_call x1, Pallas kernels: 0.65 us -> 4.03 us  [join_call(): pl.pallas_call(join_kernel, grid_spec=pltpu.PrefetchScalarGridSpec(num_sc...]
  transfers between devices with their start and end apart: 20 -> 17, of which waited for: 10 -> 8; matrix products, arithmetic and copies ran while one was open for 11% -> 1% of each run, Pallas kernels for 0% -> 8%
where the time goes in v4:
time: 125 us; the launch traced here: 124 us
  waiting for transfers between devices  44.7 us (36%)
  starting transfers between devices  37 us (30%)
  Pallas kernels  34.9 us (28%)
  local copies, waits for them, and re-layouts  6.01 us (5%)
    all_to_all x1, waiting for transfers between devices, body(): lax.all_to_all(term.reshape(devices, model // devices, -1), whole, 0, 0,...  16.2 us
    all_to_all x1, waiting for transfers between devices, body(): lax.all_to_all(copies, ('yl',) + rows_axes, 0, 0, axis_index_groups=trade...  14.5 us
    ppermute x9, waiting for transfers between devices, around(): lax.ppermute(give(k), ('yl', 'xl'), [(spot(chip), spot(chip ^ k)) for chi...  12.2 us
    pallas_call x1, Pallas kernels, backward_call(): pl.pallas_call(kernel, in_specs=[smem_spec] + [vmem_spec] * 11, out_specs...  11.9 us
    all_to_all x1, starting transfers between devices, body(): lax.all_to_all(copies, ('yl',) + rows_axes, 0, 0, axis_index_groups=trade...  10.5 us
    ppermute x9, starting transfers between devices, around(): lax.ppermute(give(k), ('yl', 'xl'), [(spot(chip), spot(chip ^ k)) for chi...  8.66 us
    ppermute x5, starting transfers between devices, partner(): return lax.ppermute(a, 'core', [(0, 1), (1, 0)])  7.69 us
    pallas_call x1, Pallas kernels, forward_call(): pl.pallas_call(kernel, in_specs=[smem_spec] + [vmem_spec] * 5, out_specs=...  7.32 us
  transfers between devices with their start and end apart: 17, of which 8 were waited for; matrix products, arithmetic and copies ran while one was open for 1% of the time, Pallas kernels for 8%

profile of v4, /device:TPU:1, one launch (start us, length us, event | category | flops | bytes accessed | tf_op | source)
XLA Modules:
  0.0 124.1 jit_solution(9035737061811756655)
XLA Ops:
  0.6 0.6 pad_add_fusion.refs_0_.place
  1.2 3.1 %pack_pieces.1 = (bf16[128,1536]{1,0:T(8,128)(2,1)}, bf16[128,1536]{1,0:T(8,128)(2,1)}, bf16[128,1536]{1,0:T(8,128)(2,1)}, bf16[128,1536]{1,0:T(8,128)(2,1)}, bf16[2,2,2,4,32,768]{5,4,3,2,1,0:T(8,128)(2,1)}) custom-call(s32[3]{0:T(128)} %pad_add_fusion.refs_0_.place, bf16[128,1024]{1,0:T(8,128)(2,1)} %bitcast.26, bf16[128,2048]{1,0:T(8,128)(2,1)} %bitcast.25, ...), custom_call_target="tpu_custom_call" | custom-call | flops 2200000000 | bytes 7000000 | tf_op jit(solution)/shard_map/pack_pieces/pallas_call | solution.py:454
  4.3 2.1 %collective-permute-start = (bf16[128,1536]{1,0:T(8,128)(2,1)}, bf16[128,1536]{1,0:T(8,128)(2,1)S(1)}, u32[]{:S(2)}, u32[]{:S(2)}) collective-permute-start(bf16[128,1536]{1,0:T(8,128)(2,1)} %get-tuple-element.37), channel_id=1, source_target_pairs={{0,64},{64,0},{4,68},{68,4},{1,65},{65,1},{5,69},{69,5},{2,66},{66... | collective-permute-start | bytes 1179656 | tf_op jit(solution)/shard_map/ppermute | solution.py:600
  6.4 1.2 collective-permute-start.1
  7.6 0.0 collective-permute-start.2
  7.6 10.5 %all-to-all-start = ((bf16[32,32,768]{2,1,0:T(8,128)(2,1)}), bf16[32,32,768]{2,1,0:T(8,128)(2,1)S(1)}, u32[]{:S(2)}, u32[]{:S(2)}) async-start(bf16[32,32,768]{2,1,0:T(8,128)(2,1)} %bitcast.20), calls=%async_computation | async-start | bytes 3145728 | tf_op jit(solution)/shard_map/all_to_all | solution.py:679
  18.1 0.0 collective-permute-done.b
  18.1 0.0 copy-start.4
  18.1 0.0 collective-permute-done.1.c
  18.1 0.0 copy-start.5
  18.1 6.2 %collective-permute-done.2.d = bf16[128,1536]{1,0:T(8,128)(2,1)S(1)} collective-permute-done((bf16[128,1536]{1,0:T(8,128)(2,1)}, bf16[128,1536]{1,0:T(8,128)(2,1)S(1)}, u32[]{:S(2)}, u32[]{:S(2)}) %collective-permute-start.2) | collective-permute-done | bytes 393248 | tf_op jit(solution)/shard_map/ppermute | solution.py:600
  24.3 0.0 copy-done.4
  24.3 0.0 copy-done.5
  24.3 0.8 copy-done.6
  25.1 3.1 %stack_pieces.1 = (bf16[4,128,1280]{2,1,0:T(8,128)(2,1)}, bf16[4,128,1280]{2,1,0:T(8,128)(2,1)}) custom-call(s32[3]{0:T(128)} %pad_add_fusion.refs_0_.place, bf16[128,1536]{1,0:T(8,128)(2,1)} %get-tuple-element.36.a, bf16[128,1536]{1,0:T(8,128)(2,1)} %copy-done.4, bf16[128,1536]{1,0:T(8,128)(2,1)} %copy-done.5, bf16[128,1536]{1,0:T(8,128)(2,1)} %copy-done.6), custom_call_target="tpu_custom_call" | custom-call | flops 13200000000 | bytes 42000000 | tf_op jit(solution)/shard_map/stack_pieces/pallas_call | solution.py:618
  28.2 3.5 %collective-permute-start.3 = (bf16[4,128,1280]{2,1,0:T(8,128)(2,1)}, bf16[4,128,1280]{2,1,0:T(8,128)(2,1)S(1)}, u32[]{:S(2)}, u32[]{:S(2)}) collective-permute-start(bf16[4,128,1280]{2,1,0:T(8,128)(2,1)} %get-tuple-element.41), channel_id=1, source_target_pairs={{0,32},{32,0},{1,33},{33,1},{2,34},{34,2},{3,35},{35,3},{4,36},{36... | collective-permute-start | bytes 3932168 | tf_op jit(solution)/shard_map/ppermute | solution.py:593
  31.7 14.5 %all-to-all-done = bf16[32,32,768]{2,1,0:T(8,128)(2,1)S(1)} async-done(((bf16[32,32,768]{2,1,0:T(8,128)(2,1)}), bf16[32,32,768]{2,1,0:T(8,128)(2,1)S(1)}, u32[]{:S(2)}, u32[]{:S(2)}) %all-to-all-start) | async-done | bytes 1572896 | tf_op jit(solution)/shard_map/all_to_all | solution.py:679
  46.2 2.5 %collective-permute-start.4 = (bf16[1024,128]{1,0:T(8,128)(2,1)S(1)}, bf16[1024,128]{1,0:T(8,128)(2,1)S(1)}, u32[]{:S(2)}, u32[]{:S(2)}) collective-permute-start(bf16[1024,128]{1,0:T(8,128)(2,1)S(1)} %slice.4), channel_id=1, source_target_pairs={{0,32},{32,0},{1,33},{33,1},{2,34},{34,2},{3,35},{35,3},{4,36},{36... | collective-permute-start | bytes 786440 | tf_op jit(solution)/shard_map/ppermute | solution.py:593
  48.7 0.0 copy-done.11
  48.7 0.1 dynamic_slice.15
  48.7 0.0 copy-done.12
  48.7 0.1 dynamic_slice.14
  48.8 0.1 dynamic_slice.12
  48.9 0.1 broadcast_in_dim.17
  49.0 0.1 stack_reshape.3
  49.1 0.1 tile.9
  49.2 0.1 tile.21
  49.3 0.8 dynamic_slice.13
  50.1 0.0 collective-permute-done.3.refs_2_
  50.1 0.0 collective-permute-done.4.refs_4_.refs_11_
  50.1 1.3 %copy-done.1 = bf16[4,128,1280]{2,1,0:T(8,128)(2,1)S(1)} copy-done((bf16[4,128,1280]{2,1,0:T(8,128)(2,1)S(1)}, bf16[4,128,1280]{2,1,0:T(8,128)(2,1)}, u32[]{:S(2)}) %copy-start.1) | copy-done | bytes 1310744
  51.4 7.3 %forward_scan.1 = (bf16[4,2,128,1024]{3,2,1,0:T(8,128)(2,1)S(1)}, bf16[4,2,128,256]{3,2,1,0:T(8,128)(2,1)S(1)}, f32[4,2,128,256]{3,2,1,0:T(8,128)S(1)}, f32[4,2,...) custom-call(s32[3]{0:T(128)S(1)} %copy-done, ...), custom_call_target="tpu_custom_call" | custom-call | flops 13200000000 | bytes 42000000 | tf_op jit(solution)/shard_map/forward_scan/pallas_call | solution.py:488
  58.8 0.1 collective-permute-start.5
  58.9 1.1 collective-permute-done.5
  60.0 0.7 collective-permute-start.8
  60.7 0.7 collective-permute-start.7
  61.4 1.2 collective-permute-start.6
  62.6 0.8 collective-permute-done.8.refs_6_
  63.4 0.0 collective-permute-done.7.refs_5_
  63.4 0.8 collective-permute-done.6.refs_4_
  64.2 1.7 %gated_norm.1 = (bf16[4,2,128,256]{3,2,1,0:T(8,128)(2,1)}, f32[4,2,128,256]{3,2,1,0:T(8,128)S(1)}, bf16[4,2,128,256]{3,2,1,0:T(8,128)(2,1)S(1)}) custom-call(f32[4,2,128,256]{3,2,1,0:T(8,128)S(1)} %get-tuple-element.46.refs_0_.refs_4_, f32[4,2,128,256]{3,2,1,0:T(8,128)S(1)} %get-tuple-element.48.refs_1_, ...), custom_call_target="tpu_custom_call" | custom-call | flops 5500000256 | bytes 17500000 | tf_op jit(solution)/shard_map/gated_norm/pallas_call | solution.py:504
  65.9 11.9 %backward_scan.1 = (f32[2,2,128,1024]{3,2,1,0:T(8,128)}, bf16[2,2,128,1024]{3,2,1,0:T(8,128)(2,1)}, bf16[1024,768]{1,0:T(8,128)(2,1)}, bf16[1024,128]{1,0:T(8,128)(2,1)}) custom-call(s32[1]{0:T(128)} %bitcast.1.refs_0_, f32[4,2,128,256]{3,2,1,0:T(8,128)S(1)} %get-tuple-element.43.refs_1_, f32[4,2,128,256]{3,2,1,0:T(8,128)S(1)} %get-tuple-element.44.refs_2_, ...), custom_call_target="tpu_custom_call" | custom-call | flops 22000001024 | bytes 70000000 | tf_op jit(solution)/shard_map/backward_scan/pallas_call | solution.py:525
  77.8 1.6 %collective-permute-start.9 = (bf16[2,2,128,1024]{3,2,1,0:T(8,128)(2,1)}, bf16[2,2,128,1024]{3,2,1,0:T(8,128)(2,1)S(1)}, u32[]{:S(2)}, u32[]{:S(2)}) collective-permute-start(bf16[2,2,128,1024]{3,2,1,0:T(8,128)(2,1)} %get-tuple-element.55), channel_id=1, source_target_pairs={{0,32},{32,0},{1,33},{33,1},{2,34},{34,2},{3,35},{35,3},{4,36},{36... | collective-permute-start | bytes 3145736 | tf_op jit(solution)/shard_map/ppermute | solution.py:593
  79.4 0.0 collective-permute-start.10
  79.4 3.9 %all-to-all-start.1 = ((bf16[8,128,256]{2,1,0:T(8,128)(2,1)}), bf16[8,128,256]{2,1,0:T(8,128)(2,1)S(1)}, u32[]{:S(2)}, u32[]{:S(2)}) async-start(bf16[8,128,256]{2,1,0:T(8,128)(2,1)} %bitcast.21), calls=%async_computation.1 | async-start | bytes 1048576 | tf_op jit(solution)/shard_map/all_to_all | solution.py:696
  83.3 0.0 collective-permute-done.10.got
  83.3 0.0 collective-permute-done.9.far
  83.3 0.7 copy-done.10
  84.0 0.3 copy-done.3
  84.3 4.0 %join_halves.1 = (bf16[128,1024]{1,0:T(8,128)(2,1)}, bf16[128,1024]{1,0:T(8,128)(2,1)}, bf16[128,1024]{1,0:T(8,128)(2,1)}, bf16[128,1024]{1,0:T(8,128)(2,1)}, bf16[1024,768]{1,0:T(8,128)(2,1)}) custom-call(s32[1]{0:T(128)} %bitcast._, f32[2,2,128,1024]{3,2,1,0:T(8,128)} %get-tuple-element.54.near, ...), custom_call_target="tpu_custom_call", output_to_operand_aliasing={{4}: (3, {})} | custom-call | flops 3300000000 | bytes 10500000 | tf_op jit(solution)/shard_map/join_halves/pallas_call | solution.py:556
  88.4 1.4 %collective-permute-start.11 = (bf16[128,1024]{1,0:T(8,128)(2,1)}, bf16[128,1024]{1,0:T(8,128)(2,1)S(1)}, u32[]{:S(2)}, u32[]{:S(2)}) collective-permute-start(bf16[128,1024]{1,0:T(8,128)(2,1)} %get-tuple-element.59), channel_id=1, source_target_pairs={{0,64},{64,0},{4,68},{68,4},{1,65},{65,1},{5,69},{69,5},{2,66},{66... | collective-permute-start | bytes 786440 | tf_op jit(solution)/shard_map/ppermute | solution.py:600
  89.8 1.2 collective-permute-start.12
  91.0 0.1 collective-permute-start.13
  91.0 0.7 all-to-all-done.1.heads
  91.7 0.8 copy-done.2
  92.5 6.3 %all-to-all-start.2 = ((bf16[128,8,768]{2,1,0:T(8,128)(2,1)}), bf16[128,8,768]{2,1,0:T(8,128)(2,1)S(1)}, u32[]{:S(2)}, u32[]{:S(2)}) async-start(bf16[128,8,768]{2,1,0:T(8,128)(2,1)} %bitcast.19), calls=%async_computation.2 | async-start | bytes 3145728 | tf_op jit(solution)/shard_map/all_to_all | solution.py:702
  98.8 0.0 collective-permute-done.11.b
  98.8 0.0 collective-permute-done.12.c
  98.8 0.0 copy-start.8
  98.8 4.5 %collective-permute-done.13.d = bf16[128,1024]{1,0:T(8,128)(2,1)S(1)} collective-permute-done((bf16[128,1024]{1,0:T(8,128)(2,1)}, bf16[128,1024]{1,0:T(8,128)(2,1)S(1)}, u32[]{:S(2)}, u32[]{:S(2)}) %collective-permute-start.13) | collective-permute-done | bytes 262176 | tf_op jit(solution)/shard_map/ppermute | solution.py:600
  103.3 0.7 copy-done.9
  104.0 2.4 %sum_pieces.1 = (bf16[128,1024]{1,0:T(8,128)(2,1)}, bf16[128,2048]{1,0:T(8,128)(2,1)}) custom-call(bf16[128,1024]{1,0:T(8,128)(2,1)} %get-tuple-element.58.a, bf16[128,1024]{1,0:T(8,128)(2,1)} %copy-done.7, bf16[128,1024]{1,0:T(8,128)(2,1)} %copy-done.8, bf16[128,1024]{1,0:T(8,128)(2,1)} %copy-done.9, bf16[8,128,256]{2,1,0:T(8,128)(2,1)} %copy-done.2), custom_call_target="tpu_custom_call" | custom-call | flops 26400000000 | bytes 84000000 | tf_op jit(solution)/shard_map/sum_pieces/pallas_call | solution.py:638
  106.4 16.2 %all-to-all-done.2 = bf16[128,8,768]{2,1,0:T(8,128)(2,1)S(1)} async-done(((bf16[128,8,768]{2,1,0:T(8,128)(2,1)}), bf16[128,8,768]{2,1,0:T(8,128)(2,1)S(1)}, u32[]{:S(2)}, u32[]{:S(2)}) %all-to-all-start.2) | async-done | bytes 1572896 | tf_op jit(solution)/shard_map/all_to_all | solution.py:702
  122.6 1.5 %total_shares.1 = (f32[8,4096]{1,0:T(8,128)}, f32[8,288]{1,0:T(8,128)}) custom-call(bf16[4,4,2,4,8,768]{5,4,3,2,1,0:T(8,128)(2,1)S(1)} %bitcast.18), custom_call_target="tpu_custom_call" | custom-call | flops 2200000000 | bytes 7000000 | tf_op jit(solution)/shard_map/total_shares/pallas_call | solution.py:580
  (23 shorter events, 0.1 us)
Async XLA Ops:
  4.3 13.8 %collective-permute-start = (bf16[128,1536]{1,0:T(8,128)(2,1)}, bf16[128,1536]{1,0:T(8,128)(2,1)S(1)}, u32[]{:S(2)}, u32[]{:S(2)}) collective-permute-start(bf16[128,1536]{1,0:T(8,128)(2,1)} %get-tuple-element.37), channel_id=1, source_target_pairs={{0,64},{64,0},{4,68},{68,4},{1,65},{65,1},{5,69},{69,5},{2,66},{66... | collective-permute-start | bytes 1179656 | tf_op jit(solution)/shard_map/ppermute | solution.py:600
  6.4 11.7 %collective-permute-start.1 = (bf16[128,1536]{1,0:T(8,128)(2,1)}, bf16[128,1536]{1,0:T(8,128)(2,1)S(1)}, u32[]{:S(2)}, u32[]{:S(2)}) collective-permute-start(bf16[128,1536]{1,0:T(8,128)(2,1)} %get-tuple-element.38), channel_id=1, source_target_pairs={{0,4},{64,68},{4,0},{68,64},{1,5},{65,69},{5,1},{69,65},{2,6},{66,... | collective-permute-start | bytes 1179656 | tf_op jit(solution)/shard_map/ppermute | solution.py:600
  7.6 16.7 %collective-permute-start.2 = (bf16[128,1536]{1,0:T(8,128)(2,1)}, bf16[128,1536]{1,0:T(8,128)(2,1)S(1)}, u32[]{:S(2)}, u32[]{:S(2)}) collective-permute-start(bf16[128,1536]{1,0:T(8,128)(2,1)} %get-tuple-element.39), channel_id=1, source_target_pairs={{0,68},{64,4},{4,64},{68,0},{1,69},{65,5},{5,65},{69,1},{2,70},{66... | collective-permute-start | bytes 1179656 | tf_op jit(solution)/shard_map/ppermute | solution.py:600
  7.6 38.6 %all-to-all-start = ((bf16[32,32,768]{2,1,0:T(8,128)(2,1)}), bf16[32,32,768]{2,1,0:T(8,128)(2,1)S(1)}, u32[]{:S(2)}, u32[]{:S(2)}) async-start(bf16[32,32,768]{2,1,0:T(8,128)(2,1)} %bitcast.20), calls=%async_computation | async-start | bytes 3145728 | tf_op jit(solution)/shard_map/all_to_all | solution.py:679
  18.1 6.2 %copy-start.4 = (bf16[128,1536]{1,0:T(8,128)(2,1)}, bf16[128,1536]{1,0:T(8,128)(2,1)S(1)}, u32[]{:S(2)}) copy-start(bf16[128,1536]{1,0:T(8,128)(2,1)S(1)} %collective-permute-done.b) | copy-start | bytes 1179652
  18.1 6.2 %copy-start.5 = (bf16[128,1536]{1,0:T(8,128)(2,1)}, bf16[128,1536]{1,0:T(8,128)(2,1)S(1)}, u32[]{:S(2)}) copy-start(bf16[128,1536]{1,0:T(8,128)(2,1)S(1)} %collective-permute-done.1.c) | copy-start | bytes 1179652
  24.3 0.8 copy-start.6
  25.1 23.6 %copy-start.11 = (f32[32]{0:T(128)S(1)}, f32[32]{0:T(128)}, u32[]{:S(2)}) copy-start(f32[32]{0:T(128)} %param.12) | copy-start | bytes 388
  25.1 23.7 %copy-start.12 = (f32[32]{0:T(128)S(1)}, f32[32]{0:T(128)}, u32[]{:S(2)}) copy-start(f32[32]{0:T(128)} %param.13) | copy-start | bytes 388
  25.1 23.7 %copy-start.13 = (f32[32]{0:T(128)S(1)}, f32[32]{0:T(128)}, u32[]{:S(2)}) copy-start(f32[32]{0:T(128)} %param.14) | copy-start | bytes 388
  25.1 25.0 %copy-start = (s32[3]{0:T(128)S(1)}, s32[3]{0:T(128)}, u32[]{:S(2)}) copy-start(s32[3]{0:T(128)} %pad_add_fusion.refs_0_.place) | copy-start | bytes 40
  28.2 21.9 %collective-permute-start.3 = (bf16[4,128,1280]{2,1,0:T(8,128)(2,1)}, bf16[4,128,1280]{2,1,0:T(8,128)(2,1)S(1)}, u32[]{:S(2)}, u32[]{:S(2)}) collective-permute-start(bf16[4,128,1280]{2,1,0:T(8,128)(2,1)} %get-tuple-element.41), channel_id=1, source_target_pairs={{0,32},{32,0},{1,33},{33,1},{2,34},{34,2},{3,35},{35,3},{4,36},{36... | collective-permute-start | bytes 3932168 | tf_op jit(solution)/shard_map/ppermute | solution.py:593
  46.2 3.9 %collective-permute-start.4 = (bf16[1024,128]{1,0:T(8,128)(2,1)S(1)}, bf16[1024,128]{1,0:T(8,128)(2,1)S(1)}, u32[]{:S(2)}, u32[]{:S(2)}) collective-permute-start(bf16[1024,128]{1,0:T(8,128)(2,1)S(1)} %slice.4), channel_id=1, source_target_pairs={{0,32},{32,0},{1,33},{33,1},{2,34},{34,2},{3,35},{35,3},{4,36},{36... | collective-permute-start | bytes 786440 | tf_op jit(solution)/shard_map/ppermute | solution.py:593
  50.1 1.3 %copy-start.1 = (bf16[4,128,1280]{2,1,0:T(8,128)(2,1)S(1)}, bf16[4,128,1280]{2,1,0:T(8,128)(2,1)}, u32[]{:S(2)}) copy-start(bf16[4,128,1280]{2,1,0:T(8,128)(2,1)} %get-tuple-element.40.refs_1_) | copy-start | bytes 3932164
  58.8 1.2 collective-permute-start.5
  60.0 3.4 %collective-permute-start.8 = (f32[2,8,128]{2,1,0:T(8,128)S(1)}, f32[2,8,128]{2,1,0:T(8,128)S(1)}, u32[]{:S(2)}, u32[]{:S(2)}) collective-permute-start(f32[2,8,128]{2,1,0:T(8,128)S(1)} %add.33.refs_3_), channel_id=1, source_target_pairs={{0,68},{64,4},{4,64},{68,0},{1,69},{65,5},{5,65},{69,1},{2,70},{66... | collective-permute-start | bytes 24584 | tf_op jit(solution)/shard_map/ppermute | solution.py:600
  60.7 2.7 %collective-permute-start.7 = (f32[2,8,128]{2,1,0:T(8,128)S(1)}, f32[2,8,128]{2,1,0:T(8,128)S(1)}, u32[]{:S(2)}, u32[]{:S(2)}) collective-permute-start(f32[2,8,128]{2,1,0:T(8,128)S(1)} %add.33.refs_3_), channel_id=1, source_target_pairs={{0,4},{64,68},{4,0},{68,64},{1,5},{65,69},{5,1},{69,65},{2,6},{66,... | collective-permute-start | bytes 24584 | tf_op jit(solution)/shard_map/ppermute | solution.py:600
  61.4 2.8 %collective-permute-start.6 = (f32[2,8,128]{2,1,0:T(8,128)S(1)}, f32[2,8,128]{2,1,0:T(8,128)S(1)}, u32[]{:S(2)}, u32[]{:S(2)}) collective-permute-start(f32[2,8,128]{2,1,0:T(8,128)S(1)} %add.33.refs_3_), channel_id=1, source_target_pairs={{0,64},{64,0},{4,68},{68,4},{1,65},{65,1},{5,69},{69,5},{2,66},{66... | collective-permute-start | bytes 24584 | tf_op jit(solution)/shard_map/ppermute | solution.py:600
  77.8 5.5 %collective-permute-start.9 = (bf16[2,2,128,1024]{3,2,1,0:T(8,128)(2,1)}, bf16[2,2,128,1024]{3,2,1,0:T(8,128)(2,1)S(1)}, u32[]{:S(2)}, u32[]{:S(2)}) collective-permute-start(bf16[2,2,128,1024]{3,2,1,0:T(8,128)(2,1)} %get-tuple-element.55), channel_id=1, source_target_pairs={{0,32},{32,0},{1,33},{33,1},{2,34},{34,2},{3,35},{35,3},{4,36},{36... | collective-permute-start | bytes 3145736 | tf_op jit(solution)/shard_map/ppermute | solution.py:593
  79.4 3.9 %collective-permute-start.10 = (bf16[1024,128]{1,0:T(8,128)(2,1)}, bf16[1024,128]{1,0:T(8,128)(2,1)S(1)}, u32[]{:S(2)}, u32[]{:S(2)}) collective-permute-start(bf16[1024,128]{1,0:T(8,128)(2,1)} %get-tuple-element.57), channel_id=1, source_target_pairs={{0,32},{32,0},{1,33},{33,1},{2,34},{34,2},{3,35},{35,3},{4,36},{36... | collective-permute-start | bytes 786440 | tf_op jit(solution)/shard_map/ppermute | solution.py:593
  79.4 12.4 %all-to-all-start.1 = ((bf16[8,128,256]{2,1,0:T(8,128)(2,1)}), bf16[8,128,256]{2,1,0:T(8,128)(2,1)S(1)}, u32[]{:S(2)}, u32[]{:S(2)}) async-start(bf16[8,128,256]{2,1,0:T(8,128)(2,1)} %bitcast.21), calls=%async_computation.1 | async-start | bytes 1048576 | tf_op jit(solution)/shard_map/all_to_all | solution.py:696
  83.3 0.7 copy-start.10
  83.3 1.0 copy-start.3
  88.4 10.4 %collective-permute-start.11 = (bf16[128,1024]{1,0:T(8,128)(2,1)}, bf16[128,1024]{1,0:T(8,128)(2,1)S(1)}, u32[]{:S(2)}, u32[]{:S(2)}) collective-permute-start(bf16[128,1024]{1,0:T(8,128)(2,1)} %get-tuple-element.59), channel_id=1, source_target_pairs={{0,64},{64,0},{4,68},{68,4},{1,65},{65,1},{5,69},{69,5},{2,66},{66... | collective-permute-start | bytes 786440 | tf_op jit(solution)/shard_map/ppermute | solution.py:600
  89.8 9.1 %collective-permute-start.12 = (bf16[128,1024]{1,0:T(8,128)(2,1)}, bf16[128,1024]{1,0:T(8,128)(2,1)S(1)}, u32[]{:S(2)}, u32[]{:S(2)}) collective-permute-start(bf16[128,1024]{1,0:T(8,128)(2,1)} %get-tuple-element.60), channel_id=1, source_target_pairs={{0,4},{64,68},{4,0},{68,64},{1,5},{65,69},{5,1},{69,65},{2,6},{66,... | collective-permute-start | bytes 786440 | tf_op jit(solution)/shard_map/ppermute | solution.py:600
  91.0 12.3 %collective-permute-start.13 = (bf16[128,1024]{1,0:T(8,128)(2,1)}, bf16[128,1024]{1,0:T(8,128)(2,1)S(1)}, u32[]{:S(2)}, u32[]{:S(2)}) collective-permute-start(bf16[128,1024]{1,0:T(8,128)(2,1)} %get-tuple-element.61), channel_id=1, source_target_pairs={{0,68},{64,4},{4,64},{68,0},{1,69},{65,5},{5,65},{69,1},{2,70},{66... | collective-permute-start | bytes 786440 | tf_op jit(solution)/shard_map/ppermute | solution.py:600
  91.7 0.8 copy-start.2
  92.5 30.1 %all-to-all-start.2 = ((bf16[128,8,768]{2,1,0:T(8,128)(2,1)}), bf16[128,8,768]{2,1,0:T(8,128)(2,1)S(1)}, u32[]{:S(2)}, u32[]{:S(2)}) async-start(bf16[128,8,768]{2,1,0:T(8,128)(2,1)} %bitcast.19), calls=%async_computation.2 | async-start | bytes 3145728 | tf_op jit(solution)/shard_map/all_to_all | solution.py:702
  98.8 4.5 %copy-start.7 = (bf16[128,1024]{1,0:T(8,128)(2,1)}, bf16[128,1024]{1,0:T(8,128)(2,1)S(1)}, u32[]{:S(2)}) copy-start(bf16[128,1024]{1,0:T(8,128)(2,1)S(1)} %collective-permute-done.11.b) | copy-start | bytes 786436
  98.8 4.5 %copy-start.8 = (bf16[128,1024]{1,0:T(8,128)(2,1)}, bf16[128,1024]{1,0:T(8,128)(2,1)S(1)}, u32[]{:S(2)}) copy-start(bf16[128,1024]{1,0:T(8,128)(2,1)S(1)} %collective-permute-done.12.c) | copy-start | bytes 786436
  103.3 0.7 copy-start.9

commit v5 on v4

--- a/solution.py
+++ b/solution.py
@@ -108,7 +108,9 @@
     return jnp.concatenate([jnp.where(left, a, zero), jnp.where(left, zero, a)], axis=0)
 
 
-def pack_kernel(place, tokens, cot, w_xz, w_bcdt, out_0, out_1, out_2, out_3, copies, *, inner, heads, states):
+def pack_kernel(tokens, cot, w_xz, w_bcdt, out_0, out_1, out_2, out_3, copies, *, inner, heads, states):
+    yl = lax.axis_index("yl")
+    place = (lax.axis_index("xl") * 2 + yl, lax.axis_index("core"), yl + lax.axis_index("yh"))
     cols = lambda block, count=1: pl.ds(pl.multiple_of(block * inner, inner), count * inner)
     mine = tokens[...]
     for k, out in enumerate((out_0, out_1, out_2, out_3)):
@@ -234,14 +236,7 @@
     return (((row == 2 * unit) & (col < inner)) | ((row == 2 * unit + 1) & (col >= inner))).astype(f32).astype(bf16)
 
 
-def norm_kernel(y, g, cot, stat_0, stat_1, stat_2, stat_3, par, out, dy, dg, *, total):
-    for i in range(y.shape[0] // chunks_per_step):
-        cut = lambda a: a.at[pl.ds(i * chunks_per_step, chunks_per_step)]
-        sums = (stat_0[i] + stat_1[i]) + (stat_2[i] + stat_3[i])
-        norm_step(cut(y), cut(g), cut(cot), sums, par, cut(out), cut(dy), cut(dg), total=total)
-
-
-def norm_step(y_i, g_i, cot, sums, par, out_o, dy_o, dg_o, *, total):
+def norm_step(y_i, g_i, cot, sums, par, out_o, *, total):
     _, seqs, block, inner = y_i.shape
     gain = par[1:2, :]
     mean = sums * (1.0 / total)
@@ -249,6 +244,7 @@
     scales = lax.rsqrt(jnp.where(even, mean, 1.0) + norm_eps)
     before = pltpu.roll(scales, 1, 0)
     stacked = halves(jnp.where(even, scales, before * before * before * mean))
+    d_y, d_gate = [], []
     for u in range(y_i.shape[0] * seqs):
         j, s = u // seqs, u % seqs
         spread = dot_ones(stacked, stat_rows(u, inner), TN)
@@ -259,25 +255,29 @@
         mixed = full * gate_silu
         out_o[j, s] = (mixed * scale * gain).astype(bf16)
         d_mixed = cot[j, s].astype(f32) * gain * scale - mixed * pull
-        dy_o[j, s] = d_mixed * gate_silu
-        dg_o[j, s] = (d_mixed * full * (gate_sig * (1.0 + gate * (1.0 - gate_sig)))).astype(bf16)
-
-
-def backward_kernel(core, *refs, width, inner):
-    ins, (par, w_main, w_other) = refs[:8], refs[8:11]
-    near, far, term_o, give_o, grad_state, next_state, term = refs[11:]
+        d_y.append(d_mixed * gate_silu)
+        d_gate.append((d_mixed * full * (gate_sig * (1.0 + gate * (1.0 - gate_sig)))).astype(bf16))
+    return beside(d_y), d_gate
+
+
+def backward_kernel(core, *refs, width, inner, total):
+    ins, stats, (par, w_main, w_other) = refs[:8], refs[8:12], refs[12:15]
+    out, near, far, term_o, give_o, grad_state, next_state, here_all = refs[15:]
     grad_state[...] = jnp.zeros_like(grad_state)
     next_state[...] = jnp.zeros_like(next_state)
     first = core[0] == 0
     weights = whole_weights(w_main, w_other, first, inner)
     steps = near.shape[0]
     for i in reversed(range(steps)):
-        views = [a.at[pl.ds(i * (a.shape[0] // steps), a.shape[0] // steps)] for a in ins + (near, far)]
-        added = backward_step(first, *views, par, weights, grad_state, next_state, width=width, inner=inner)
-        if i == steps - 1:
-            term[...] = added
-        else:
-            term[...] += added
+        views = [a.at[pl.ds(i * (a.shape[0] // steps), a.shape[0] // steps)] for a in ins + (out, near, far)]
+        sums = (stats[0][i] + stats[1][i]) + (stats[2][i] + stats[3][i])
+        added = backward_step(
+            first, *views, sums, par, weights, grad_state, next_state, width=width, inner=inner, total=total
+        )
+        rows = added.shape[0]
+        here_all[i * rows : (i + 1) * rows, :] = added
+    tok = ins[7]
+    term = lax.dot_general(tok[...].reshape(steps * rows, -1), here_all[...], TN, preferred_element_type=f32)
 
     wide = 2 * inner
     term_o[:, :wide] = term[:, :wide].astype(bf16)
@@ -288,8 +288,8 @@
 
 
 def backward_step(
-    first_core, xv_i, bc_i, low_i, y_i, st_i, dy_i, dg_i, tok, near_o, far_o, par, weights, grad_state, next_state,
-    *, width, inner
+    first_core, xv_i, g_i, bc_i, low_i, y_i, st_i, cot, tok, out_o, near_o, far_o, sums, par, weights,
+    grad_state, next_state, *, width, inner, total
 ):
     per_step, seqs, block, model = tok.shape
     units = [(j, s) for j in range(per_step) for s in range(seqs)]
@@ -309,7 +309,7 @@
     c_two = [halves(bc_i[j, s, :, lanes:]) for j, s in units]
     scores_t = [dot3(b_two[u], c_two[u], NT) for u in range(count)]
     xv = beside(xv_i[j, s] for j, s in units)
-    d_y = beside(dy_i[j, s] for j, s in units)
+    d_y, d_gate = norm_step(y_i, g_i, cot, sums, par, out_o, total=total)
     sig = jax.nn.sigmoid(xv)
     values = xv * sig
     y = beside(y_i[j, s] for j, s in units) - skip * values
@@ -370,32 +370,25 @@
     d_xv = (d_values * (sig * (1.0 + xv * (1.0 - sig)))).astype(bf16)
     here = jnp.concatenate(
         [
-            beside([part(d_xv, u), dg_i[j, s], d_b[u].astype(bf16), d_c[u].astype(bf16)]
+            beside([part(d_xv, u), d_gate[u], d_b[u].astype(bf16), d_c[u].astype(bf16)]
                    + [unpacked(d_raw, u, heads).astype(bf16)])
             for u, (j, s) in enumerate(units)
         ],
         axis=0,
     )
-    added = lax.dot_general(tok[...].reshape(count * block, model), here, TN, preferred_element_type=f32)
     partial = lax.dot_general(here, weights, NT, preferred_element_type=f32)
     partial = partial.reshape(per_step, seqs, block, model)
     near_o[0] = jnp.where(first_core, partial[0], partial[1])
     far_o[0] = jnp.where(first_core, partial[1], partial[0]).astype(bf16)
-    return added
-
-
-def join_kernel(_, near, far, term, got, out_0, out_1, out_2, out_3, term_o):
-    step = pl.program_id(0)
-    both = (near[0, 0] + far[0, 0].astype(f32)).astype(bf16)
+    return here
+
+
+def join_kernel(place, near, far, term, got, out_0, out_1, out_2, out_3, term_o):
     for k, out in enumerate((out_0, out_1, out_2, out_3)):
-
-        @pl.when(step == k)
-        def _(out=out):
-            out[...] = both
-
-    @pl.when(step == 0)
-    def _():
-        term_o[...] = (term[...].astype(f32) + got[...].astype(f32)).astype(bf16)
+        chip = lax.bitwise_xor(place[0], k)
+        yl, xl = lax.rem(chip, 2), lax.div(chip, 2)
+        out[...] = (near[yl, xl] + far[yl, xl].astype(f32)).astype(bf16)
+    term_o[...] = (term[...].astype(f32) + got[...].astype(f32)).astype(bf16)
 
 
 def total_kernel(shares, xz_o, bcdt_o, *, inner, heads, group):
@@ -441,7 +434,7 @@
 HBM = pltpu.HBM
 
 
-def pack_call(place, tokens, cot, w_xz, w_bcdt, sides, group, heads):
+def pack_call(tokens, cot, w_xz, w_bcdt, sides, group, heads):
     block, total = cot.shape
     inner = total // group
     states = (w_bcdt.shape[1] - heads * group) // 2
@@ -453,13 +446,13 @@
 
     return pl.pallas_call(
         kernel,
-        in_specs=[pl.BlockSpec(memory_space=pltpu.SMEM)] + [pl.BlockSpec(memory_space=pltpu.VMEM)] * 4,
-        out_specs=[pl.BlockSpec(memory_space=pltpu.VMEM)] * 5,
+        in_specs=[vmem_spec] * 4,
+        out_specs=[vmem_spec] * 5,
         out_shape=[HBM(piece, bf16)] * 4 + [HBM(copies, bf16)],
         compiler_params=pltpu.CompilerParams(vmem_limit_bytes=wide_vmem),
         cost_estimate=cost(2),
         name="pack_pieces",
-    )(place, tokens, cot, w_xz, w_bcdt)
+    )(tokens, cot, w_xz, w_bcdt)
 
 
 def forward_call(place, own, far, weights, w_other, par, width):
@@ -497,36 +490,22 @@
     )(place, own, far, weights, w_other, par)
 
 
-def norm_call(y, gate, cot, stats, par, total):
-    def kernel(*refs):
-        norm_kernel(*refs, total=total)
-
-    return pl.pallas_call(
-        kernel,
-        in_specs=[vmem_spec] * 8,
-        out_specs=[vmem_spec] * 3,
-        out_shape=[HBM(y.shape, bf16), jax.ShapeDtypeStruct(y.shape, f32), jax.ShapeDtypeStruct(y.shape, bf16)],
-        compiler_params=pltpu.CompilerParams(vmem_limit_bytes=vmem),
-        cost_estimate=cost(5),
-        name="gated_norm",
-    )(y, gate, cot, *stats, par)
-
-
-def backward_call(core, xv, bc, low, y, states, d_y, d_gate, tok, par, weights, w_other, width):
+def backward_call(core, scanned, stats, par, weights, w_other, width, total):
+    xv = scanned[0]
     chunks, seqs, block, inner = xv.shape
     model, columns = weights.shape
     columns = columns + lanes
-    steps = chunks // chunks_per_step
-    half = (steps, seqs, block, model)
+    half = (chunks // chunks_per_step, seqs, block, model)
 
     def kernel(*refs):
-        backward_kernel(*refs, width=width, inner=inner)
+        backward_kernel(*refs, width=width, inner=inner, total=total)
 
     return pl.pallas_call(
         kernel,
-        in_specs=[smem_spec] + [vmem_spec] * 11,
-        out_specs=[vmem_spec] * 4,
+        in_specs=[smem_spec] + [vmem_spec] * 15,
+        out_specs=[vmem_spec] * 5,
         out_shape=[
+            HBM(xv.shape, bf16),
             HBM(half, f32),
             HBM(half, bf16),
             HBM((model, columns - lanes), bf16),
@@ -535,34 +514,25 @@
         scratch_shapes=[
             pltpu.VMEM((seqs, lanes, inner), f32),
             pltpu.VMEM((seqs, lanes, inner), f32),
-            pltpu.VMEM((model, columns), f32),
+            pltpu.VMEM((chunks * seqs * block, columns), bf16),
         ],
         compiler_params=pltpu.CompilerParams(vmem_limit_bytes=vmem),
         cost_estimate=cost(20),
         name="backward_scan",
-    )(core, xv, bc, low, y, states, d_y, d_gate, tok, par, weights, w_other)
+    )(core, *scanned, *stats, par, weights, w_other)
 
 
 def join_call(here, near, far, term, got, inner):
-    halves_of, seqs, block, model = near.shape
-    count = halves_of * seqs
-    bc_spec = pl.BlockSpec((term.shape[0], lanes), lambda k, here: (0, 2 * inner // lanes))
-
-    def place(k, here):
-        y = lax.bitwise_xor(here[0], k)
-        return (lax.rem(y, 2), lax.div(y, 2), 0, 0)
-
-    spec = pl.BlockSpec((1, 1, block, model), place)
+    _, _, block, model = near.shape
+    fixed = lambda shape: pl.BlockSpec(shape, lambda i: (0,) * len(shape))
+    bc_spec = pl.BlockSpec((term.shape[0], lanes), lambda i: (0, 2 * inner // lanes))
     return pl.pallas_call(
         join_kernel,
-        grid_spec=pltpu.PrefetchScalarGridSpec(
-            num_scalar_prefetch=1,
-            grid=(count,),
-            in_specs=[spec, spec, bc_spec, pl.BlockSpec(got.shape, lambda k, here: (0, 0))],
-            out_specs=[pl.BlockSpec((block, model), lambda k, here: (0, 0))] * count + [bc_spec],
-        ),
-        out_shape=[HBM((block, model), bf16)] * count + [HBM(term.shape, bf16)],
-        input_output_aliases={3: count},
+        grid=(1,),
+        in_specs=[smem_spec, fixed(near.shape), fixed(far.shape), bc_spec, fixed(got.shape)],
+        out_specs=[fixed((block, model))] * 4 + [bc_spec],
+        out_shape=[HBM((block, model), bf16)] * 4 + [HBM(term.shape, bf16)],
+        input_output_aliases={3: 4},
         compiler_params=pltpu.CompilerParams(vmem_limit_bytes=wide_vmem),
         cost_estimate=cost(3),
         name="join_halves",
@@ -601,7 +571,7 @@
     return came
 
 
-def stack_kernel(place, a, b, c, d, own_o, give_o):
+def stack_kernel(place, a, b, c, d, _, own_o, give_o):
     inner = own_o.shape[2] // 5
     model = 4 * inner
     for k, came in enumerate((a, b, c, d)):
@@ -612,18 +582,18 @@
         give_o[k] = jnp.concatenate([tokens, jnp.where(first, two, one)], axis=1)
 
 
-def stack_call(place, came):
+def stack_call(place, came, early):
     block, columns = came[0].shape
     stacked = (4, block, columns // 6 * 5)
     return pl.pallas_call(
         stack_kernel,
-        in_specs=[pl.BlockSpec(memory_space=pltpu.SMEM)] + [pl.BlockSpec(memory_space=pltpu.VMEM)] * 4,
-        out_specs=[pl.BlockSpec(memory_space=pltpu.VMEM)] * 2,
+        in_specs=[pl.BlockSpec(memory_space=pltpu.SMEM)] + [vmem_spec] * 4 + [pl.BlockSpec(memory_space=pl.ANY)],
+        out_specs=[vmem_spec] * 2,
         out_shape=[HBM(stacked, bf16), HBM(stacked, bf16)],
         compiler_params=pltpu.CompilerParams(vmem_limit_bytes=wide_vmem),
         cost_estimate=cost(stack_cost),
         name="stack_pieces",
-    )(place, *came)
+    )(place, *came, early)
 
 
 def sum_kernel(a, b, c, d, heads, out, layer_o):
@@ -663,12 +633,19 @@
 
     core = lax.axis_index("core")
     here = lax.axis_index(("xl", "yl"))
-    place = jnp.stack([here, core, lax.axis_index("yl") + lax.axis_index("yh")]).astype(jnp.int32)
+    place = jnp.stack([here, core]).astype(jnp.int32)
     sides = tuple(lax.axis_size(name) for name in rows_axes)
-    *pieces, copies = pack_call(place, tokens[0], cotangent[0], w_xz, w_bcdt, sides, group, heads)
+    *pieces, copies = pack_call(tokens[0], cotangent[0], w_xz, w_bcdt, sides, group, heads)
     copies = copies.reshape((owners,) + copies.shape[4:])
 
-    own_came, give_came = stack_call(place, around(lambda shift: pieces[shift]))
+    own = lambda a: lax.dynamic_slice_in_dim(a, mine * heads, heads, 0)
+    padded = lambda a: jnp.pad(jnp.tile(own(a), lanes // heads), (0, inner - lanes))
+    par = jnp.stack(
+        [jnp.repeat(own(skip), width), lax.dynamic_slice_in_dim(gain, mine * inner, inner, 0)]
+        + [padded(dt_bias), padded(rate)]
+        + [jnp.zeros((inner,), f32)] * 4
+    )
+    own_came, give_came = stack_call(place, around(lambda shift: pieces[shift]), par)
     far_came = partner(give_came)
 
     rest = owners // sides[0]
@@ -680,24 +657,17 @@
     weights = weights.reshape(model, -1)
     w_other = partner(weights[:, 2 * inner : 2 * inner + lanes])
 
-    own = lambda a: lax.dynamic_slice_in_dim(a, mine * heads, heads, 0)
-    padded = lambda a: jnp.pad(jnp.tile(own(a), lanes // heads), (0, inner - lanes))
-    par = jnp.stack(
-        [jnp.repeat(own(skip), width), lax.dynamic_slice_in_dim(gain, mine * inner, inner, 0)]
-        + [padded(dt_bias), padded(rate)]
-        + [jnp.zeros((inner,), f32)] * 4
-    )
     tok, cot, xv, gate, bc, low, y, chunk_states, stats = forward_call(
         place, own_came, far_came, weights, w_other, par, width
     )
     stats = stats + partner(stats)
     stats = around(lambda shift: stats)
-    out, d_y, d_gate = norm_call(y, gate, cot, stats, par, float(total))
+    scalar = lambda a: jnp.full((1,), a, jnp.int32)
+    scanned = (xv, gate, bc, low, y, chunk_states, cot, tok)
+    out, near, far, term, give = backward_call(
+        scalar(core), scanned, stats, par, weights, w_other, width, float(total)
+    )
     layer_out = lax.all_to_all(out.reshape(group, block, inner), group_axes, 0, 0, tiled=True)
-    scalar = lambda a: jnp.full((1,), a, jnp.int32)
-    near, far, term, give = backward_call(
-        scalar(core), xv, bc, low, y, chunk_states, d_y, d_gate, tok, par, weights, w_other, width
-    )
     *sums, term = join_call(scalar(here), near, partner(far), term, partner(give), inner)
     shares = lax.all_to_all(term.reshape(devices, model // devices, -1), whole, 0, 0, tiled=True)
     came = around(lambda shift: sums[shift])

time: 125 us -> 122 us (0.976)
  Pallas kernels: 34.9 us -> 32.8 us
  waiting for transfers between devices: 44.7 us -> 43.4 us
    ppermute x9, waiting for transfers between devices: 12.2 us -> 9.6 us  [around(): lax.ppermute(give(k), ('yl', 'xl'), [(spot(chip), spot(chip ^ k)) for chi...]
    pallas_call x4 -> x3, Pallas kernels: 20.7 us -> 18.6 us  [the longest x1 12.3 us: backward_call(): pl.pallas_call(kernel, in_specs=[smem_spec] + [vmem_spec] * 15, out_specs...]
    unnamed x28 -> x30, local copies, waits for them, and re-layouts: 4.6 us -> 4.61 us
  transfers between devices with their start and end apart: 17 -> 17, of which waited for: 8 -> 9; matrix products, arithmetic and copies ran while one was open for 1% -> 2% of each run, Pallas kernels for 8% -> 7%
where the time goes in v5:
time: 122 us
  waiting for transfers between devices  43.4 us (36%)
  starting transfers between devices  37.7 us (31%)
  Pallas kernels  32.8 us (27%)
  local copies, waits for them, and re-layouts  6.62 us (5%)
    all_to_all x1, waiting for transfers between devices, body(): lax.all_to_all(term.reshape(devices, model // devices, -1), whole, 0, 0,...  15.8 us
    all_to_all x1, waiting for transfers between devices, body(): lax.all_to_all(copies, ('yl',) + rows_axes, 0, 0, axis_index_groups=trade...  14.5 us
    pallas_call x1, Pallas kernels, backward_call(): pl.pallas_call(kernel, in_specs=[smem_spec] + [vmem_spec] * 15, out_specs...  12.3 us
    all_to_all x1, starting transfers between devices, body(): lax.all_to_all(copies, ('yl',) + rows_axes, 0, 0, axis_index_groups=trade...  10.6 us
    ppermute x9, waiting for transfers between devices, around(): lax.ppermute(give(k), ('yl', 'xl'), [(spot(chip), spot(chip ^ k)) for chi...  9.6 us
    ppermute x9, starting transfers between devices, around(): lax.ppermute(give(k), ('yl', 'xl'), [(spot(chip), spot(chip ^ k)) for chi...  8.66 us
    ppermute x5, starting transfers between devices, partner(): return lax.ppermute(a, 'core', [(0, 1), (1, 0)])  8.18 us
    pallas_call x1, Pallas kernels, forward_call(): pl.pallas_call(kernel, in_specs=[smem_spec] + [vmem_spec] * 5, out_specs=...  7.31 us
  transfers between devices with their start and end apart: 17, of which 9 were waited for; matrix products, arithmetic and copies ran while one was open for 2% of the time, Pallas kernels for 7%

profile of v5, /device:TPU:1, one launch (start us, length us, event | category | flops | bytes accessed | tf_op | source)
XLA Modules:
  0.0 121.9 jit_solution(12799859761224091958)
XLA Ops:
  0.6 3.1 %pack_pieces.1 = (bf16[128,1536]{1,0:T(8,128)(2,1)}, bf16[128,1536]{1,0:T(8,128)(2,1)}, bf16[128,1536]{1,0:T(8,128)(2,1)}, bf16[128,1536]{1,0:T(8,128)(2,1)}, bf16[2,2,2,4,32,768]{5,4,3,2,1,0:T(8,128)(2,1)}) custom-call(bf16[128,1024]{1,0:T(8,128)(2,1)} %bitcast.25, bf16[128,2048]{1,0:T(8,128)(2,1)} %bitcast.24, bf16[32,4096]{1,0:T(8,128)(2,1)} %refs_2_.1, ...), custom_call_target="tpu_custom_call" | custom-call | flops 2200000000 | bytes 7000000 | tf_op jit(solution)/shard_map/pack_pieces/pallas_call | solution.py:447
  3.7 2.1 %collective-permute-start = (bf16[128,1536]{1,0:T(8,128)(2,1)}, bf16[128,1536]{1,0:T(8,128)(2,1)S(1)}, u32[]{:S(2)}, u32[]{:S(2)}) collective-permute-start(bf16[128,1536]{1,0:T(8,128)(2,1)} %get-tuple-element.35), channel_id=1, source_target_pairs={{0,64},{64,0},{4,68},{68,4},{1,65},{65,1},{5,69},{69,5},{2,66},{66... | collective-permute-start | bytes 1179656 | tf_op jit(solution)/shard_map/ppermute | solution.py:570
  5.8 1.2 collective-permute-start.1
  7.0 0.0 collective-permute-start.2
  7.1 10.6 %all-to-all-start = ((bf16[32,32,768]{2,1,0:T(8,128)(2,1)}), bf16[32,32,768]{2,1,0:T(8,128)(2,1)S(1)}, u32[]{:S(2)}, u32[]{:S(2)}) async-start(bf16[32,32,768]{2,1,0:T(8,128)(2,1)} %bitcast.18), calls=%async_computation | async-start | bytes 3145728 | tf_op jit(solution)/shard_map/all_to_all | solution.py:656
  17.7 0.0 copy-done.12
  17.7 0.1 dynamic_slice.15
  17.8 0.0 copy-done.13
  17.8 0.1 dynamic_slice.14
  17.8 0.0 copy-done.14
  17.9 0.1 dynamic_slice.12
  17.9 0.1 broadcast_in_dim.17
  18.0 0.1 stack_reshape.3
  18.1 0.1 tile.9
  18.2 0.1 tile.21
  18.3 0.8 dynamic_slice.13
  19.1 0.6 stack.25._.refs_5_.refs_13_
  19.7 0.6 pad_add_fusion.place.refs_0_
  20.3 0.0 collective-permute-done.b
  20.3 0.0 collective-permute-done.1.c
  20.3 0.0 copy-start.6
  20.3 3.4 %collective-permute-done.2.d = bf16[128,1536]{1,0:T(8,128)(2,1)S(1)} collective-permute-done((bf16[128,1536]{1,0:T(8,128)(2,1)}, bf16[128,1536]{1,0:T(8,128)(2,1)S(1)}, u32[]{:S(2)}, u32[]{:S(2)}) %collective-permute-start.2) | collective-permute-done | bytes 393248 | tf_op jit(solution)/shard_map/ppermute | solution.py:570
  23.8 0.8 copy-done.7
  24.5 3.0 %stack_pieces.1 = (bf16[4,128,1280]{2,1,0:T(8,128)(2,1)}, bf16[4,128,1280]{2,1,0:T(8,128)(2,1)}) custom-call(s32[2]{0:T(128)} %pad_add_fusion.place.refs_0_, bf16[128,1536]{1,0:T(8,128)(2,1)} %get-tuple-element.34.a, bf16[128,1536]{1,0:T(8,128)(2,1)} %copy-done.5, bf16[128,1536]{1,0:T(8,128)(2,1)} %copy-done.6, bf16[128,1536]{1,0:T(8,128)(2,1)} %copy-done.7, ...), custom_call_target="tpu_custom_call" | custom-call | flops 13200000000 | bytes 42000000 | tf_op jit(solution)/shard_map/stack_pieces/pallas_call | solution.py:588
  27.6 3.5 %collective-permute-start.3 = (bf16[4,128,1280]{2,1,0:T(8,128)(2,1)}, bf16[4,128,1280]{2,1,0:T(8,128)(2,1)S(1)}, u32[]{:S(2)}, u32[]{:S(2)}) collective-permute-start(bf16[4,128,1280]{2,1,0:T(8,128)(2,1)} %get-tuple-element.39), channel_id=1, source_target_pairs={{0,32},{32,0},{1,33},{33,1},{2,34},{34,2},{3,35},{35,3},{4,36},{36... | collective-permute-start | bytes 3932168 | tf_op jit(solution)/shard_map/ppermute | solution.py:563
  31.1 14.5 %all-to-all-done = bf16[32,32,768]{2,1,0:T(8,128)(2,1)S(1)} async-done(((bf16[32,32,768]{2,1,0:T(8,128)(2,1)}), bf16[32,32,768]{2,1,0:T(8,128)(2,1)S(1)}, u32[]{:S(2)}, u32[]{:S(2)}) %all-to-all-start) | async-done | bytes 1572896 | tf_op jit(solution)/shard_map/all_to_all | solution.py:656
  45.6 2.5 %collective-permute-start.4 = (bf16[1024,128]{1,0:T(8,128)(2,1)S(1)}, bf16[1024,128]{1,0:T(8,128)(2,1)S(1)}, u32[]{:S(2)}, u32[]{:S(2)}) collective-permute-start(bf16[1024,128]{1,0:T(8,128)(2,1)S(1)} %slice.4), channel_id=1, source_target_pairs={{0,32},{32,0},{1,33},{33,1},{2,34},{34,2},{3,35},{35,3},{4,36},{36... | collective-permute-start | bytes 786440 | tf_op jit(solution)/shard_map/ppermute | solution.py:563
  48.1 0.0 collective-permute-done.3.refs_2_
  48.1 1.2 collective-permute-done.4.refs_4_.refs_15_
  49.3 1.3 %copy-done.2 = bf16[4,128,1280]{2,1,0:T(8,128)(2,1)S(1)} copy-done((bf16[4,128,1280]{2,1,0:T(8,128)(2,1)S(1)}, bf16[4,128,1280]{2,1,0:T(8,128)(2,1)}, u32[]{:S(2)}) %copy-start.2) | copy-done | bytes 1310744
  50.6 7.3 %forward_scan.1 = (bf16[4,2,128,1024]{3,2,1,0:T(8,128)(2,1)S(1)}, bf16[4,2,128,256]{3,2,1,0:T(8,128)(2,1)S(1)}, f32[4,2,128,256]{3,2,1,0:T(8,128)S(1)}, f32[4,2,...) custom-call(s32[2]{0:T(128)S(1)} %copy-done.1, ...), custom_call_target="tpu_custom_call" | custom-call | flops 13200000000 | bytes 42000000 | tf_op jit(solution)/shard_map/forward_scan/pallas_call | solution.py:481
  57.9 0.4 collective-permute-start.5
  58.3 0.8 collective-permute-done.5
  59.1 0.7 collective-permute-start.8
  59.9 0.7 collective-permute-start.7
  60.6 1.2 collective-permute-start.6
  61.8 0.8 collective-permute-done.8.refs_12_
  62.5 0.0 collective-permute-done.7.refs_11_
  62.5 0.8 collective-permute-done.6.refs_10_
  63.4 12.3 %backward_scan.1 = (bf16[4,2,128,256]{3,2,1,0:T(8,128)(2,1)}, f32[2,2,128,1024]{3,2,1,0:T(8,128)}, bf16[2,2,128,1024]{3,2,1,0:T(8,128)(2,1)}, bf16[1024,768]{1,0:T(8,128)(2,1)}, bf16[1024,128]{1,0:T(8,128)(2,1)}) custom-call(s32[1]{0:T(128)} %bitcast.1.refs_0_, f32[4,2,128,256]{3,2,1,0:T(8,128)S(1)} %get-tuple-element.41.refs_1_, ...), custom_call_target="tpu_custom_call" | custom-call | flops 22000001024 | bytes 70000000 | tf_op jit(solution)/shard_map/backward_scan/pallas_call | solution.py:503
  75.6 1.8 %collective-permute-start.9 = (bf16[2,2,128,1024]{3,2,1,0:T(8,128)(2,1)}, bf16[2,2,128,1024]{3,2,1,0:T(8,128)(2,1)S(1)}, u32[]{:S(2)}, u32[]{:S(2)}) collective-permute-start(bf16[2,2,128,1024]{3,2,1,0:T(8,128)(2,1)} %get-tuple-element.51), channel_id=1, source_target_pairs={{0,32},{32,0},{1,33},{33,1},{2,34},{34,2},{3,35},{35,3},{4,36},{36... | collective-permute-start | bytes 3145736 | tf_op jit(solution)/shard_map/ppermute | solution.py:563
  77.4 0.0 collective-permute-start.10
  77.4 3.9 %all-to-all-start.1 = ((bf16[8,128,256]{2,1,0:T(8,128)(2,1)}), bf16[8,128,256]{2,1,0:T(8,128)(2,1)S(1)}, u32[]{:S(2)}, u32[]{:S(2)}) async-start(bf16[8,128,256]{2,1,0:T(8,128)(2,1)} %bitcast.20), calls=%async_computation.1 | async-start | bytes 1048576 | tf_op jit(solution)/shard_map/all_to_all | solution.py:670
  81.3 0.0 collective-permute-done.10.got
  81.3 0.0 collective-permute-done.9.far
  81.3 0.0 copy-start.4
  81.3 0.7 copy-done.11
  82.0 0.3 copy-done.4
  82.3 3.2 %join_halves.1 = (bf16[128,1024]{1,0:T(8,128)(2,1)}, bf16[128,1024]{1,0:T(8,128)(2,1)}, bf16[128,1024]{1,0:T(8,128)(2,1)}, bf16[128,1024]{1,0:T(8,128)(2,1)}, bf16[1024,768]{1,0:T(8,128)(2,1)}) custom-call(s32[1]{0:T(128)} %bitcast.place, f32[2,2,128,1024]{3,2,1,0:T(8,128)} %get-tuple-element.50.near, ...), custom_call_target="tpu_custom_call", output_to_operand_aliasing={{4}: (3, {})} | custom-call | flops 3300000000 | bytes 10500000 | tf_op jit(solution)/shard_map/join_halves/pallas_call | solution.py:529
  85.6 1.4 %collective-permute-start.11 = (bf16[128,1024]{1,0:T(8,128)(2,1)}, bf16[128,1024]{1,0:T(8,128)(2,1)S(1)}, u32[]{:S(2)}, u32[]{:S(2)}) collective-permute-start(bf16[128,1024]{1,0:T(8,128)(2,1)} %get-tuple-element.55), channel_id=1, source_target_pairs={{0,64},{64,0},{4,68},{68,4},{1,65},{65,1},{5,69},{69,5},{2,66},{66... | collective-permute-start | bytes 786440 | tf_op jit(solution)/shard_map/ppermute | solution.py:570
  87.0 1.2 collective-permute-start.12
  88.2 0.1 collective-permute-start.13
  88.3 1.5 %all-to-all-done.1.heads = bf16[8,128,256]{2,1,0:T(8,128)(2,1)S(1)} async-done(((bf16[8,128,256]{2,1,0:T(8,128)(2,1)}), bf16[8,128,256]{2,1,0:T(8,128)(2,1)S(1)}, u32[]{:S(2)}, u32[]{:S(2)}) %all-to-all-start.1) | async-done | bytes 524320 | tf_op jit(solution)/shard_map/all_to_all | solution.py:670
  89.7 0.8 copy-done.3
  90.5 6.3 %all-to-all-start.2 = ((bf16[128,8,768]{2,1,0:T(8,128)(2,1)}), bf16[128,8,768]{2,1,0:T(8,128)(2,1)S(1)}, u32[]{:S(2)}, u32[]{:S(2)}) async-start(bf16[128,8,768]{2,1,0:T(8,128)(2,1)} %bitcast.19), calls=%async_computation.2 | async-start | bytes 3145728 | tf_op jit(solution)/shard_map/all_to_all | solution.py:672
  96.9 0.0 collective-permute-done.11.b
  96.9 0.0 collective-permute-done.12.c
  96.9 0.0 copy-start.9
  96.9 4.6 %collective-permute-done.13.d = bf16[128,1024]{1,0:T(8,128)(2,1)S(1)} collective-permute-done((bf16[128,1024]{1,0:T(8,128)(2,1)}, bf16[128,1024]{1,0:T(8,128)(2,1)S(1)}, u32[]{:S(2)}, u32[]{:S(2)}) %collective-permute-start.13) | collective-permute-done | bytes 262176 | tf_op jit(solution)/shard_map/ppermute | solution.py:570
  101.5 0.0 copy-done.9
  101.5 0.7 copy-done.10
  102.2 2.4 %sum_pieces.1 = (bf16[128,1024]{1,0:T(8,128)(2,1)}, bf16[128,2048]{1,0:T(8,128)(2,1)}) custom-call(bf16[128,1024]{1,0:T(8,128)(2,1)} %get-tuple-element.54.a, bf16[128,1024]{1,0:T(8,128)(2,1)} %copy-done.8, bf16[128,1024]{1,0:T(8,128)(2,1)} %copy-done.9, bf16[128,1024]{1,0:T(8,128)(2,1)} %copy-done.10, bf16[8,128,256]{2,1,0:T(8,128)(2,1)} %copy-done.3), custom_call_target="tpu_custom_call" | custom-call | flops 26400000000 | bytes 84000000 | tf_op jit(solution)/shard_map/sum_pieces/pallas_call | solution.py:608
  104.5 15.8 %all-to-all-done.2 = bf16[128,8,768]{2,1,0:T(8,128)(2,1)S(1)} async-done(((bf16[128,8,768]{2,1,0:T(8,128)(2,1)}), bf16[128,8,768]{2,1,0:T(8,128)(2,1)S(1)}, u32[]{:S(2)}, u32[]{:S(2)}) %all-to-all-start.2) | async-done | bytes 1572896 | tf_op jit(solution)/shard_map/all_to_all | solution.py:672
  120.4 1.5 %total_shares.1 = (f32[8,4096]{1,0:T(8,128)}, f32[8,288]{1,0:T(8,128)}) custom-call(bf16[4,4,2,4,8,768]{5,4,3,2,1,0:T(8,128)(2,1)S(1)} %bitcast.17), custom_call_target="tpu_custom_call" | custom-call | flops 2200000000 | bytes 7000000 | tf_op jit(solution)/shard_map/total_shares/pallas_call | solution.py:550
  (24 shorter events, 0.1 us)
Async XLA Ops:
  3.7 16.6 %collective-permute-start = (bf16[128,1536]{1,0:T(8,128)(2,1)}, bf16[128,1536]{1,0:T(8,128)(2,1)S(1)}, u32[]{:S(2)}, u32[]{:S(2)}) collective-permute-start(bf16[128,1536]{1,0:T(8,128)(2,1)} %get-tuple-element.35), channel_id=1, source_target_pairs={{0,64},{64,0},{4,68},{68,4},{1,65},{65,1},{5,69},{69,5},{2,66},{66... | collective-permute-start | bytes 1179656 | tf_op jit(solution)/shard_map/ppermute | solution.py:570
  5.8 14.5 %collective-permute-start.1 = (bf16[128,1536]{1,0:T(8,128)(2,1)}, bf16[128,1536]{1,0:T(8,128)(2,1)S(1)}, u32[]{:S(2)}, u32[]{:S(2)}) collective-permute-start(bf16[128,1536]{1,0:T(8,128)(2,1)} %get-tuple-element.36), channel_id=1, source_target_pairs={{0,4},{64,68},{4,0},{68,64},{1,5},{65,69},{5,1},{69,65},{2,6},{66,... | collective-permute-start | bytes 1179656 | tf_op jit(solution)/shard_map/ppermute | solution.py:570
  7.0 16.7 %collective-permute-start.2 = (bf16[128,1536]{1,0:T(8,128)(2,1)}, bf16[128,1536]{1,0:T(8,128)(2,1)S(1)}, u32[]{:S(2)}, u32[]{:S(2)}) collective-permute-start(bf16[128,1536]{1,0:T(8,128)(2,1)} %get-tuple-element.37), channel_id=1, source_target_pairs={{0,68},{64,4},{4,64},{68,0},{1,69},{65,5},{5,65},{69,1},{2,70},{66... | collective-permute-start | bytes 1179656 | tf_op jit(solution)/shard_map/ppermute | solution.py:570
  7.0 10.6 %copy-start.12 = (f32[32]{0:T(128)S(1)}, f32[32]{0:T(128)}, u32[]{:S(2)}) copy-start(f32[32]{0:T(128)} %param.12) | copy-start | bytes 388
  7.0 10.7 %copy-start.13 = (f32[32]{0:T(128)S(1)}, f32[32]{0:T(128)}, u32[]{:S(2)}) copy-start(f32[32]{0:T(128)} %param.13) | copy-start | bytes 388
  7.1 10.8 %copy-start.14 = (f32[32]{0:T(128)S(1)}, f32[32]{0:T(128)}, u32[]{:S(2)}) copy-start(f32[32]{0:T(128)} %param.14) | copy-start | bytes 388
  7.1 38.5 %all-to-all-start = ((bf16[32,32,768]{2,1,0:T(8,128)(2,1)}), bf16[32,32,768]{2,1,0:T(8,128)(2,1)S(1)}, u32[]{:S(2)}, u32[]{:S(2)}) async-start(bf16[32,32,768]{2,1,0:T(8,128)(2,1)} %bitcast.18), calls=%async_computation | async-start | bytes 3145728 | tf_op jit(solution)/shard_map/all_to_all | solution.py:656
  20.3 3.5 %copy-start.5 = (bf16[128,1536]{1,0:T(8,128)(2,1)}, bf16[128,1536]{1,0:T(8,128)(2,1)S(1)}, u32[]{:S(2)}) copy-start(bf16[128,1536]{1,0:T(8,128)(2,1)S(1)} %collective-permute-done.b) | copy-start | bytes 1179652
  20.3 3.5 %copy-start.6 = (bf16[128,1536]{1,0:T(8,128)(2,1)}, bf16[128,1536]{1,0:T(8,128)(2,1)S(1)}, u32[]{:S(2)}) copy-start(bf16[128,1536]{1,0:T(8,128)(2,1)S(1)} %collective-permute-done.1.c) | copy-start | bytes 1179652
  23.8 0.8 copy-start.7
  24.5 24.7 %copy-start = (f32[8,256]{1,0:T(8,128)S(1)}, f32[8,256]{1,0:T(8,128)}, u32[]{:S(2)}) copy-start(f32[8,256]{1,0:T(8,128)} %stack.25._.refs_5_.refs_13_) | copy-start | bytes 24580
  24.5 24.7 %copy-start.1 = (s32[2]{0:T(128)S(1)}, s32[2]{0:T(128)}, u32[]{:S(2)}) copy-start(s32[2]{0:T(128)} %pad_add_fusion.place.refs_0_) | copy-start | bytes 28
  27.6 20.5 %collective-permute-start.3 = (bf16[4,128,1280]{2,1,0:T(8,128)(2,1)}, bf16[4,128,1280]{2,1,0:T(8,128)(2,1)S(1)}, u32[]{:S(2)}, u32[]{:S(2)}) collective-permute-start(bf16[4,128,1280]{2,1,0:T(8,128)(2,1)} %get-tuple-element.39), channel_id=1, source_target_pairs={{0,32},{32,0},{1,33},{33,1},{2,34},{34,2},{3,35},{35,3},{4,36},{36... | collective-permute-start | bytes 3932168 | tf_op jit(solution)/shard_map/ppermute | solution.py:563
  45.6 3.6 %collective-permute-start.4 = (bf16[1024,128]{1,0:T(8,128)(2,1)S(1)}, bf16[1024,128]{1,0:T(8,128)(2,1)S(1)}, u32[]{:S(2)}, u32[]{:S(2)}) collective-permute-start(bf16[1024,128]{1,0:T(8,128)(2,1)S(1)} %slice.4), channel_id=1, source_target_pairs={{0,32},{32,0},{1,33},{33,1},{2,34},{34,2},{3,35},{35,3},{4,36},{36... | collective-permute-start | bytes 786440 | tf_op jit(solution)/shard_map/ppermute | solution.py:563
  49.3 1.3 %copy-start.2 = (bf16[4,128,1280]{2,1,0:T(8,128)(2,1)S(1)}, bf16[4,128,1280]{2,1,0:T(8,128)(2,1)}, u32[]{:S(2)}) copy-start(bf16[4,128,1280]{2,1,0:T(8,128)(2,1)} %get-tuple-element.38.refs_1_) | copy-start | bytes 3932164
  57.9 1.2 %collective-permute-start.5 = (f32[2,8,128]{2,1,0:T(8,128)S(1)}, f32[2,8,128]{2,1,0:T(8,128)S(1)}, u32[]{:S(2)}, u32[]{:S(2)}) collective-permute-start(f32[2,8,128]{2,1,0:T(8,128)S(1)} %get-tuple-element.49), channel_id=1, source_target_pairs={{0,32},{32,0},{1,33},{33,1},{2,34},{34,2},{3,35},{35,3},{4,36},{36... | collective-permute-start | bytes 24584 | tf_op jit(solution)/shard_map/ppermute | solution.py:563
  59.1 3.4 %collective-permute-start.8 = (f32[2,8,128]{2,1,0:T(8,128)S(1)}, f32[2,8,128]{2,1,0:T(8,128)S(1)}, u32[]{:S(2)}, u32[]{:S(2)}) collective-permute-start(f32[2,8,128]{2,1,0:T(8,128)S(1)} %add.29.refs_9_), channel_id=1, source_target_pairs={{0,68},{64,4},{4,64},{68,0},{1,69},{65,5},{5,65},{69,1},{2,70},{66... | collective-permute-start | bytes 24584 | tf_op jit(solution)/shard_map/ppermute | solution.py:570
  59.9 2.7 %collective-permute-start.7 = (f32[2,8,128]{2,1,0:T(8,128)S(1)}, f32[2,8,128]{2,1,0:T(8,128)S(1)}, u32[]{:S(2)}, u32[]{:S(2)}) collective-permute-start(f32[2,8,128]{2,1,0:T(8,128)S(1)} %add.29.refs_9_), channel_id=1, source_target_pairs={{0,4},{64,68},{4,0},{68,64},{1,5},{65,69},{5,1},{69,65},{2,6},{66,... | collective-permute-start | bytes 24584 | tf_op jit(solution)/shard_map/ppermute | solution.py:570
  60.6 2.8 %collective-permute-start.6 = (f32[2,8,128]{2,1,0:T(8,128)S(1)}, f32[2,8,128]{2,1,0:T(8,128)S(1)}, u32[]{:S(2)}, u32[]{:S(2)}) collective-permute-start(f32[2,8,128]{2,1,0:T(8,128)S(1)} %add.29.refs_9_), channel_id=1, source_target_pairs={{0,64},{64,0},{4,68},{68,4},{1,65},{65,1},{5,69},{69,5},{2,66},{66... | collective-permute-start | bytes 24584 | tf_op jit(solution)/shard_map/ppermute | solution.py:570
  75.6 5.7 %collective-permute-start.9 = (bf16[2,2,128,1024]{3,2,1,0:T(8,128)(2,1)}, bf16[2,2,128,1024]{3,2,1,0:T(8,128)(2,1)S(1)}, u32[]{:S(2)}, u32[]{:S(2)}) collective-permute-start(bf16[2,2,128,1024]{3,2,1,0:T(8,128)(2,1)} %get-tuple-element.51), channel_id=1, source_target_pairs={{0,32},{32,0},{1,33},{33,1},{2,34},{34,2},{3,35},{35,3},{4,36},{36... | collective-permute-start | bytes 3145736 | tf_op jit(solution)/shard_map/ppermute | solution.py:563
  77.4 3.9 %collective-permute-start.10 = (bf16[1024,128]{1,0:T(8,128)(2,1)}, bf16[1024,128]{1,0:T(8,128)(2,1)S(1)}, u32[]{:S(2)}, u32[]{:S(2)}) collective-permute-start(bf16[1024,128]{1,0:T(8,128)(2,1)} %get-tuple-element.53), channel_id=1, source_target_pairs={{0,32},{32,0},{1,33},{33,1},{2,34},{34,2},{3,35},{35,3},{4,36},{36... | collective-permute-start | bytes 786440 | tf_op jit(solution)/shard_map/ppermute | solution.py:563
  77.4 12.4 %all-to-all-start.1 = ((bf16[8,128,256]{2,1,0:T(8,128)(2,1)}), bf16[8,128,256]{2,1,0:T(8,128)(2,1)S(1)}, u32[]{:S(2)}, u32[]{:S(2)}) async-start(bf16[8,128,256]{2,1,0:T(8,128)(2,1)} %bitcast.20), calls=%async_computation.1 | async-start | bytes 1048576 | tf_op jit(solution)/shard_map/all_to_all | solution.py:670
  81.3 0.7 copy-start.11
  81.3 1.0 copy-start.4
  85.6 11.3 %collective-permute-start.11 = (bf16[128,1024]{1,0:T(8,128)(2,1)}, bf16[128,1024]{1,0:T(8,128)(2,1)S(1)}, u32[]{:S(2)}, u32[]{:S(2)}) collective-permute-start(bf16[128,1024]{1,0:T(8,128)(2,1)} %get-tuple-element.55), channel_id=1, source_target_pairs={{0,64},{64,0},{4,68},{68,4},{1,65},{65,1},{5,69},{69,5},{2,66},{66... | collective-permute-start | bytes 786440 | tf_op jit(solution)/shard_map/ppermute | solution.py:570
  87.0 9.9 %collective-permute-start.12 = (bf16[128,1024]{1,0:T(8,128)(2,1)}, bf16[128,1024]{1,0:T(8,128)(2,1)S(1)}, u32[]{:S(2)}, u32[]{:S(2)}) collective-permute-start(bf16[128,1024]{1,0:T(8,128)(2,1)} %get-tuple-element.56), channel_id=1, source_target_pairs={{0,4},{64,68},{4,0},{68,64},{1,5},{65,69},{5,1},{69,65},{2,6},{66,... | collective-permute-start | bytes 786440 | tf_op jit(solution)/shard_map/ppermute | solution.py:570
  88.2 13.3 %collective-permute-start.13 = (bf16[128,1024]{1,0:T(8,128)(2,1)}, bf16[128,1024]{1,0:T(8,128)(2,1)S(1)}, u32[]{:S(2)}, u32[]{:S(2)}) collective-permute-start(bf16[128,1024]{1,0:T(8,128)(2,1)} %get-tuple-element.57), channel_id=1, source_target_pairs={{0,68},{64,4},{4,64},{68,0},{1,69},{65,5},{5,65},{69,1},{2,70},{66... | collective-permute-start | bytes 786440 | tf_op jit(solution)/shard_map/ppermute | solution.py:570
  89.7 0.8 copy-start.3
  90.5 29.9 %all-to-all-start.2 = ((bf16[128,8,768]{2,1,0:T(8,128)(2,1)}), bf16[128,8,768]{2,1,0:T(8,128)(2,1)S(1)}, u32[]{:S(2)}, u32[]{:S(2)}) async-start(bf16[128,8,768]{2,1,0:T(8,128)(2,1)} %bitcast.19), calls=%async_computation.2 | async-start | bytes 3145728 | tf_op jit(solution)/shard_map/all_to_all | solution.py:672
  96.9 4.6 %copy-start.8 = (bf16[128,1024]{1,0:T(8,128)(2,1)}, bf16[128,1024]{1,0:T(8,128)(2,1)S(1)}, u32[]{:S(2)}) copy-start(bf16[128,1024]{1,0:T(8,128)(2,1)S(1)} %collective-permute-done.11.b) | copy-start | bytes 786436
  96.9 4.6 %copy-start.9 = (bf16[128,1024]{1,0:T(8,128)(2,1)}, bf16[128,1024]{1,0:T(8,128)(2,1)S(1)}, u32[]{:S(2)}) copy-start(bf16[128,1024]{1,0:T(8,128)(2,1)S(1)} %collective-permute-done.12.c) | copy-start | bytes 786436
  101.5 0.7 copy-start.10

commit v6 on v5

--- a/solution.py
+++ b/solution.py
@@ -262,29 +262,47 @@
 
 def backward_kernel(core, *refs, width, inner, total):
     ins, stats, (par, w_main, w_other) = refs[:8], refs[8:12], refs[12:15]
-    out, near, far, term_o, give_o, grad_state, next_state, here_all = refs[15:]
+    far_outs, (out, near, far, term, give), (grad_state, next_state, here_all, sems) = refs[15:20], refs[20:25], refs[25:]
+    copies = []
+
+    def send(index, first_row, rows):
+        here, there = (out, near, far, term, give)[index], far_outs[index]
+        span = pl.ds(first_row, rows)
+        copies.append(pltpu.make_async_copy(here.at[span], there.at[span], sems.at[len(copies)]))
+        copies[-1].start()
+
     grad_state[...] = jnp.zeros_like(grad_state)
     next_state[...] = jnp.zeros_like(next_state)
     first = core[0] == 0
     weights = whole_weights(w_main, w_other, first, inner)
     steps = near.shape[0]
+    rows = here_all.shape[0] // steps
     for i in reversed(range(steps)):
         views = [a.at[pl.ds(i * (a.shape[0] // steps), a.shape[0] // steps)] for a in ins + (out, near, far)]
         sums = (stats[0][i] + stats[1][i]) + (stats[2][i] + stats[3][i])
-        added = backward_step(
+        here_all[i * rows : (i + 1) * rows, :] = backward_step(
             first, *views, sums, par, weights, grad_state, next_state, width=width, inner=inner, total=total
         )
-        rows = added.shape[0]
-        here_all[i * rows : (i + 1) * rows, :] = added
+        for index in (2, 1, 0):
+            size = (out, near, far)[index].shape[0] // steps
+            send(index, i * size, size)
+
     tok = ins[7]
-    term = lax.dot_general(tok[...].reshape(steps * rows, -1), here_all[...], TN, preferred_element_type=f32)
-
     wide = 2 * inner
-    term_o[:, :wide] = term[:, :wide].astype(bf16)
-    term_o[:, wide + lanes :] = term[:, wide + 2 * lanes :].astype(bf16)
-    b_part, c_part = term[:, wide : wide + lanes], term[:, wide + lanes : wide + 2 * lanes]
-    term_o[:, wide : wide + lanes] = jnp.where(first, b_part, c_part).astype(bf16)
-    give_o[...] = jnp.where(first, c_part, b_part).astype(bf16)
+    slab = term.shape[0] // slabs
+    for q in range(slabs):
+        span = slice(q * slab, (q + 1) * slab)
+        left = tok[:, :, :, span].reshape(steps * rows, slab)
+        part = lax.dot_general(left, here_all[...], TN, preferred_element_type=f32).astype(bf16)
+        b_part, c_part = part[:, wide : wide + lanes], part[:, wide + lanes : wide + 2 * lanes]
+        give[span, :] = jnp.where(first, c_part, b_part)
+        term[span, :] = jnp.concatenate(
+            [part[:, :wide], jnp.where(first, b_part, c_part), part[:, wide + 2 * lanes :]], axis=1
+        )
+        send(4, q * slab, slab)
+        send(3, q * slab, slab)
+    for copy in copies:
+        copy.wait()
 
 
 def backward_step(
@@ -429,6 +447,7 @@
 
 
 chunks_per_step = 2
+slabs = 2
 smem_spec = pl.BlockSpec(memory_space=pltpu.SMEM)
 vmem_spec = pl.BlockSpec(memory_space=pltpu.VMEM)
 HBM = pltpu.HBM
@@ -496,6 +515,13 @@
     model, columns = weights.shape
     columns = columns + lanes
     half = (chunks // chunks_per_step, seqs, block, model)
+    outs = [
+        (xv.shape, bf16),
+        (half, f32),
+        (half, bf16),
+        ((model, columns - lanes), bf16),
+        ((model, lanes), bf16),
+    ]
 
     def kernel(*refs):
         backward_kernel(*refs, width=width, inner=inner, total=total)
@@ -503,18 +529,14 @@
     return pl.pallas_call(
         kernel,
         in_specs=[smem_spec] + [vmem_spec] * 15,
-        out_specs=[vmem_spec] * 5,
-        out_shape=[
-            HBM(xv.shape, bf16),
-            HBM(half, f32),
-            HBM(half, bf16),
-            HBM((model, columns - lanes), bf16),
-            HBM((model, lanes), bf16),
-        ],
-        scratch_shapes=[
+        out_specs=[pl.BlockSpec(memory_space=pltpu.HBM)] * 5,
+        out_shape=[HBM(shape, kind) for shape, kind in outs],
+        scratch_shapes=[pltpu.VMEM(shape, kind) for shape, kind in outs]
+        + [
             pltpu.VMEM((seqs, lanes, inner), f32),
             pltpu.VMEM((seqs, lanes, inner), f32),
             pltpu.VMEM((chunks * seqs * block, columns), bf16),
+            pltpu.SemaphoreType.DMA((3 * half[0] + 2 * slabs,)),
         ],
         compiler_params=pltpu.CompilerParams(vmem_limit_bytes=vmem),
         cost_estimate=cost(20),

time: 122 us -> 122 us (level)
  no operation moved by 1% of the time
where the time goes in v6:
time: 122 us
  waiting for transfers between devices  43.4 us (36%)
  starting transfers between devices  37.8 us (31%)
  Pallas kernels  32.4 us (27%)
  local copies, waits for them, and re-layouts  6.62 us (5%)
    all_to_all x1, waiting for transfers between devices, body(): lax.all_to_all(term.reshape(devices, model // devices, -1), whole, 0, 0,...  15.8 us
    all_to_all x1, waiting for transfers between devices, body(): lax.all_to_all(copies, ('yl',) + rows_axes, 0, 0, axis_index_groups=trade...  14.5 us
    pallas_call x1, Pallas kernels, backward_call(): pl.pallas_call(kernel, in_specs=[smem_spec] + [vmem_spec] * 15, out_specs...  11.9 us
    all_to_all x1, starting transfers between devices, body(): lax.all_to_all(copies, ('yl',) + rows_axes, 0, 0, axis_index_groups=trade...  10.6 us
    ppermute x9, waiting for transfers between devices, around(): lax.ppermute(give(k), ('yl', 'xl'), [(spot(chip), spot(chip ^ k)) for chi...  9.6 us
    ppermute x9, starting transfers between devices, around(): lax.ppermute(give(k), ('yl', 'xl'), [(spot(chip), spot(chip ^ k)) for chi...  8.66 us
    ppermute x5, starting transfers between devices, partner(): return lax.ppermute(a, 'core', [(0, 1), (1, 0)])  8.35 us
    pallas_call x1, Pallas kernels, forward_call(): pl.pallas_call(kernel, in_specs=[smem_spec] + [vmem_spec] * 5, out_specs=...  7.31 us
  transfers between devices with their start and end apart: 17, of which 9 were waited for; matrix products, arithmetic and copies ran while one was open for 2% of the time, Pallas kernels for 7%

profile of v6, /device:TPU:1, one launch (start us, length us, event | category | flops | bytes accessed | tf_op | source)
XLA Modules:
  0.0 121.6 jit_solution(6076565705197504553)
XLA Ops:
  0.6 3.1 %pack_pieces.1 = (bf16[128,1536]{1,0:T(8,128)(2,1)}, bf16[128,1536]{1,0:T(8,128)(2,1)}, bf16[128,1536]{1,0:T(8,128)(2,1)}, bf16[128,1536]{1,0:T(8,128)(2,1)}, bf16[2,2,2,4,32,768]{5,4,3,2,1,0:T(8,128)(2,1)}) custom-call(bf16[128,1024]{1,0:T(8,128)(2,1)} %bitcast.25, bf16[128,2048]{1,0:T(8,128)(2,1)} %bitcast.24, bf16[32,4096]{1,0:T(8,128)(2,1)} %refs_2_.1, ...), custom_call_target="tpu_custom_call" | custom-call | flops 2200000000 | bytes 7000000 | tf_op jit(solution)/shard_map/pack_pieces/pallas_call | solution.py:466
  3.7 2.1 %collective-permute-start = (bf16[128,1536]{1,0:T(8,128)(2,1)}, bf16[128,1536]{1,0:T(8,128)(2,1)S(1)}, u32[]{:S(2)}, u32[]{:S(2)}) collective-permute-start(bf16[128,1536]{1,0:T(8,128)(2,1)} %get-tuple-element.35), channel_id=1, source_target_pairs={{0,64},{64,0},{4,68},{68,4},{1,65},{65,1},{5,69},{69,5},{2,66},{66... | collective-permute-start | bytes 1179656 | tf_op jit(solution)/shard_map/ppermute | solution.py:592
  5.8 1.2 collective-permute-start.1
  7.0 0.0 collective-permute-start.2
  7.1 10.6 %all-to-all-start = ((bf16[32,32,768]{2,1,0:T(8,128)(2,1)}), bf16[32,32,768]{2,1,0:T(8,128)(2,1)S(1)}, u32[]{:S(2)}, u32[]{:S(2)}) async-start(bf16[32,32,768]{2,1,0:T(8,128)(2,1)} %bitcast.18), calls=%async_computation | async-start | bytes 3145728 | tf_op jit(solution)/shard_map/all_to_all | solution.py:678
  17.7 0.0 copy-done.12
  17.7 0.1 dynamic_slice.15
  17.8 0.0 copy-done.13
  17.8 0.1 dynamic_slice.14
  17.8 0.0 copy-done.14
  17.9 0.1 dynamic_slice.12
  17.9 0.1 broadcast_in_dim.17
  18.0 0.1 stack_reshape.3
  18.1 0.1 tile.9
  18.2 0.1 tile.21
  18.3 0.8 dynamic_slice.13
  19.1 0.6 stack.25._.refs_5_.refs_13_
  19.7 0.6 pad_add_fusion.place.refs_0_
  20.3 0.0 collective-permute-done.b
  20.3 0.0 collective-permute-done.1.c
  20.3 0.0 copy-start.6
  20.3 3.4 %collective-permute-done.2.d = bf16[128,1536]{1,0:T(8,128)(2,1)S(1)} collective-permute-done((bf16[128,1536]{1,0:T(8,128)(2,1)}, bf16[128,1536]{1,0:T(8,128)(2,1)S(1)}, u32[]{:S(2)}, u32[]{:S(2)}) %collective-permute-start.2) | collective-permute-done | bytes 393248 | tf_op jit(solution)/shard_map/ppermute | solution.py:592
  23.8 0.0 copy-done.5
  23.8 0.8 copy-done.7
  24.5 3.0 %stack_pieces.1 = (bf16[4,128,1280]{2,1,0:T(8,128)(2,1)}, bf16[4,128,1280]{2,1,0:T(8,128)(2,1)}) custom-call(s32[2]{0:T(128)} %pad_add_fusion.place.refs_0_, bf16[128,1536]{1,0:T(8,128)(2,1)} %get-tuple-element.34.a, bf16[128,1536]{1,0:T(8,128)(2,1)} %copy-done.5, bf16[128,1536]{1,0:T(8,128)(2,1)} %copy-done.6, bf16[128,1536]{1,0:T(8,128)(2,1)} %copy-done.7, ...), custom_call_target="tpu_custom_call" | custom-call | flops 13200000000 | bytes 42000000 | tf_op jit(solution)/shard_map/stack_pieces/pallas_call | solution.py:610
  27.6 3.5 %collective-permute-start.3 = (bf16[4,128,1280]{2,1,0:T(8,128)(2,1)}, bf16[4,128,1280]{2,1,0:T(8,128)(2,1)S(1)}, u32[]{:S(2)}, u32[]{:S(2)}) collective-permute-start(bf16[4,128,1280]{2,1,0:T(8,128)(2,1)} %get-tuple-element.39), channel_id=1, source_target_pairs={{0,32},{32,0},{1,33},{33,1},{2,34},{34,2},{3,35},{35,3},{4,36},{36... | collective-permute-start | bytes 3932168 | tf_op jit(solution)/shard_map/ppermute | solution.py:585
  31.1 14.5 %all-to-all-done = bf16[32,32,768]{2,1,0:T(8,128)(2,1)S(1)} async-done(((bf16[32,32,768]{2,1,0:T(8,128)(2,1)}), bf16[32,32,768]{2,1,0:T(8,128)(2,1)S(1)}, u32[]{:S(2)}, u32[]{:S(2)}) %all-to-all-start) | async-done | bytes 1572896 | tf_op jit(solution)/shard_map/all_to_all | solution.py:678
  45.6 2.5 %collective-permute-start.4 = (bf16[1024,128]{1,0:T(8,128)(2,1)S(1)}, bf16[1024,128]{1,0:T(8,128)(2,1)S(1)}, u32[]{:S(2)}, u32[]{:S(2)}) collective-permute-start(bf16[1024,128]{1,0:T(8,128)(2,1)S(1)} %slice.4), channel_id=1, source_target_pairs={{0,32},{32,0},{1,33},{33,1},{2,34},{34,2},{3,35},{35,3},{4,36},{36... | collective-permute-start | bytes 786440 | tf_op jit(solution)/shard_map/ppermute | solution.py:585
  48.1 0.0 collective-permute-done.3.refs_2_
  48.1 1.2 collective-permute-done.4.refs_4_.refs_15_
  49.3 1.3 %copy-done.2 = bf16[4,128,1280]{2,1,0:T(8,128)(2,1)S(1)} copy-done((bf16[4,128,1280]{2,1,0:T(8,128)(2,1)S(1)}, bf16[4,128,1280]{2,1,0:T(8,128)(2,1)}, u32[]{:S(2)}) %copy-start.2) | copy-done | bytes 1310744
  50.6 7.3 %forward_scan.1 = (bf16[4,2,128,1024]{3,2,1,0:T(8,128)(2,1)S(1)}, bf16[4,2,128,256]{3,2,1,0:T(8,128)(2,1)S(1)}, f32[4,2,128,256]{3,2,1,0:T(8,128)S(1)}, f32[4,2,...) custom-call(s32[2]{0:T(128)S(1)} %copy-done.1, ...), custom_call_target="tpu_custom_call" | custom-call | flops 13200000000 | bytes 42000000 | tf_op jit(solution)/shard_map/forward_scan/pallas_call | solution.py:500
  57.9 0.4 collective-permute-start.5
  58.3 0.8 collective-permute-done.5
  59.1 0.7 collective-permute-start.8
  59.9 0.7 collective-permute-start.7
  60.6 1.2 %collective-permute-start.6 = (f32[2,8,128]{2,1,0:T(8,128)S(1)}, f32[2,8,128]{2,1,0:T(8,128)S(1)}, u32[]{:S(2)}, u32[]{:S(2)}) collective-permute-start(f32[2,8,128]{2,1,0:T(8,128)S(1)} %add.29.refs_9_), channel_id=1, source_target_pairs={{0,64},{64,0},{4,68},{68,4},{1,65},{65,1},{5,69},{69,5},{2,66},{66... | collective-permute-start | bytes 24584 | tf_op jit(solution)/shard_map/ppermute | solution.py:592
  61.8 0.8 collective-permute-done.8.refs_12_
  62.5 0.0 collective-permute-done.7.refs_11_
  62.5 0.8 collective-permute-done.6.refs_10_
  63.4 11.9 %backward_scan.1 = (bf16[4,2,128,256]{3,2,1,0:T(8,128)(2,1)}, f32[2,2,128,1024]{3,2,1,0:T(8,128)}, bf16[2,2,128,1024]{3,2,1,0:T(8,128)(2,1)}, bf16[1024,768]{1,0:T(8,128)(2,1)}, bf16[1024,128]{1,0:T(8,128)(2,1)}) custom-call(s32[1]{0:T(128)} %bitcast.1.refs_0_, f32[4,2,128,256]{3,2,1,0:T(8,128)S(1)} %get-tuple-element.41.refs_1_, ...), custom_call_target="tpu_custom_call" | custom-call | flops 22000001024 | bytes 70000000 | tf_op jit(solution)/shard_map/backward_scan/pallas_call | solution.py:529
  75.3 1.8 %collective-permute-start.9 = (bf16[2,2,128,1024]{3,2,1,0:T(8,128)(2,1)}, bf16[2,2,128,1024]{3,2,1,0:T(8,128)(2,1)S(1)}, u32[]{:S(2)}, u32[]{:S(2)}) collective-permute-start(bf16[2,2,128,1024]{3,2,1,0:T(8,128)(2,1)} %get-tuple-element.51), channel_id=1, source_target_pairs={{0,32},{32,0},{1,33},{33,1},{2,34},{34,2},{3,35},{35,3},{4,36},{36... | collective-permute-start | bytes 3145736 | tf_op jit(solution)/shard_map/ppermute | solution.py:585
  77.1 0.1 collective-permute-start.10
  77.2 3.8 %all-to-all-start.1 = ((bf16[8,128,256]{2,1,0:T(8,128)(2,1)}), bf16[8,128,256]{2,1,0:T(8,128)(2,1)S(1)}, u32[]{:S(2)}, u32[]{:S(2)}) async-start(bf16[8,128,256]{2,1,0:T(8,128)(2,1)} %bitcast.20), calls=%async_computation.1 | async-start | bytes 1048576 | tf_op jit(solution)/shard_map/all_to_all | solution.py:692
  81.0 0.0 collective-permute-done.10.got
  81.0 0.0 collective-permute-done.9.far
  81.0 0.7 copy-done.11
  81.7 0.3 copy-done.4
  82.1 3.2 %join_halves.1 = (bf16[128,1024]{1,0:T(8,128)(2,1)}, bf16[128,1024]{1,0:T(8,128)(2,1)}, bf16[128,1024]{1,0:T(8,128)(2,1)}, bf16[128,1024]{1,0:T(8,128)(2,1)}, bf16[1024,768]{1,0:T(8,128)(2,1)}) custom-call(s32[1]{0:T(128)} %bitcast.place, f32[2,2,128,1024]{3,2,1,0:T(8,128)} %get-tuple-element.50.near, ...), custom_call_target="tpu_custom_call", output_to_operand_aliasing={{4}: (3, {})} | custom-call | flops 3300000000 | bytes 10500000 | tf_op jit(solution)/shard_map/join_halves/pallas_call | solution.py:551
  85.3 1.4 %collective-permute-start.11 = (bf16[128,1024]{1,0:T(8,128)(2,1)}, bf16[128,1024]{1,0:T(8,128)(2,1)S(1)}, u32[]{:S(2)}, u32[]{:S(2)}) collective-permute-start(bf16[128,1024]{1,0:T(8,128)(2,1)} %get-tuple-element.55), channel_id=1, source_target_pairs={{0,64},{64,0},{4,68},{68,4},{1,65},{65,1},{5,69},{69,5},{2,66},{66... | collective-permute-start | bytes 786440 | tf_op jit(solution)/shard_map/ppermute | solution.py:592
  86.7 1.2 collective-permute-start.12
  87.9 0.1 collective-permute-start.13
  88.0 1.5 %all-to-all-done.1.heads = bf16[8,128,256]{2,1,0:T(8,128)(2,1)S(1)} async-done(((bf16[8,128,256]{2,1,0:T(8,128)(2,1)}), bf16[8,128,256]{2,1,0:T(8,128)(2,1)S(1)}, u32[]{:S(2)}, u32[]{:S(2)}) %all-to-all-start.1) | async-done | bytes 524320 | tf_op jit(solution)/shard_map/all_to_all | solution.py:692
  89.5 0.8 copy-done.3
  90.2 6.3 %all-to-all-start.2 = ((bf16[128,8,768]{2,1,0:T(8,128)(2,1)}), bf16[128,8,768]{2,1,0:T(8,128)(2,1)S(1)}, u32[]{:S(2)}, u32[]{:S(2)}) async-start(bf16[128,8,768]{2,1,0:T(8,128)(2,1)} %bitcast.19), calls=%async_computation.2 | async-start | bytes 3145728 | tf_op jit(solution)/shard_map/all_to_all | solution.py:694
  96.6 0.0 collective-permute-done.11.b
  96.6 0.0 collective-permute-done.12.c
  96.6 0.0 copy-start.9
  96.6 4.6 %collective-permute-done.13.d = bf16[128,1024]{1,0:T(8,128)(2,1)S(1)} collective-permute-done((bf16[128,1024]{1,0:T(8,128)(2,1)}, bf16[128,1024]{1,0:T(8,128)(2,1)S(1)}, u32[]{:S(2)}, u32[]{:S(2)}) %collective-permute-start.13) | collective-permute-done | bytes 262176 | tf_op jit(solution)/shard_map/ppermute | solution.py:592
  101.2 0.0 copy-done.8
  101.2 0.7 copy-done.10
  101.9 2.4 %sum_pieces.1 = (bf16[128,1024]{1,0:T(8,128)(2,1)}, bf16[128,2048]{1,0:T(8,128)(2,1)}) custom-call(bf16[128,1024]{1,0:T(8,128)(2,1)} %get-tuple-element.54.a, bf16[128,1024]{1,0:T(8,128)(2,1)} %copy-done.8, bf16[128,1024]{1,0:T(8,128)(2,1)} %copy-done.9, bf16[128,1024]{1,0:T(8,128)(2,1)} %copy-done.10, bf16[8,128,256]{2,1,0:T(8,128)(2,1)} %copy-done.3), custom_call_target="tpu_custom_call" | custom-call | flops 26400000000 | bytes 84000000 | tf_op jit(solution)/shard_map/sum_pieces/pallas_call | solution.py:630
  104.3 15.8 %all-to-all-done.2 = bf16[128,8,768]{2,1,0:T(8,128)(2,1)S(1)} async-done(((bf16[128,8,768]{2,1,0:T(8,128)(2,1)}), bf16[128,8,768]{2,1,0:T(8,128)(2,1)S(1)}, u32[]{:S(2)}, u32[]{:S(2)}) %all-to-all-start.2) | async-done | bytes 1572896 | tf_op jit(solution)/shard_map/all_to_all | solution.py:694
  120.1 1.5 %total_shares.1 = (f32[8,4096]{1,0:T(8,128)}, f32[8,288]{1,0:T(8,128)}) custom-call(bf16[4,4,2,4,8,768]{5,4,3,2,1,0:T(8,128)(2,1)S(1)} %bitcast.17), custom_call_target="tpu_custom_call" | custom-call | flops 2200000000 | bytes 7000000 | tf_op jit(solution)/shard_map/total_shares/pallas_call | solution.py:572
  (24 shorter events, 0.1 us)
Async XLA Ops:
  3.7 16.6 %collective-permute-start = (bf16[128,1536]{1,0:T(8,128)(2,1)}, bf16[128,1536]{1,0:T(8,128)(2,1)S(1)}, u32[]{:S(2)}, u32[]{:S(2)}) collective-permute-start(bf16[128,1536]{1,0:T(8,128)(2,1)} %get-tuple-element.35), channel_id=1, source_target_pairs={{0,64},{64,0},{4,68},{68,4},{1,65},{65,1},{5,69},{69,5},{2,66},{66... | collective-permute-start | bytes 1179656 | tf_op jit(solution)/shard_map/ppermute | solution.py:592
  5.8 14.5 %collective-permute-start.1 = (bf16[128,1536]{1,0:T(8,128)(2,1)}, bf16[128,1536]{1,0:T(8,128)(2,1)S(1)}, u32[]{:S(2)}, u32[]{:S(2)}) collective-permute-start(bf16[128,1536]{1,0:T(8,128)(2,1)} %get-tuple-element.36), channel_id=1, source_target_pairs={{0,4},{64,68},{4,0},{68,64},{1,5},{65,69},{5,1},{69,65},{2,6},{66,... | collective-permute-start | bytes 1179656 | tf_op jit(solution)/shard_map/ppermute | solution.py:592
  7.0 16.7 %collective-permute-start.2 = (bf16[128,1536]{1,0:T(8,128)(2,1)}, bf16[128,1536]{1,0:T(8,128)(2,1)S(1)}, u32[]{:S(2)}, u32[]{:S(2)}) collective-permute-start(bf16[128,1536]{1,0:T(8,128)(2,1)} %get-tuple-element.37), channel_id=1, source_target_pairs={{0,68},{64,4},{4,64},{68,0},{1,69},{65,5},{5,65},{69,1},{2,70},{66... | collective-permute-start | bytes 1179656 | tf_op jit(solution)/shard_map/ppermute | solution.py:592
  7.0 10.6 %copy-start.12 = (f32[32]{0:T(128)S(1)}, f32[32]{0:T(128)}, u32[]{:S(2)}) copy-start(f32[32]{0:T(128)} %param.12) | copy-start | bytes 388
  7.0 10.7 %copy-start.13 = (f32[32]{0:T(128)S(1)}, f32[32]{0:T(128)}, u32[]{:S(2)}) copy-start(f32[32]{0:T(128)} %param.13) | copy-start | bytes 388
  7.1 10.8 %copy-start.14 = (f32[32]{0:T(128)S(1)}, f32[32]{0:T(128)}, u32[]{:S(2)}) copy-start(f32[32]{0:T(128)} %param.14) | copy-start | bytes 388
  7.1 38.5 %all-to-all-start = ((bf16[32,32,768]{2,1,0:T(8,128)(2,1)}), bf16[32,32,768]{2,1,0:T(8,128)(2,1)S(1)}, u32[]{:S(2)}, u32[]{:S(2)}) async-start(bf16[32,32,768]{2,1,0:T(8,128)(2,1)} %bitcast.18), calls=%async_computation | async-start | bytes 3145728 | tf_op jit(solution)/shard_map/all_to_all | solution.py:678
  20.3 3.5 %copy-start.5 = (bf16[128,1536]{1,0:T(8,128)(2,1)}, bf16[128,1536]{1,0:T(8,128)(2,1)S(1)}, u32[]{:S(2)}) copy-start(bf16[128,1536]{1,0:T(8,128)(2,1)S(1)} %collective-permute-done.b) | copy-start | bytes 1179652
  20.3 3.5 %copy-start.6 = (bf16[128,1536]{1,0:T(8,128)(2,1)}, bf16[128,1536]{1,0:T(8,128)(2,1)S(1)}, u32[]{:S(2)}) copy-start(bf16[128,1536]{1,0:T(8,128)(2,1)S(1)} %collective-permute-done.1.c) | copy-start | bytes 1179652
  23.8 0.8 copy-start.7
  24.5 24.7 %copy-start = (f32[8,256]{1,0:T(8,128)S(1)}, f32[8,256]{1,0:T(8,128)}, u32[]{:S(2)}) copy-start(f32[8,256]{1,0:T(8,128)} %stack.25._.refs_5_.refs_13_) | copy-start | bytes 24580
  24.5 24.7 %copy-start.1 = (s32[2]{0:T(128)S(1)}, s32[2]{0:T(128)}, u32[]{:S(2)}) copy-start(s32[2]{0:T(128)} %pad_add_fusion.place.refs_0_) | copy-start | bytes 28
  27.6 20.5 %collective-permute-start.3 = (bf16[4,128,1280]{2,1,0:T(8,128)(2,1)}, bf16[4,128,1280]{2,1,0:T(8,128)(2,1)S(1)}, u32[]{:S(2)}, u32[]{:S(2)}) collective-permute-start(bf16[4,128,1280]{2,1,0:T(8,128)(2,1)} %get-tuple-element.39), channel_id=1, source_target_pairs={{0,32},{32,0},{1,33},{33,1},{2,34},{34,2},{3,35},{35,3},{4,36},{36... | collective-permute-start | bytes 3932168 | tf_op jit(solution)/shard_map/ppermute | solution.py:585
  45.6 3.6 %collective-permute-start.4 = (bf16[1024,128]{1,0:T(8,128)(2,1)S(1)}, bf16[1024,128]{1,0:T(8,128)(2,1)S(1)}, u32[]{:S(2)}, u32[]{:S(2)}) collective-permute-start(bf16[1024,128]{1,0:T(8,128)(2,1)S(1)} %slice.4), channel_id=1, source_target_pairs={{0,32},{32,0},{1,33},{33,1},{2,34},{34,2},{3,35},{35,3},{4,36},{36... | collective-permute-start | bytes 786440 | tf_op jit(solution)/shard_map/ppermute | solution.py:585
  49.3 1.3 %copy-start.2 = (bf16[4,128,1280]{2,1,0:T(8,128)(2,1)S(1)}, bf16[4,128,1280]{2,1,0:T(8,128)(2,1)}, u32[]{:S(2)}) copy-start(bf16[4,128,1280]{2,1,0:T(8,128)(2,1)} %get-tuple-element.38.refs_1_) | copy-start | bytes 3932164
  57.9 1.2 %collective-permute-start.5 = (f32[2,8,128]{2,1,0:T(8,128)S(1)}, f32[2,8,128]{2,1,0:T(8,128)S(1)}, u32[]{:S(2)}, u32[]{:S(2)}) collective-permute-start(f32[2,8,128]{2,1,0:T(8,128)S(1)} %get-tuple-element.49), channel_id=1, source_target_pairs={{0,32},{32,0},{1,33},{33,1},{2,34},{34,2},{3,35},{35,3},{4,36},{36... | collective-permute-start | bytes 24584 | tf_op jit(solution)/shard_map/ppermute | solution.py:585
  59.1 3.4 %collective-permute-start.8 = (f32[2,8,128]{2,1,0:T(8,128)S(1)}, f32[2,8,128]{2,1,0:T(8,128)S(1)}, u32[]{:S(2)}, u32[]{:S(2)}) collective-permute-start(f32[2,8,128]{2,1,0:T(8,128)S(1)} %add.29.refs_9_), channel_id=1, source_target_pairs={{0,68},{64,4},{4,64},{68,0},{1,69},{65,5},{5,65},{69,1},{2,70},{66... | collective-permute-start | bytes 24584 | tf_op jit(solution)/shard_map/ppermute | solution.py:592
  59.9 2.7 %collective-permute-start.7 = (f32[2,8,128]{2,1,0:T(8,128)S(1)}, f32[2,8,128]{2,1,0:T(8,128)S(1)}, u32[]{:S(2)}, u32[]{:S(2)}) collective-permute-start(f32[2,8,128]{2,1,0:T(8,128)S(1)} %add.29.refs_9_), channel_id=1, source_target_pairs={{0,4},{64,68},{4,0},{68,64},{1,5},{65,69},{5,1},{69,65},{2,6},{66,... | collective-permute-start | bytes 24584 | tf_op jit(solution)/shard_map/ppermute | solution.py:592
  60.6 2.8 %collective-permute-start.6 = (f32[2,8,128]{2,1,0:T(8,128)S(1)}, f32[2,8,128]{2,1,0:T(8,128)S(1)}, u32[]{:S(2)}, u32[]{:S(2)}) collective-permute-start(f32[2,8,128]{2,1,0:T(8,128)S(1)} %add.29.refs_9_), channel_id=1, source_target_pairs={{0,64},{64,0},{4,68},{68,4},{1,65},{65,1},{5,69},{69,5},{2,66},{66... | collective-permute-start | bytes 24584 | tf_op jit(solution)/shard_map/ppermute | solution.py:592
  75.3 5.8 %collective-permute-start.9 = (bf16[2,2,128,1024]{3,2,1,0:T(8,128)(2,1)}, bf16[2,2,128,1024]{3,2,1,0:T(8,128)(2,1)S(1)}, u32[]{:S(2)}, u32[]{:S(2)}) collective-permute-start(bf16[2,2,128,1024]{3,2,1,0:T(8,128)(2,1)} %get-tuple-element.51), channel_id=1, source_target_pairs={{0,32},{32,0},{1,33},{33,1},{2,34},{34,2},{3,35},{35,3},{4,36},{36... | collective-permute-start | bytes 3145736 | tf_op jit(solution)/shard_map/ppermute | solution.py:585
  77.1 3.9 %collective-permute-start.10 = (bf16[1024,128]{1,0:T(8,128)(2,1)}, bf16[1024,128]{1,0:T(8,128)(2,1)S(1)}, u32[]{:S(2)}, u32[]{:S(2)}) collective-permute-start(bf16[1024,128]{1,0:T(8,128)(2,1)} %get-tuple-element.53), channel_id=1, source_target_pairs={{0,32},{32,0},{1,33},{33,1},{2,34},{34,2},{3,35},{35,3},{4,36},{36... | collective-permute-start | bytes 786440 | tf_op jit(solution)/shard_map/ppermute | solution.py:585
  77.2 12.3 %all-to-all-start.1 = ((bf16[8,128,256]{2,1,0:T(8,128)(2,1)}), bf16[8,128,256]{2,1,0:T(8,128)(2,1)S(1)}, u32[]{:S(2)}, u32[]{:S(2)}) async-start(bf16[8,128,256]{2,1,0:T(8,128)(2,1)} %bitcast.20), calls=%async_computation.1 | async-start | bytes 1048576 | tf_op jit(solution)/shard_map/all_to_all | solution.py:692
  81.0 0.7 copy-start.11
  81.0 1.0 copy-start.4
  85.3 11.3 %collective-permute-start.11 = (bf16[128,1024]{1,0:T(8,128)(2,1)}, bf16[128,1024]{1,0:T(8,128)(2,1)S(1)}, u32[]{:S(2)}, u32[]{:S(2)}) collective-permute-start(bf16[128,1024]{1,0:T(8,128)(2,1)} %get-tuple-element.55), channel_id=1, source_target_pairs={{0,64},{64,0},{4,68},{68,4},{1,65},{65,1},{5,69},{69,5},{2,66},{66... | collective-permute-start | bytes 786440 | tf_op jit(solution)/shard_map/ppermute | solution.py:592
  86.7 9.9 %collective-permute-start.12 = (bf16[128,1024]{1,0:T(8,128)(2,1)}, bf16[128,1024]{1,0:T(8,128)(2,1)S(1)}, u32[]{:S(2)}, u32[]{:S(2)}) collective-permute-start(bf16[128,1024]{1,0:T(8,128)(2,1)} %get-tuple-element.56), channel_id=1, source_target_pairs={{0,4},{64,68},{4,0},{68,64},{1,5},{65,69},{5,1},{69,65},{2,6},{66,... | collective-permute-start | bytes 786440 | tf_op jit(solution)/shard_map/ppermute | solution.py:592
  87.9 13.3 %collective-permute-start.13 = (bf16[128,1024]{1,0:T(8,128)(2,1)}, bf16[128,1024]{1,0:T(8,128)(2,1)S(1)}, u32[]{:S(2)}, u32[]{:S(2)}) collective-permute-start(bf16[128,1024]{1,0:T(8,128)(2,1)} %get-tuple-element.57), channel_id=1, source_target_pairs={{0,68},{64,4},{4,64},{68,0},{1,69},{65,5},{5,65},{69,1},{2,70},{66... | collective-permute-start | bytes 786440 | tf_op jit(solution)/shard_map/ppermute | solution.py:592
  89.5 0.8 copy-start.3
  90.2 29.9 %all-to-all-start.2 = ((bf16[128,8,768]{2,1,0:T(8,128)(2,1)}), bf16[128,8,768]{2,1,0:T(8,128)(2,1)S(1)}, u32[]{:S(2)}, u32[]{:S(2)}) async-start(bf16[128,8,768]{2,1,0:T(8,128)(2,1)} %bitcast.19), calls=%async_computation.2 | async-start | bytes 3145728 | tf_op jit(solution)/shard_map/all_to_all | solution.py:694
  96.6 4.6 %copy-start.8 = (bf16[128,1024]{1,0:T(8,128)(2,1)}, bf16[128,1024]{1,0:T(8,128)(2,1)S(1)}, u32[]{:S(2)}) copy-start(bf16[128,1024]{1,0:T(8,128)(2,1)S(1)} %collective-permute-done.11.b) | copy-start | bytes 786436
  96.6 4.6 %copy-start.9 = (bf16[128,1024]{1,0:T(8,128)(2,1)}, bf16[128,1024]{1,0:T(8,128)(2,1)S(1)}, u32[]{:S(2)}) copy-start(bf16[128,1024]{1,0:T(8,128)(2,1)S(1)} %collective-permute-done.12.c) | copy-start | bytes 786436
  101.2 0.7 copy-start.10

commit v7 on v6

--- a/solution.py
+++ b/solution.py
@@ -586,11 +586,11 @@
 
 
 def around(give):
-    came = [give(0)]
+    came = {0: give(0)}
     spot = lambda chip: (chip % 2) * 2 + chip // 2
-    for k in (1, 2, 3):
-        came.append(lax.ppermute(give(k), ("yl", "xl"), [(spot(chip), spot(chip ^ k)) for chip in range(4)]))
-    return came
+    for k in (3, 1, 2):
+        came[k] = lax.ppermute(give(k), ("yl", "xl"), [(spot(chip), spot(chip ^ k)) for chip in range(4)])
+    return [came[k] for k in range(4)]
 
 
 def stack_kernel(place, a, b, c, d, _, own_o, give_o):

time: 122 us -> 122 us (level)
  no operation moved by 1% of the time
where the time goes in v7:
time: 122 us
  waiting for transfers between devices  43.4 us (36%)
  starting transfers between devices  37.8 us (31%)
  Pallas kernels  32.4 us (27%)
  local copies, waits for them, and re-layouts  6.62 us (5%)
    all_to_all x1, waiting for transfers between devices, body(): lax.all_to_all(term.reshape(devices, model // devices, -1), whole, 0, 0,...  15.8 us
    all_to_all x1, waiting for transfers between devices, body(): lax.all_to_all(copies, ('yl',) + rows_axes, 0, 0, axis_index_groups=trade...  14.5 us
    pallas_call x1, Pallas kernels, backward_call(): pl.pallas_call(kernel, in_specs=[smem_spec] + [vmem_spec] * 15, out_specs...  11.9 us
    all_to_all x1, starting transfers between devices, body(): lax.all_to_all(copies, ('yl',) + rows_axes, 0, 0, axis_index_groups=trade...  10.6 us
    ppermute x9, waiting for transfers between devices, around(): lax.ppermute(give(k), ('yl', 'xl'), [(spot(chip), spot(chip ^ k)) for chi...  9.6 us
    ppermute x9, starting transfers between devices, around(): lax.ppermute(give(k), ('yl', 'xl'), [(spot(chip), spot(chip ^ k)) for chi...  8.66 us
    ppermute x5, starting transfers between devices, partner(): return lax.ppermute(a, 'core', [(0, 1), (1, 0)])  8.35 us
    pallas_call x1, Pallas kernels, forward_call(): pl.pallas_call(kernel, in_specs=[smem_spec] + [vmem_spec] * 5, out_specs=...  7.31 us
  transfers between devices with their start and end apart: 17, of which 9 were waited for; matrix products, arithmetic and copies ran while one was open for 2% of the time, Pallas kernels for 7%

profile of v7, /device:TPU:1, one launch (start us, length us, event | category | flops | bytes accessed | tf_op | source)
XLA Modules:
  0.0 121.6 jit_solution(6076565705197504553)
XLA Ops:
  0.6 3.1 %pack_pieces.1 = (bf16[128,1536]{1,0:T(8,128)(2,1)}, bf16[128,1536]{1,0:T(8,128)(2,1)}, bf16[128,1536]{1,0:T(8,128)(2,1)}, bf16[128,1536]{1,0:T(8,128)(2,1)}, bf16[2,2,2,4,32,768]{5,4,3,2,1,0:T(8,128)(2,1)}) custom-call(bf16[128,1024]{1,0:T(8,128)(2,1)} %bitcast.25, bf16[128,2048]{1,0:T(8,128)(2,1)} %bitcast.24, bf16[32,4096]{1,0:T(8,128)(2,1)} %refs_2_.1, ...), custom_call_target="tpu_custom_call" | custom-call | flops 2200000000 | bytes 7000000 | tf_op jit(solution)/shard_map/pack_pieces/pallas_call | solution.py:466
  3.7 2.1 %collective-permute-start = (bf16[128,1536]{1,0:T(8,128)(2,1)}, bf16[128,1536]{1,0:T(8,128)(2,1)S(1)}, u32[]{:S(2)}, u32[]{:S(2)}) collective-permute-start(bf16[128,1536]{1,0:T(8,128)(2,1)} %get-tuple-element.35), channel_id=1, source_target_pairs={{0,64},{64,0},{4,68},{68,4},{1,65},{65,1},{5,69},{69,5},{2,66},{66... | collective-permute-start | bytes 1179656 | tf_op jit(solution)/shard_map/ppermute | solution.py:592
  5.8 1.2 collective-permute-start.1
  7.0 0.0 collective-permute-start.2
  7.1 10.6 %all-to-all-start = ((bf16[32,32,768]{2,1,0:T(8,128)(2,1)}), bf16[32,32,768]{2,1,0:T(8,128)(2,1)S(1)}, u32[]{:S(2)}, u32[]{:S(2)}) async-start(bf16[32,32,768]{2,1,0:T(8,128)(2,1)} %bitcast.18), calls=%async_computation | async-start | bytes 3145728 | tf_op jit(solution)/shard_map/all_to_all | solution.py:678
  17.7 0.0 copy-done.12
  17.7 0.1 dynamic_slice.15
  17.8 0.0 copy-done.13
  17.8 0.1 dynamic_slice.14
  17.8 0.0 copy-done.14
  17.9 0.1 dynamic_slice.12
  17.9 0.1 broadcast_in_dim.17
  18.0 0.1 stack_reshape.3
  18.1 0.1 tile.9
  18.2 0.1 tile.21
  18.3 0.8 dynamic_slice.13
  19.1 0.6 stack.25._.refs_5_.refs_13_
  19.7 0.6 pad_add_fusion.place.refs_0_
  20.3 0.0 collective-permute-done.b
  20.3 0.0 collective-permute-done.1.c
  20.3 0.0 copy-start.6
  20.3 3.4 %collective-permute-done.2.d = bf16[128,1536]{1,0:T(8,128)(2,1)S(1)} collective-permute-done((bf16[128,1536]{1,0:T(8,128)(2,1)}, bf16[128,1536]{1,0:T(8,128)(2,1)S(1)}, u32[]{:S(2)}, u32[]{:S(2)}) %collective-permute-start.2) | collective-permute-done | bytes 393248 | tf_op jit(solution)/shard_map/ppermute | solution.py:592
  23.8 0.0 copy-done.5
  23.8 0.8 copy-done.7
  24.5 3.0 %stack_pieces.1 = (bf16[4,128,1280]{2,1,0:T(8,128)(2,1)}, bf16[4,128,1280]{2,1,0:T(8,128)(2,1)}) custom-call(s32[2]{0:T(128)} %pad_add_fusion.place.refs_0_, bf16[128,1536]{1,0:T(8,128)(2,1)} %get-tuple-element.34.a, bf16[128,1536]{1,0:T(8,128)(2,1)} %copy-done.5, bf16[128,1536]{1,0:T(8,128)(2,1)} %copy-done.6, bf16[128,1536]{1,0:T(8,128)(2,1)} %copy-done.7, ...), custom_call_target="tpu_custom_call" | custom-call | flops 13200000000 | bytes 42000000 | tf_op jit(solution)/shard_map/stack_pieces/pallas_call | solution.py:610
  27.6 3.5 %collective-permute-start.3 = (bf16[4,128,1280]{2,1,0:T(8,128)(2,1)}, bf16[4,128,1280]{2,1,0:T(8,128)(2,1)S(1)}, u32[]{:S(2)}, u32[]{:S(2)}) collective-permute-start(bf16[4,128,1280]{2,1,0:T(8,128)(2,1)} %get-tuple-element.39), channel_id=1, source_target_pairs={{0,32},{32,0},{1,33},{33,1},{2,34},{34,2},{3,35},{35,3},{4,36},{36... | collective-permute-start | bytes 3932168 | tf_op jit(solution)/shard_map/ppermute | solution.py:585
  31.1 14.5 %all-to-all-done = bf16[32,32,768]{2,1,0:T(8,128)(2,1)S(1)} async-done(((bf16[32,32,768]{2,1,0:T(8,128)(2,1)}), bf16[32,32,768]{2,1,0:T(8,128)(2,1)S(1)}, u32[]{:S(2)}, u32[]{:S(2)}) %all-to-all-start) | async-done | bytes 1572896 | tf_op jit(solution)/shard_map/all_to_all | solution.py:678
  45.6 2.5 %collective-permute-start.4 = (bf16[1024,128]{1,0:T(8,128)(2,1)S(1)}, bf16[1024,128]{1,0:T(8,128)(2,1)S(1)}, u32[]{:S(2)}, u32[]{:S(2)}) collective-permute-start(bf16[1024,128]{1,0:T(8,128)(2,1)S(1)} %slice.4), channel_id=1, source_target_pairs={{0,32},{32,0},{1,33},{33,1},{2,34},{34,2},{3,35},{35,3},{4,36},{36... | collective-permute-start | bytes 786440 | tf_op jit(solution)/shard_map/ppermute | solution.py:585
  48.1 0.0 collective-permute-done.3.refs_2_
  48.1 1.2 collective-permute-done.4.refs_4_.refs_15_
  49.3 1.3 %copy-done.2 = bf16[4,128,1280]{2,1,0:T(8,128)(2,1)S(1)} copy-done((bf16[4,128,1280]{2,1,0:T(8,128)(2,1)S(1)}, bf16[4,128,1280]{2,1,0:T(8,128)(2,1)}, u32[]{:S(2)}) %copy-start.2) | copy-done | bytes 1310744
  50.6 7.3 %forward_scan.1 = (bf16[4,2,128,1024]{3,2,1,0:T(8,128)(2,1)S(1)}, bf16[4,2,128,256]{3,2,1,0:T(8,128)(2,1)S(1)}, f32[4,2,128,256]{3,2,1,0:T(8,128)S(1)}, f32[4,2,...) custom-call(s32[2]{0:T(128)S(1)} %copy-done.1, ...), custom_call_target="tpu_custom_call" | custom-call | flops 13200000000 | bytes 42000000 | tf_op jit(solution)/shard_map/forward_scan/pallas_call | solution.py:500
  57.9 0.4 collective-permute-start.5
  58.3 0.8 collective-permute-done.5
  59.1 0.7 collective-permute-start.8
  59.9 0.7 collective-permute-start.7
  60.6 1.2 %collective-permute-start.6 = (f32[2,8,128]{2,1,0:T(8,128)S(1)}, f32[2,8,128]{2,1,0:T(8,128)S(1)}, u32[]{:S(2)}, u32[]{:S(2)}) collective-permute-start(f32[2,8,128]{2,1,0:T(8,128)S(1)} %add.29.refs_9_), channel_id=1, source_target_pairs={{0,64},{64,0},{4,68},{68,4},{1,65},{65,1},{5,69},{69,5},{2,66},{66... | collective-permute-start | bytes 24584 | tf_op jit(solution)/shard_map/ppermute | solution.py:592
  61.8 0.8 collective-permute-done.8.refs_12_
  62.5 0.0 collective-permute-done.7.refs_11_
  62.5 0.8 collective-permute-done.6.refs_10_
  63.4 11.9 %backward_scan.1 = (bf16[4,2,128,256]{3,2,1,0:T(8,128)(2,1)}, f32[2,2,128,1024]{3,2,1,0:T(8,128)}, bf16[2,2,128,1024]{3,2,1,0:T(8,128)(2,1)}, bf16[1024,768]{1,0:T(8,128)(2,1)}, bf16[1024,128]{1,0:T(8,128)(2,1)}) custom-call(s32[1]{0:T(128)} %bitcast.1.refs_0_, f32[4,2,128,256]{3,2,1,0:T(8,128)S(1)} %get-tuple-element.41.refs_1_, ...), custom_call_target="tpu_custom_call" | custom-call | flops 22000001024 | bytes 70000000 | tf_op jit(solution)/shard_map/backward_scan/pallas_call | solution.py:529
  75.3 1.8 %collective-permute-start.9 = (bf16[2,2,128,1024]{3,2,1,0:T(8,128)(2,1)}, bf16[2,2,128,1024]{3,2,1,0:T(8,128)(2,1)S(1)}, u32[]{:S(2)}, u32[]{:S(2)}) collective-permute-start(bf16[2,2,128,1024]{3,2,1,0:T(8,128)(2,1)} %get-tuple-element.51), channel_id=1, source_target_pairs={{0,32},{32,0},{1,33},{33,1},{2,34},{34,2},{3,35},{35,3},{4,36},{36... | collective-permute-start | bytes 3145736 | tf_op jit(solution)/shard_map/ppermute | solution.py:585
  77.1 0.1 collective-permute-start.10
  77.2 3.8 %all-to-all-start.1 = ((bf16[8,128,256]{2,1,0:T(8,128)(2,1)}), bf16[8,128,256]{2,1,0:T(8,128)(2,1)S(1)}, u32[]{:S(2)}, u32[]{:S(2)}) async-start(bf16[8,128,256]{2,1,0:T(8,128)(2,1)} %bitcast.20), calls=%async_computation.1 | async-start | bytes 1048576 | tf_op jit(solution)/shard_map/all_to_all | solution.py:692
  81.0 0.0 collective-permute-done.10.got
  81.0 0.0 collective-permute-done.9.far
  81.0 0.7 copy-done.11
  81.7 0.3 copy-done.4
  82.1 3.2 %join_halves.1 = (bf16[128,1024]{1,0:T(8,128)(2,1)}, bf16[128,1024]{1,0:T(8,128)(2,1)}, bf16[128,1024]{1,0:T(8,128)(2,1)}, bf16[128,1024]{1,0:T(8,128)(2,1)}, bf16[1024,768]{1,0:T(8,128)(2,1)}) custom-call(s32[1]{0:T(128)} %bitcast.place, f32[2,2,128,1024]{3,2,1,0:T(8,128)} %get-tuple-element.50.near, ...), custom_call_target="tpu_custom_call", output_to_operand_aliasing={{4}: (3, {})} | custom-call | flops 3300000000 | bytes 10500000 | tf_op jit(solution)/shard_map/join_halves/pallas_call | solution.py:551
  85.3 1.4 %collective-permute-start.11 = (bf16[128,1024]{1,0:T(8,128)(2,1)}, bf16[128,1024]{1,0:T(8,128)(2,1)S(1)}, u32[]{:S(2)}, u32[]{:S(2)}) collective-permute-start(bf16[128,1024]{1,0:T(8,128)(2,1)} %get-tuple-element.55), channel_id=1, source_target_pairs={{0,64},{64,0},{4,68},{68,4},{1,65},{65,1},{5,69},{69,5},{2,66},{66... | collective-permute-start | bytes 786440 | tf_op jit(solution)/shard_map/ppermute | solution.py:592
  86.7 1.2 collective-permute-start.12
  87.9 0.1 collective-permute-start.13
  88.0 1.5 %all-to-all-done.1.heads = bf16[8,128,256]{2,1,0:T(8,128)(2,1)S(1)} async-done(((bf16[8,128,256]{2,1,0:T(8,128)(2,1)}), bf16[8,128,256]{2,1,0:T(8,128)(2,1)S(1)}, u32[]{:S(2)}, u32[]{:S(2)}) %all-to-all-start.1) | async-done | bytes 524320 | tf_op jit(solution)/shard_map/all_to_all | solution.py:692
  89.5 0.8 copy-done.3
  90.2 6.3 %all-to-all-start.2 = ((bf16[128,8,768]{2,1,0:T(8,128)(2,1)}), bf16[128,8,768]{2,1,0:T(8,128)(2,1)S(1)}, u32[]{:S(2)}, u32[]{:S(2)}) async-start(bf16[128,8,768]{2,1,0:T(8,128)(2,1)} %bitcast.19), calls=%async_computation.2 | async-start | bytes 3145728 | tf_op jit(solution)/shard_map/all_to_all | solution.py:694
  96.6 0.0 collective-permute-done.11.b
  96.6 0.0 collective-permute-done.12.c
  96.6 0.0 copy-start.9
  96.6 4.6 %collective-permute-done.13.d = bf16[128,1024]{1,0:T(8,128)(2,1)S(1)} collective-permute-done((bf16[128,1024]{1,0:T(8,128)(2,1)}, bf16[128,1024]{1,0:T(8,128)(2,1)S(1)}, u32[]{:S(2)}, u32[]{:S(2)}) %collective-permute-start.13) | collective-permute-done | bytes 262176 | tf_op jit(solution)/shard_map/ppermute | solution.py:592
  101.2 0.0 copy-done.8
  101.2 0.7 copy-done.10
  101.9 2.4 %sum_pieces.1 = (bf16[128,1024]{1,0:T(8,128)(2,1)}, bf16[128,2048]{1,0:T(8,128)(2,1)}) custom-call(bf16[128,1024]{1,0:T(8,128)(2,1)} %get-tuple-element.54.a, bf16[128,1024]{1,0:T(8,128)(2,1)} %copy-done.8, bf16[128,1024]{1,0:T(8,128)(2,1)} %copy-done.9, bf16[128,1024]{1,0:T(8,128)(2,1)} %copy-done.10, bf16[8,128,256]{2,1,0:T(8,128)(2,1)} %copy-done.3), custom_call_target="tpu_custom_call" | custom-call | flops 26400000000 | bytes 84000000 | tf_op jit(solution)/shard_map/sum_pieces/pallas_call | solution.py:630
  104.3 15.8 %all-to-all-done.2 = bf16[128,8,768]{2,1,0:T(8,128)(2,1)S(1)} async-done(((bf16[128,8,768]{2,1,0:T(8,128)(2,1)}), bf16[128,8,768]{2,1,0:T(8,128)(2,1)S(1)}, u32[]{:S(2)}, u32[]{:S(2)}) %all-to-all-start.2) | async-done | bytes 1572896 | tf_op jit(solution)/shard_map/all_to_all | solution.py:694
  120.1 1.5 %total_shares.1 = (f32[8,4096]{1,0:T(8,128)}, f32[8,288]{1,0:T(8,128)}) custom-call(bf16[4,4,2,4,8,768]{5,4,3,2,1,0:T(8,128)(2,1)S(1)} %bitcast.17), custom_call_target="tpu_custom_call" | custom-call | flops 2200000000 | bytes 7000000 | tf_op jit(solution)/shard_map/total_shares/pallas_call | solution.py:572
  (24 shorter events, 0.1 us)
Async XLA Ops:
  3.7 16.6 %collective-permute-start = (bf16[128,1536]{1,0:T(8,128)(2,1)}, bf16[128,1536]{1,0:T(8,128)(2,1)S(1)}, u32[]{:S(2)}, u32[]{:S(2)}) collective-permute-start(bf16[128,1536]{1,0:T(8,128)(2,1)} %get-tuple-element.35), channel_id=1, source_target_pairs={{0,64},{64,0},{4,68},{68,4},{1,65},{65,1},{5,69},{69,5},{2,66},{66... | collective-permute-start | bytes 1179656 | tf_op jit(solution)/shard_map/ppermute | solution.py:592
  5.8 14.5 %collective-permute-start.1 = (bf16[128,1536]{1,0:T(8,128)(2,1)}, bf16[128,1536]{1,0:T(8,128)(2,1)S(1)}, u32[]{:S(2)}, u32[]{:S(2)}) collective-permute-start(bf16[128,1536]{1,0:T(8,128)(2,1)} %get-tuple-element.36), channel_id=1, source_target_pairs={{0,4},{64,68},{4,0},{68,64},{1,5},{65,69},{5,1},{69,65},{2,6},{66,... | collective-permute-start | bytes 1179656 | tf_op jit(solution)/shard_map/ppermute | solution.py:592
  7.0 16.7 %collective-permute-start.2 = (bf16[128,1536]{1,0:T(8,128)(2,1)}, bf16[128,1536]{1,0:T(8,128)(2,1)S(1)}, u32[]{:S(2)}, u32[]{:S(2)}) collective-permute-start(bf16[128,1536]{1,0:T(8,128)(2,1)} %get-tuple-element.37), channel_id=1, source_target_pairs={{0,68},{64,4},{4,64},{68,0},{1,69},{65,5},{5,65},{69,1},{2,70},{66... | collective-permute-start | bytes 1179656 | tf_op jit(solution)/shard_map/ppermute | solution.py:592
  7.0 10.6 %copy-start.12 = (f32[32]{0:T(128)S(1)}, f32[32]{0:T(128)}, u32[]{:S(2)}) copy-start(f32[32]{0:T(128)} %param.12) | copy-start | bytes 388
  7.0 10.7 %copy-start.13 = (f32[32]{0:T(128)S(1)}, f32[32]{0:T(128)}, u32[]{:S(2)}) copy-start(f32[32]{0:T(128)} %param.13) | copy-start | bytes 388
  7.1 10.8 %copy-start.14 = (f32[32]{0:T(128)S(1)}, f32[32]{0:T(128)}, u32[]{:S(2)}) copy-start(f32[32]{0:T(128)} %param.14) | copy-start | bytes 388
  7.1 38.5 %all-to-all-start = ((bf16[32,32,768]{2,1,0:T(8,128)(2,1)}), bf16[32,32,768]{2,1,0:T(8,128)(2,1)S(1)}, u32[]{:S(2)}, u32[]{:S(2)}) async-start(bf16[32,32,768]{2,1,0:T(8,128)(2,1)} %bitcast.18), calls=%async_computation | async-start | bytes 3145728 | tf_op jit(solution)/shard_map/all_to_all | solution.py:678
  20.3 3.5 %copy-start.5 = (bf16[128,1536]{1,0:T(8,128)(2,1)}, bf16[128,1536]{1,0:T(8,128)(2,1)S(1)}, u32[]{:S(2)}) copy-start(bf16[128,1536]{1,0:T(8,128)(2,1)S(1)} %collective-permute-done.b) | copy-start | bytes 1179652
  20.3 3.5 %copy-start.6 = (bf16[128,1536]{1,0:T(8,128)(2,1)}, bf16[128,1536]{1,0:T(8,128)(2,1)S(1)}, u32[]{:S(2)}) copy-start(bf16[128,1536]{1,0:T(8,128)(2,1)S(1)} %collective-permute-done.1.c) | copy-start | bytes 1179652
  23.8 0.8 copy-start.7
  24.5 24.7 %copy-start = (f32[8,256]{1,0:T(8,128)S(1)}, f32[8,256]{1,0:T(8,128)}, u32[]{:S(2)}) copy-start(f32[8,256]{1,0:T(8,128)} %stack.25._.refs_5_.refs_13_) | copy-start | bytes 24580
  24.5 24.7 %copy-start.1 = (s32[2]{0:T(128)S(1)}, s32[2]{0:T(128)}, u32[]{:S(2)}) copy-start(s32[2]{0:T(128)} %pad_add_fusion.place.refs_0_) | copy-start | bytes 28
  27.6 20.5 %collective-permute-start.3 = (bf16[4,128,1280]{2,1,0:T(8,128)(2,1)}, bf16[4,128,1280]{2,1,0:T(8,128)(2,1)S(1)}, u32[]{:S(2)}, u32[]{:S(2)}) collective-permute-start(bf16[4,128,1280]{2,1,0:T(8,128)(2,1)} %get-tuple-element.39), channel_id=1, source_target_pairs={{0,32},{32,0},{1,33},{33,1},{2,34},{34,2},{3,35},{35,3},{4,36},{36... | collective-permute-start | bytes 3932168 | tf_op jit(solution)/shard_map/ppermute | solution.py:585
  45.6 3.6 %collective-permute-start.4 = (bf16[1024,128]{1,0:T(8,128)(2,1)S(1)}, bf16[1024,128]{1,0:T(8,128)(2,1)S(1)}, u32[]{:S(2)}, u32[]{:S(2)}) collective-permute-start(bf16[1024,128]{1,0:T(8,128)(2,1)S(1)} %slice.4), channel_id=1, source_target_pairs={{0,32},{32,0},{1,33},{33,1},{2,34},{34,2},{3,35},{35,3},{4,36},{36... | collective-permute-start | bytes 786440 | tf_op jit(solution)/shard_map/ppermute | solution.py:585
  49.3 1.3 %copy-start.2 = (bf16[4,128,1280]{2,1,0:T(8,128)(2,1)S(1)}, bf16[4,128,1280]{2,1,0:T(8,128)(2,1)}, u32[]{:S(2)}) copy-start(bf16[4,128,1280]{2,1,0:T(8,128)(2,1)} %get-tuple-element.38.refs_1_) | copy-start | bytes 3932164
  57.9 1.2 %collective-permute-start.5 = (f32[2,8,128]{2,1,0:T(8,128)S(1)}, f32[2,8,128]{2,1,0:T(8,128)S(1)}, u32[]{:S(2)}, u32[]{:S(2)}) collective-permute-start(f32[2,8,128]{2,1,0:T(8,128)S(1)} %get-tuple-element.49), channel_id=1, source_target_pairs={{0,32},{32,0},{1,33},{33,1},{2,34},{34,2},{3,35},{35,3},{4,36},{36... | collective-permute-start | bytes 24584 | tf_op jit(solution)/shard_map/ppermute | solution.py:585
  59.1 3.4 %collective-permute-start.8 = (f32[2,8,128]{2,1,0:T(8,128)S(1)}, f32[2,8,128]{2,1,0:T(8,128)S(1)}, u32[]{:S(2)}, u32[]{:S(2)}) collective-permute-start(f32[2,8,128]{2,1,0:T(8,128)S(1)} %add.29.refs_9_), channel_id=1, source_target_pairs={{0,68},{64,4},{4,64},{68,0},{1,69},{65,5},{5,65},{69,1},{2,70},{66... | collective-permute-start | bytes 24584 | tf_op jit(solution)/shard_map/ppermute | solution.py:592
  59.9 2.7 %collective-permute-start.7 = (f32[2,8,128]{2,1,0:T(8,128)S(1)}, f32[2,8,128]{2,1,0:T(8,128)S(1)}, u32[]{:S(2)}, u32[]{:S(2)}) collective-permute-start(f32[2,8,128]{2,1,0:T(8,128)S(1)} %add.29.refs_9_), channel_id=1, source_target_pairs={{0,4},{64,68},{4,0},{68,64},{1,5},{65,69},{5,1},{69,65},{2,6},{66,... | collective-permute-start | bytes 24584 | tf_op jit(solution)/shard_map/ppermute | solution.py:592
  60.6 2.8 %collective-permute-start.6 = (f32[2,8,128]{2,1,0:T(8,128)S(1)}, f32[2,8,128]{2,1,0:T(8,128)S(1)}, u32[]{:S(2)}, u32[]{:S(2)}) collective-permute-start(f32[2,8,128]{2,1,0:T(8,128)S(1)} %add.29.refs_9_), channel_id=1, source_target_pairs={{0,64},{64,0},{4,68},{68,4},{1,65},{65,1},{5,69},{69,5},{2,66},{66... | collective-permute-start | bytes 24584 | tf_op jit(solution)/shard_map/ppermute | solution.py:592
  75.3 5.8 %collective-permute-start.9 = (bf16[2,2,128,1024]{3,2,1,0:T(8,128)(2,1)}, bf16[2,2,128,1024]{3,2,1,0:T(8,128)(2,1)S(1)}, u32[]{:S(2)}, u32[]{:S(2)}) collective-permute-start(bf16[2,2,128,1024]{3,2,1,0:T(8,128)(2,1)} %get-tuple-element.51), channel_id=1, source_target_pairs={{0,32},{32,0},{1,33},{33,1},{2,34},{34,2},{3,35},{35,3},{4,36},{36... | collective-permute-start | bytes 3145736 | tf_op jit(solution)/shard_map/ppermute | solution.py:585
  77.1 3.9 %collective-permute-start.10 = (bf16[1024,128]{1,0:T(8,128)(2,1)}, bf16[1024,128]{1,0:T(8,128)(2,1)S(1)}, u32[]{:S(2)}, u32[]{:S(2)}) collective-permute-start(bf16[1024,128]{1,0:T(8,128)(2,1)} %get-tuple-element.53), channel_id=1, source_target_pairs={{0,32},{32,0},{1,33},{33,1},{2,34},{34,2},{3,35},{35,3},{4,36},{36... | collective-permute-start | bytes 786440 | tf_op jit(solution)/shard_map/ppermute | solution.py:585
  77.2 12.3 %all-to-all-start.1 = ((bf16[8,128,256]{2,1,0:T(8,128)(2,1)}), bf16[8,128,256]{2,1,0:T(8,128)(2,1)S(1)}, u32[]{:S(2)}, u32[]{:S(2)}) async-start(bf16[8,128,256]{2,1,0:T(8,128)(2,1)} %bitcast.20), calls=%async_computation.1 | async-start | bytes 1048576 | tf_op jit(solution)/shard_map/all_to_all | solution.py:692
  81.0 0.7 copy-start.11
  81.0 1.0 copy-start.4
  85.3 11.3 %collective-permute-start.11 = (bf16[128,1024]{1,0:T(8,128)(2,1)}, bf16[128,1024]{1,0:T(8,128)(2,1)S(1)}, u32[]{:S(2)}, u32[]{:S(2)}) collective-permute-start(bf16[128,1024]{1,0:T(8,128)(2,1)} %get-tuple-element.55), channel_id=1, source_target_pairs={{0,64},{64,0},{4,68},{68,4},{1,65},{65,1},{5,69},{69,5},{2,66},{66... | collective-permute-start | bytes 786440 | tf_op jit(solution)/shard_map/ppermute | solution.py:592
  86.7 9.9 %collective-permute-start.12 = (bf16[128,1024]{1,0:T(8,128)(2,1)}, bf16[128,1024]{1,0:T(8,128)(2,1)S(1)}, u32[]{:S(2)}, u32[]{:S(2)}) collective-permute-start(bf16[128,1024]{1,0:T(8,128)(2,1)} %get-tuple-element.56), channel_id=1, source_target_pairs={{0,4},{64,68},{4,0},{68,64},{1,5},{65,69},{5,1},{69,65},{2,6},{66,... | collective-permute-start | bytes 786440 | tf_op jit(solution)/shard_map/ppermute | solution.py:592
  87.9 13.3 %collective-permute-start.13 = (bf16[128,1024]{1,0:T(8,128)(2,1)}, bf16[128,1024]{1,0:T(8,128)(2,1)S(1)}, u32[]{:S(2)}, u32[]{:S(2)}) collective-permute-start(bf16[128,1024]{1,0:T(8,128)(2,1)} %get-tuple-element.57), channel_id=1, source_target_pairs={{0,68},{64,4},{4,64},{68,0},{1,69},{65,5},{5,65},{69,1},{2,70},{66... | collective-permute-start | bytes 786440 | tf_op jit(solution)/shard_map/ppermute | solution.py:592
  89.5 0.8 copy-start.3
  90.2 29.9 %all-to-all-start.2 = ((bf16[128,8,768]{2,1,0:T(8,128)(2,1)}), bf16[128,8,768]{2,1,0:T(8,128)(2,1)S(1)}, u32[]{:S(2)}, u32[]{:S(2)}) async-start(bf16[128,8,768]{2,1,0:T(8,128)(2,1)} %bitcast.19), calls=%async_computation.2 | async-start | bytes 3145728 | tf_op jit(solution)/shard_map/all_to_all | solution.py:694
  96.6 4.6 %copy-start.8 = (bf16[128,1024]{1,0:T(8,128)(2,1)}, bf16[128,1024]{1,0:T(8,128)(2,1)S(1)}, u32[]{:S(2)}) copy-start(bf16[128,1024]{1,0:T(8,128)(2,1)S(1)} %collective-permute-done.11.b) | copy-start | bytes 786436
  96.6 4.6 %copy-start.9 = (bf16[128,1024]{1,0:T(8,128)(2,1)}, bf16[128,1024]{1,0:T(8,128)(2,1)S(1)}, u32[]{:S(2)}) copy-start(bf16[128,1024]{1,0:T(8,128)(2,1)S(1)} %collective-permute-done.12.c) | copy-start | bytes 786436
  101.2 0.7 copy-start.10
